TPU v7x, 256 devices: a whole 4x4x8 slice. The times are simulated.
256 devices in a mesh: grp: 8 (over x, core), tbl: 32 (over y, z).
Axes of the slice: x: 4, y: 4, z: 8, core: 2. Of those that a mesh axis runs over, the one named last changes fastest.
Arguments:
- cross_input: bfloat16 [32768, 3456], P(('grp', 'tbl')), may hold values from -6 to 6
- upstream: bfloat16 [32768, 3456], P(('grp', 'tbl')), may hold values from -6 to 6
- v_weight: bfloat16 [256, 3456], replicated, may hold values from -0.109375 to 0.109375
- u_weight: bfloat16 [256, 3456], replicated, may hold values from -0.375 to 0.375
- bias: float32 [3456], replicated, may hold values from -3 to 3
- placement: int32 [26], replicated, may hold values from 0 to 31, as said below
- owned_ids: int32 [64, 4, 32768], P('tbl', None, 'grp'), may hold values from 0 to 255
Outputs:
- cross_grad: float32 [256, 6912], P(('grp', 'tbl'))
- table_grad: float32 [64, 256, 128], P('tbl', 'grp')
Inputs may be any that keep to these rules, and one draw needn't show every extreme that they name: `placement`: no device holds more than 2 tables, and some device holds exactly 2.
All inputs are finite; a program needn't handle non-finite values.
Results may differ from a plain program's by a relative error of at most 0.004.
Values may be sent and summed in bfloat16 or wider, within the bound.
No kernel may reach another device: no remote copies, remote signals or barrier semaphores. Data moves between devices by JAX's collectives and lax.ppermute only.
A program may use at most 64 MiB of HBM per device.

v0:
```python
import math

import jax
import jax.numpy as jnp
from jax import lax
from jax.sharding import PartitionSpec as P

EMB = 128
TABLES = 26
ROWS = 256


def in_blocks(shard, dim, length):
    shape = shard.shape
    blocks = shard.reshape(*shape[:dim], length, shape[dim] // length, *shape[dim + 1 :])
    return jnp.moveaxis(blocks, dim, 0)


def sum_at_owner(shard, axis, dim):
    blocks = in_blocks(shard, dim, lax.axis_size(axis))
    arrived = lax.all_to_all(blocks, axis, split_axis=0, concat_axis=0, tiled=True)
    return arrived.sum(axis=0)


def outer_sum(left, right):
    return jnp.einsum("br,bd->rd", left, right, preferred_element_type=jnp.float32)


def on_device(cross_input, upstream, v_weight, u_weight, bias, placement, owned_ids):
    n_grp = lax.axis_size("grp")
    n_tbl = lax.axis_size("tbl")
    samples = cross_input.shape[0]
    slots_dev = owned_ids.shape[0]
    scale = 1.0 / math.sqrt(samples * n_grp * n_tbl)
    hidden = jnp.dot(cross_input, v_weight.T, preferred_element_type=jnp.float32).astype(
        jnp.bfloat16
    )
    mixed = jnp.dot(hidden, u_weight, preferred_element_type=jnp.float32) + bias
    up_float = upstream.astype(jnp.float32)
    product_grad = (up_float * cross_input.astype(jnp.float32)).astype(jnp.bfloat16)
    hidden_grad = jnp.dot(product_grad, u_weight.T, preferred_element_type=jnp.float32).astype(
        jnp.bfloat16
    )
    input_grad = up_float * (1.0 + mixed) + jnp.dot(
        hidden_grad, v_weight, preferred_element_type=jnp.float32
    )
    pooled = input_grad[:, EMB:].astype(jnp.bfloat16).reshape(samples, TABLES, EMB)
    same = placement[:, None] == placement[None, :]
    earlier = jnp.arange(TABLES)[None, :] < jnp.arange(TABLES)[:, None]
    slot = jnp.sum((same & earlier).astype(jnp.int32), axis=1)
    target = slot * n_tbl + placement
    select = (jnp.arange(slots_dev * n_tbl, dtype=jnp.int32)[:, None] == target[None, :]).astype(
        jnp.bfloat16
    )
    outgoing = jnp.einsum("st,bte->sbe", select, pooled, preferred_element_type=jnp.float32)
    outgoing = outgoing.astype(jnp.bfloat16).reshape(slots_dev, n_tbl, samples, EMB)
    arriving = lax.all_to_all(outgoing, "tbl", split_axis=1, concat_axis=1, tiled=True)
    arriving = arriving.reshape(slots_dev, n_tbl * samples, EMB)
    row_numbers = jnp.arange(ROWS, dtype=jnp.int32)
    counts = jnp.sum(
        (owned_ids[:, :, None, :] == row_numbers[None, None, :, None]).astype(jnp.bfloat16), axis=1
    )
    row_terms = jnp.einsum("srm,sme->sre", counts, arriving, preferred_element_type=jnp.float32)
    table_grad = sum_at_owner(row_terms, "grp", 1)
    term = jnp.concatenate(
        [outer_sum(hidden, product_grad), outer_sum(hidden_grad, cross_input)], axis=1
    )
    partial_sum = lax.psum_scatter(term, "grp", scatter_dimension=0, tiled=True)
    summed = sum_at_owner(partial_sum, "tbl", 0)
    cross_grad = summed * scale
    return (cross_grad, table_grad)


def solution(mesh):
    in_specs = (
        P(("grp", "tbl"), None),
        P(("grp", "tbl"), None),
        P(),
        P(),
        P(),
        P(),
        P("tbl", None, "grp"),
    )
    out_specs = (P(("grp", "tbl"), None), P("tbl", "grp", None))
    return jax.shard_map(
        on_device, mesh=mesh, in_specs=in_specs, out_specs=out_specs, check_vma=False
    )
```

profile of v0, /device:TPU:32, one launch (start us, length us, event | category | flops | bytes accessed | tf_op | source)
XLA Modules:
  0.0 143.4 jit_solution(3677128592539829109)
XLA Ops:
  7.2 0.0 copy-start
  7.2 0.0 copy-start.2
  7.2 0.0 copy-start.3
  7.2 0.0 reduce-scatter.2.cloned.1.call-start
  7.2 2.6 %convolution_convert_fusion.2 = bf16[128,256]{1,0:T(8,128)(2,1)S(1)} fusion(bf16[128,3456]{1,0:T(8,128)(2,1)} %param.7, bf16[256,3456]{1,0:T(8,128)(2,1)} %param.9), kind=kOutput, calls=%fused_computation.12 | convolution fusion | flops 226525184 | bytes 2719744 | tf_op jit(solution)/shard_map/dot_general | solution.py:35
  9.8 0.0 copy-done
  9.8 0.0 copy-done.2
  9.9 0.1 copy-done.3
  9.9 0.7 convolution_convert_fusion.1
  10.7 0.0 copy-done.7
  10.7 0.0 copy-start.5
  10.7 0.7 fusion.4
  11.3 0.0 copy-done.5
  11.3 0.7 fusion.9
  12.0 3.4 %pad_maximum_fusion = f32[256,6912]{1,0:T(8,128)} fusion(f32[256,3456]{1,0:T(8,128)S(1)} %fusion.9, f32[256,3456]{1,0:T(8,128)S(1)} %fusion.4), kind=kLoop, calls=%fused_computation.3 | loop fusion | flops 1769472 | bytes 14155776 | tf_op jit(solution)/shard_map/concatenate | solution.py:65
  15.4 0.0 reduce-scatter.2.cloned.1.call-update
  15.4 0.0 copy-start.10
  15.4 0.0 copy-start.8
  15.4 0.1 convert_element_type.29
  15.6 0.6 copy-done.10
  16.1 0.1 copy-done.8
  16.3 0.4 fusion.10
  16.7 1.0 copy-done.4
  17.8 0.4 fusion.11
  18.2 0.3 fusion.2
  18.4 0.0 copy-start.11
  18.4 1.3 copy.20
  19.7 1.9 %copy.21 = bf16[128,26,128]{2,1,0:T(8,128)(2,1)S(1)} copy(bf16[128,26,128]{0,2,1:T(8,128)(2,1)} %bitcast.26) | data formatting | bytes 1703936 | tf_op jit(solution)/shard_map/reshape | solution.py:47
  21.7 0.2 convert_reduce_fusion
  21.9 0.8 convolution_convert_fusion
  22.7 3.5 %copy.22 = bf16[2,32,128,128]{3,0,2,1:T(2,128)(2,1)} copy(bf16[2,32,128,128]{3,1,0,2:T(8,128)(2,1)S(1)} %bitcast.25) | data formatting | bytes 4194304 | tf_op jit(solution)/shard_map/reshape | solution.py:56
  26.2 11.6 %all-to-all-start.1 = ((bf16[2,32,128,128]{3,0,2,1:T(2,128)(2,1)}), bf16[2,32,128,128]{3,0,2,1:T(2,128)(2,1)}, u32[]{:S(2)}, u32[]{:S(2)}) async-start(bf16[2,32,128,128]{3,0,2,1:T(2,128)(2,1)} %copy.22), calls=%async_computation.2 | async-start | bytes 4194304 | tf_op jit(solution)/shard_map/all_to_all | solution.py:57
  37.7 0.0 copy-done.9
  37.7 7.6 %fusion.1 = bf16[2,256,4096]{2,1,0:T(8,128)(2,1)} fusion(s32[2,4,4096]{2,1,0:T(4,128)S(1)} %copy-done.9), kind=kLoop, calls=%fused_computation.2 | loop fusion | flops 23068672 | bytes 4325376 | tf_op jit(solution)/shard_map/reduce_sum | solution.py:60
  45.3 41.5 %all-to-all-done.1 = bf16[2,32,128,128]{3,0,2,1:T(2,128)(2,1)} async-done(((bf16[2,32,128,128]{3,0,2,1:T(2,128)(2,1)}), bf16[2,32,128,128]{3,0,2,1:T(2,128)(2,1)}, u32[]{:S(2)}, u32[]{:S(2)}) %all-to-all-start.1) | async-done | bytes 2097184 | tf_op jit(solution)/shard_map/all_to_all | solution.py:57
  86.8 2.3 %copy.23 = bf16[2,32,128,128]{3,2,1,0:T(8,128)(2,1)S(1)} copy(bf16[2,32,128,128]{3,0,2,1:T(2,128)(2,1)} %all-to-all-done.1) | data formatting | bytes 4194304 | tf_op jit(solution)/shard_map/all_to_all | solution.py:57
  89.1 0.5 copy-done.1
  89.6 1.2 fusion.12
  90.9 0.7 copy.26
  91.6 4.3 %all-to-all-start.2 = ((f32[8,2,32,128]{3,2,1,0:T(8,128)}), f32[8,2,32,128]{3,2,1,0:T(8,128)S(1)}, u32[]{:S(2)}, u32[]{:S(2)}) async-start(f32[8,2,32,128]{3,2,1,0:T(8,128)} %bitcast.23), calls=%async_computation.3 | async-start | bytes 524288 | tf_op jit(solution)/shard_map/all_to_all | solution.py:21
  95.9 0.0 reduce-scatter.2.cloned.1.call-done
  95.9 3.0 %copy.19 = f32[32,1,6912]{2,1,0:T(1,128)} copy(f32[32,1,6912]{2,0,1:T(8,128)} %bitcast.28) | data formatting | bytes 1769472 | tf_op jit(solution)/shard_map/reshape | solution.py:15
  98.9 4.5 %all-to-all-done.2 = f32[8,2,32,128]{3,2,1,0:T(8,128)S(1)} async-done(((f32[8,2,32,128]{3,2,1,0:T(8,128)}), f32[8,2,32,128]{3,2,1,0:T(8,128)S(1)}, u32[]{:S(2)}, u32[]{:S(2)}) %all-to-all-start.2) | async-done | bytes 262176 | tf_op jit(solution)/shard_map/all_to_all | solution.py:21
  103.5 7.1 %all-to-all-start = ((f32[32,1,6912]{2,1,0:T(1,128)}), f32[32,1,6912]{2,1,0:T(1,128)S(1)}, u32[]{:S(2)}, u32[]{:S(2)}) async-start(f32[32,1,6912]{2,1,0:T(1,128)} %copy.19), calls=%async_computation.1 | async-start | bytes 1769472 | tf_op jit(solution)/shard_map/all_to_all | solution.py:21
  110.6 0.6 reduce_sum.42
  111.2 24.2 %all-to-all-done = f32[32,1,6912]{2,1,0:T(1,128)S(1)} async-done(((f32[32,1,6912]{2,1,0:T(1,128)}), f32[32,1,6912]{2,1,0:T(1,128)S(1)}, u32[]{:S(2)}, u32[]{:S(2)}) %all-to-all-start) | async-done | bytes 884768 | tf_op jit(solution)/shard_map/all_to_all | solution.py:21
  135.4 0.5 reduce_sum.39
  135.9 0.6 mul.29
  (10 shorter events, 0.0 us)
Async XLA Ops:
  7.2 2.7 %copy-start = (bf16[256,3456]{1,0:T(8,128)(2,1)S(1)}, bf16[256,3456]{1,0:T(8,128)(2,1)}, u32[]{:S(2)}) copy-start(bf16[256,3456]{1,0:T(8,128)(2,1)} %param.10) | copy-start | bytes 5308420
  7.2 2.7 %copy-start.2 = (bf16[128,3456]{1,0:T(8,128)(2,1)S(1)}, bf16[128,3456]{1,0:T(8,128)(2,1)}, u32[]{:S(2)}) copy-start(bf16[128,3456]{1,0:T(8,128)(2,1)} %param.7) | copy-start | bytes 2654212
  7.2 2.7 %copy-start.3 = (bf16[128,3456]{1,0:T(8,128)(2,1)S(1)}, bf16[128,3456]{1,0:T(8,128)(2,1)}, u32[]{:S(2)}) copy-start(bf16[128,3456]{1,0:T(8,128)(2,1)} %param.8) | copy-start | bytes 2654212
  7.2 88.7 %reduce-scatter.2.cloned.1.call-start = ((), (), s32[]{:S(2)}) async-start(), calls=%async_computation.4 | async-start | bytes 7962624 | tf_op jit(solution)/shard_map/reduce_scatter | solution.py:68
  9.9 0.7 copy-start.7
  10.7 0.7 copy-start.5
  15.4 0.7 copy-start.10
  15.4 0.8 copy-start.8
  16.3 1.5 %copy-start.4 = (bf16[256,3456]{1,0:T(8,128)(2,1)S(1)}, bf16[256,3456]{1,0:T(8,128)(2,1)}, u32[]{:S(2)}) copy-start(bf16[256,3456]{1,0:T(8,128)(2,1)} %param.9) | copy-start | bytes 5308420
  16.3 1.5 %copy-start.6 = (bf16[128,256]{1,0:T(8,128)(2,1)S(1)}, bf16[128,256]{1,0:T(8,128)(2,1)}, u32[]{:S(2)}) copy-start(bf16[128,256]{1,0:T(8,128)(2,1)} %copy-done.5) | copy-start | bytes 196612
  18.4 3.2 %copy-start.11 = (s32[26]{0:T(128)S(1)}, s32[26]{0:T(128)}, u32[]{:S(2)}) copy-start(s32[26]{0:T(128)} %param.12) | copy-start | bytes 316
  26.2 11.6 %copy-start.9 = (s32[2,4,4096]{2,1,0:T(4,128)S(1)}, s32[2,4,4096]{2,1,0:T(4,128)}, u32[]{:S(2)}) copy-start(s32[2,4,4096]{2,1,0:T(4,128)} %param.13) | copy-start | bytes 393220
  26.2 60.7 %all-to-all-start.1 = ((bf16[2,32,128,128]{3,0,2,1:T(2,128)(2,1)}), bf16[2,32,128,128]{3,0,2,1:T(2,128)(2,1)}, u32[]{:S(2)}, u32[]{:S(2)}) async-start(bf16[2,32,128,128]{3,0,2,1:T(2,128)(2,1)} %copy.22), calls=%async_computation.2 | async-start | bytes 4194304 | tf_op jit(solution)/shard_map/all_to_all | solution.py:57
  86.8 2.8 %copy-start.1 = (bf16[2,256,4096]{2,1,0:T(8,128)(2,1)S(1)}, bf16[2,256,4096]{2,1,0:T(8,128)(2,1)}, u32[]{:S(2)}) copy-start(bf16[2,256,4096]{2,1,0:T(8,128)(2,1)} %fusion.1) | copy-start | bytes 12582916
  91.6 11.8 %all-to-all-start.2 = ((f32[8,2,32,128]{3,2,1,0:T(8,128)}), f32[8,2,32,128]{3,2,1,0:T(8,128)S(1)}, u32[]{:S(2)}, u32[]{:S(2)}) async-start(f32[8,2,32,128]{3,2,1,0:T(8,128)} %bitcast.23), calls=%async_computation.3 | async-start | bytes 524288 | tf_op jit(solution)/shard_map/all_to_all | solution.py:21
  103.5 31.9 %all-to-all-start = ((f32[32,1,6912]{2,1,0:T(1,128)}), f32[32,1,6912]{2,1,0:T(1,128)S(1)}, u32[]{:S(2)}, u32[]{:S(2)}) async-start(f32[32,1,6912]{2,1,0:T(1,128)} %copy.19), calls=%async_computation.1 | async-start | bytes 1769472 | tf_op jit(solution)/shard_map/all_to_all | solution.py:21
Sparse Core Ops, SparseCore 0:
  15.5 51.3 reduce-scatter.1
where the time goes:
time: 144 us; the launch traced here: 143 us
  waiting for transfers between devices  70.2 us (49%)
  starting transfers between devices  23 us (16%)
  local copies, waits for them, and re-layouts  15.7 us (11%)
  between operations  14.3 us (10%)
  other arithmetic  12.7 us (9%)
  matrix products  7.52 us (5%)
    all_to_all x1, waiting for transfers between devices, on_device(): lax.all_to_all(outgoing, 'tbl', split_axis=1, concat_axis=1, tiled=True)  41.5 us
    all_to_all x2, waiting for transfers between devices, sum_at_owner(): lax.all_to_all(blocks, axis, split_axis=0, concat_axis=0, tiled=True)  28.7 us
    all_to_all x1, starting transfers between devices, on_device(): lax.all_to_all(outgoing, 'tbl', split_axis=1, concat_axis=1, tiled=True)  11.6 us
    all_to_all x2, starting transfers between devices, sum_at_owner(): lax.all_to_all(blocks, axis, split_axis=0, concat_axis=0, tiled=True)  11.4 us
    reduce_sum x1, other arithmetic, on_device(): jnp.sum((owned_ids[:, :, None, :] == row_numbers[None, None, :, None]).as...  7.58 us
    reshape x2, local copies, waits for them, and re-layouts, in_blocks(): shard.reshape(*shape[:dim], length, shape[dim] // length, *shape[dim + 1:])  3.73 us
    reshape x1, local copies, waits for them, and re-layouts, on_device(): outgoing.astype(jnp.bfloat16).reshape(slots_dev, n_tbl, samples, EMB)  3.48 us
    concatenate x1, other arithmetic, on_device(): jnp.concatenate([outer_sum(hidden, product_grad), outer_sum(hidden_grad,...  3.38 us
  transfers between devices with their start and end apart: 4, of which 3 were waited for; matrix products, arithmetic and copies ran while one was open for 17% of the time, Pallas kernels for 0%

commit v1 on v0

v1 whole, which is shorter than its diff:
```python
import functools
import math

import jax
import jax.numpy as jnp
from jax import lax
from jax.experimental import pallas as pl
from jax.experimental.pallas import tpu as pltpu
from jax.sharding import Mesh
from jax.sharding import PartitionSpec as P

EMB = 128
TABLES = 26
ROWS = 256
RANK = 256
BF = jnp.bfloat16
F32 = jnp.float32


def nt(left, right):
    return lax.dot_general(left, right, (((1,), (1,)), ((), ())), preferred_element_type=F32)


def tn(left, right):
    return lax.dot_general(left, right, (((0,), (0,)), ((), ())), preferred_element_type=F32)


def own_rows(full, core):
    picks = [
        jnp.where(core == 0, full[i * 64 : i * 64 + 32], full[i * 64 + 32 : i * 64 + 64])
        for i in range(4)
    ]
    return jnp.concatenate(picks, axis=0)


def dense_kernel(meta, x, px, up, pup, v, u, hid_t, hgr_t, by_x, by_y, both, prod):
    core = meta[0]
    n = x.shape[0]
    both[:n] = x[...]
    both[n:] = px[...]
    prod[:n] = (x[...].astype(F32) * up[...].astype(F32)).astype(BF)
    prod[n:] = (px[...].astype(F32) * pup[...].astype(F32)).astype(BF)
    hid = nt(v[...], both[...])
    hgr = nt(u[...], prod[...])
    hid_t[...] = hid.astype(BF)
    hgr_t[...] = hgr.astype(BF)
    hid_own = own_rows(hid, core).astype(BF)
    hgr_own = own_rows(hgr, core).astype(BF)
    width = 1152
    for k in range(x.shape[1] // width):
        cols = slice(k * width, (k + 1) * width)
        first = jnp.dot(hid_own, prod[:, cols], preferred_element_type=F32)
        for i in range(4):
            by_x[i, :, cols] = first[i * 32 : (i + 1) * 32].astype(BF)
        second = jnp.dot(hgr_own, both[:, cols], preferred_element_type=F32)
        for j in range(4):
            rows = [second[(i * 4 + j) * 8 : (i * 4 + j) * 8 + 8] for i in range(4)]
            by_y[j, :, cols] = jnp.concatenate(rows, axis=0).astype(BF)


def table_kernel(meta, hid_t, hgr_t, up, pup, u, v, bias, ids, pids, by_x, by_y, hid, hgr):
    core = meta[0]
    n = up.shape[0]
    hid[...] = hid_t[...].astype(F32).T.astype(BF)
    hgr[...] = hgr_t[...].astype(F32).T.astype(BF)
    at = lax.broadcasted_iota(jnp.int32, (128, n), 0)
    row_x = (at // 32) * 64 + core * 32 + at % 32
    row_y = ((at // 8) % 4) * 64 + core * 32 + (at // 32) * 8 + at % 8
    for pair in range(TABLES // 2):
        cols = slice(EMB + pair * 256, EMB + pair * 256 + 256)
        mixed = jnp.dot(hid[...], u[:, cols], preferred_element_type=F32) + bias[:, cols]
        back = jnp.dot(hgr[...], v[:, cols], preferred_element_type=F32)
        up_float = jnp.concatenate([up[:, cols], pup[:, cols]], axis=0).astype(F32)
        pooled = (up_float * (1.0 + mixed) + back).astype(BF)
        for which in range(2):
            table = 2 * pair + which
            owner = meta[1 + table]
            slot = meta[1 + TABLES + table]
            row = row_y if which else row_x
            counts = []
            for source in (ids, pids):
                eight = source[owner]
                four = jnp.where(slot == 0, eight[:4], eight[4:])
                count = jnp.where(four[0:1] == row, 1.0, 0.0)
                for k in range(1, 4):
                    count = count + jnp.where(four[k : k + 1] == row, 1.0, 0.0)
                counts.append(count.astype(BF))
            total = jnp.dot(
                jnp.concatenate(counts, axis=1),
                pooled[:, which * EMB : (which + 1) * EMB],
                preferred_element_type=F32,
            )
            out = by_y if which else by_x
            for i in range(4):
                out[i, pair] = total[i * 32 : (i + 1) * 32].astype(BF)


def sum4(arrived):
    return arrived.astype(F32).sum(axis=0)


def on_device(cross_input, upstream, v_weight, u_weight, bias, placement, owned_ids):
    samples, width = cross_input.shape
    scale = 1.0 / math.sqrt(samples * 256)
    core = lax.axis_index("c").astype(jnp.int32)
    swap = [(0, 1), (1, 0)]
    vmem = pl.BlockSpec(memory_space=pltpu.VMEM)
    smem = pl.BlockSpec(memory_space=pltpu.SMEM)
    params = pltpu.CompilerParams(vmem_limit_bytes=48 << 20)

    with jax.named_scope("ids"):
        ids = owned_ids.astype(jnp.int16).reshape(8, 32, samples).transpose(1, 0, 2)
        ids = lax.all_to_all(ids, ("y", "z"), 0, 0, tiled=True)
        pids = lax.ppermute(ids, "c", swap)
        ids = ids.astype(jnp.int32)
        pids = pids.astype(jnp.int32)

    same = placement[:, None] == placement[None, :]
    earlier = jnp.arange(TABLES)[None, :] < jnp.arange(TABLES)[:, None]
    slot = jnp.sum((same & earlier).astype(jnp.int32), axis=1)
    meta = jnp.concatenate([core[None], placement, slot])

    with jax.named_scope("swap"):
        px = lax.ppermute(cross_input, "c", swap)
        pup = lax.ppermute(upstream, "c", swap)

    hid_t, hgr_t, cross_x, cross_y = pl.pallas_call(
        dense_kernel,
        out_shape=(
            jax.ShapeDtypeStruct((RANK, 2 * samples), BF),
            jax.ShapeDtypeStruct((RANK, 2 * samples), BF),
            jax.ShapeDtypeStruct((4, 32, width), BF),
            jax.ShapeDtypeStruct((4, 32, width), BF),
        ),
        in_specs=[smem] + [vmem] * 6,
        out_specs=(vmem,) * 4,
        scratch_shapes=[
            pltpu.VMEM((2 * samples, width), BF),
            pltpu.VMEM((2 * samples, width), BF),
        ],
        compiler_params=params,
        name="dense",
    )(meta, cross_input, px, upstream, pup, v_weight, u_weight)

    with jax.named_scope("cross1"):
        cross_x = lax.all_to_all(cross_x, "x", 0, 0, tiled=True)
        cross_y = lax.all_to_all(cross_y, "y", 0, 0, tiled=True)

    table_x, table_y = pl.pallas_call(
        table_kernel,
        out_shape=(
            jax.ShapeDtypeStruct((4, TABLES // 2, 32, EMB), BF),
            jax.ShapeDtypeStruct((4, TABLES // 2, 32, EMB), BF),
        ),
        in_specs=[smem] + [vmem] * 9,
        out_specs=(vmem,) * 2,
        scratch_shapes=[
            pltpu.VMEM((2 * samples, RANK), BF),
            pltpu.VMEM((2 * samples, RANK), BF),
        ],
        compiler_params=params,
        name="tables",
    )(meta, hid_t, hgr_t, upstream, pup, u_weight, v_weight, bias[None], ids, pids)

    with jax.named_scope("table1"):
        table_x = lax.all_to_all(table_x, "x", 0, 0, tiled=True)
        table_y = lax.all_to_all(table_y, "y", 0, 0, tiled=True)

    with jax.named_scope("cross2"):
        cross_x = sum4(cross_x).astype(BF).reshape(4, 8, width)
        cross_y = sum4(cross_y).astype(BF).reshape(4, 8, width)
        cross_x = lax.all_to_all(cross_x, "y", 0, 0, tiled=True)
        cross_y = lax.all_to_all(cross_y, "x", 0, 0, tiled=True)

    with jax.named_scope("table2"):
        table_x = sum4(table_x).astype(BF).reshape(TABLES // 2, 4, 8, EMB).transpose(1, 0, 2, 3)
        table_y = sum4(table_y).astype(BF).reshape(TABLES // 2, 4, 8, EMB).transpose(1, 0, 2, 3)
        table_x = lax.all_to_all(table_x, "y", 0, 0, tiled=True)
        table_y = lax.all_to_all(table_y, "x", 0, 0, tiled=True)

    with jax.named_scope("cross3"):
        cross = jnp.concatenate([sum4(cross_x), sum4(cross_y)], axis=1)
        cross = cross.reshape(8, 54, EMB)
        cross = lax.all_to_all(cross, "z", 0, 0, tiled=True)
        cross_grad = (cross.sum(axis=0) * scale).reshape(1, 2 * width)

    with jax.named_scope("table3"):
        tables = jnp.stack([sum4(table_x), sum4(table_y)], axis=1).reshape(TABLES, 8 * EMB)
        place = (placement % 8) * 8 + (placement // 8) * 2 + slot
        select = (jnp.arange(64, dtype=jnp.int32)[:, None] == place[None, :]).astype(BF)
        routed = jnp.dot(select, tables.astype(BF), preferred_element_type=F32).astype(BF)
        routed = routed.reshape(8, 8, 8, EMB)
        routed = lax.all_to_all(routed, "z", 0, 0, tiled=True)
        routed = routed.astype(F32).sum(axis=0).reshape(4, 2, 8, EMB)

    with jax.named_scope("table4"):
        routed = lax.all_to_all(routed, "y", 0, 0, tiled=True)
        table_grad = routed.transpose(1, 0, 2, 3).reshape(2, 32, EMB)
    return (cross_grad, table_grad)


def solution(mesh):
    fine = Mesh(mesh.devices.reshape(4, 2, 4, 8), ("x", "c", "y", "z"))
    grp, tbl = ("x", "c"), ("y", "z")
    in_specs = (
        P(grp + tbl, None),
        P(grp + tbl, None),
        P(),
        P(),
        P(),
        P(),
        P(tbl, None, grp),
    )
    out_specs = (P(grp + tbl, None), P(tbl, grp, None))
    return jax.shard_map(
        on_device, mesh=fine, in_specs=in_specs, out_specs=out_specs, check_vma=False
    )
```

time: 144 us -> 161 us (1.12)
  blocking collectives: 0 us -> 35.1 us
  starting transfers between devices: 23 us -> 41.1 us
  between operations: 14.3 us -> 0.86 us
  waiting for transfers between devices: 70.2 us -> 59.1 us
  Pallas kernels: 0 us -> 10.9 us
  other arithmetic: 12.7 us -> 4.6 us
  local copies, waits for them, and re-layouts: 15.7 us -> 7.86 us
  matrix products: 7.52 us -> 0.16 us
    all_to_all x0 -> x3, blocking collectives: none -> 35.1 us  [the longest x1 12.4 us: on_device(): cross_y = lax.all_to_all(cross_y, 'y', 0, 0, tiled=True)]
    all_to_all x3 -> x9, starting transfers between devices: 23 us -> 40.6 us  [the longest x1 11.4 us: on_device(): ids = lax.all_to_all(ids, ('y', 'z'), 0, 0, tiled=True)]
    all_to_all x3 -> x9, waiting for transfers between devices: 70.2 us -> 58.6 us  [the longest x1 9.47 us: on_device(): cross_x = lax.all_to_all(cross_x, 'x', 0, 0, tiled=True)]
    pallas_call x0 -> x2, Pallas kernels: none -> 10.9 us  [the longest x1 6.16 us: on_device(): pl.pallas_call(table_kernel, out_shape=(jax.ShapeDtypeStruct((4, TABLES /...]
    dot_general x8 -> x1, matrix products: 7.52 us -> 0.16 us  [on_device(): jnp.dot(select, tables.astype(BF), preferred_element_type=F32).astype(BF)]
    reshape x4, local copies, waits for them, and re-layouts: 9.13 us -> 2.06 us  [the longest x2 0.73 us: on_device(): ids = owned_ids.astype(jnp.int16).reshape(8, 32, samples).transpose(1, 0, 2)]
    reduce_sum x3 -> x10, other arithmetic: 8.72 us -> 1.95 us  [the longest x8 1.91 us: sum4(): return arrived.astype(F32).sum(axis=0)]
    concatenate x1, other arithmetic: 3.38 us -> 0.73 us  [on_device(): meta = jnp.concatenate([core[None], placement, slot])]
  transfers between devices with their start and end apart: 4 -> 12, of which waited for: 3 -> 10; matrix products, arithmetic and copies ran while one was open for 17% -> 6% of each run, Pallas kernels for 0% -> 0%
where the time goes in v1:
time: 161 us; the launch traced here: 160 us
  waiting for transfers between devices  59.1 us (37%)
  starting transfers between devices  41.1 us (26%)
  blocking collectives  35.1 us (22%)
  Pallas kernels  10.9 us (7%)
  local copies, waits for them, and re-layouts  7.86 us (5%)
  other arithmetic  4.6 us (3%)
    all_to_all x1, blocking collectives, on_device(): cross_y = lax.all_to_all(cross_y, 'y', 0, 0, tiled=True)  12.4 us
    all_to_all x1, blocking collectives, on_device(): table_y = lax.all_to_all(table_y, 'y', 0, 0, tiled=True)  11.5 us
    all_to_all x1, starting transfers between devices, on_device(): ids = lax.all_to_all(ids, ('y', 'z'), 0, 0, tiled=True)  11.4 us
    all_to_all x1, blocking collectives, on_device(): routed = lax.all_to_all(routed, 'z', 0, 0, tiled=True)  11.2 us
    all_to_all x1, waiting for transfers between devices, on_device(): cross_x = lax.all_to_all(cross_x, 'x', 0, 0, tiled=True)  9.47 us
    all_to_all x1, waiting for transfers between devices, on_device(): cross = lax.all_to_all(cross, 'z', 0, 0, tiled=True)  7.82 us
    all_to_all x1, waiting for transfers between devices, on_device(): ids = lax.all_to_all(ids, ('y', 'z'), 0, 0, tiled=True)  7.48 us
    all_to_all x1, waiting for transfers between devices, on_device(): table_x = lax.all_to_all(table_x, 'x', 0, 0, tiled=True)  7.01 us
  transfers between devices with their start and end apart: 12, of which 10 were waited for; matrix products, arithmetic and copies ran while one was open for 6% of the time, Pallas kernels for 0%

profile of v1, /device:TPU:32, one launch (start us, length us, event | category | flops | bytes accessed | tf_op | source)
XLA Modules:
  0.0 159.7 jit_solution(16368103207053329351)
XLA Ops:
  0.6 0.1 collective-permute-start
  0.7 0.5 collective-permute-start.1
  1.2 0.9 convert_element_type.46
  2.2 0.1 reshape.52
  2.2 0.6 copy.32
  2.9 11.4 %all-to-all-start.5 = ((s16[32,8,128]{2,1,0:T(8,128)(2,1)}), s16[32,8,128]{2,1,0:T(8,128)(2,1)S(1)}, u32[]{:S(2)}, u32[]{:S(2)}) async-start(s16[32,8,128]{2,1,0:T(8,128)(2,1)} %bitcast.33), calls=%async_computation.5 | async-start | bytes 131072 | tf_op jit(solution)/shard_map/ids/all_to_all | solution.py:113
  14.3 0.7 broadcast_in_dim.5.bias
  15.0 0.9 convert_reduce_fusion.3
  15.9 7.5 %all-to-all-done.5 = s16[32,8,128]{2,1,0:T(8,128)(2,1)S(1)} async-done(((s16[32,8,128]{2,1,0:T(8,128)(2,1)}), s16[32,8,128]{2,1,0:T(8,128)(2,1)S(1)}, u32[]{:S(2)}, u32[]{:S(2)}) %all-to-all-start.5) | async-done | bytes 65568 | tf_op jit(solution)/shard_map/ids/all_to_all | solution.py:113
  23.4 0.7 pad_add_fusion.meta
  24.1 0.5 collective-permute-done.2
  24.7 0.0 copy-start
  24.7 0.0 collective-permute-done.1.pup
  24.7 0.0 copy-start.1
  24.7 1.3 copy-done.1
  26.0 1.2 copy-done.2
  27.1 4.7 %dense.1 = (bf16[256,256]{1,0:T(8,128)(2,1)S(1)}, bf16[256,256]{1,0:T(8,128)(2,1)S(1)}, bf16[4,32,3456]{2,1,0:T(8,128)(2,1)}, bf16[4,32,3456]{2,1,0:T(8,128)(2,1)S(1)}) custom-call(s32[53]{0:T(128)S(1)} %pad_add_fusion.meta, bf16[128,3456]{1,0:T(8,128)(2,1)S(1)} %copy-done.2, bf16[128,3456]{1,0:T(8,128)(2,1)S(1)} %collective-permute-done.px, ...), custom_call_target="tpu_custom_call" | custom-call | tf_op jit(solution)/shard_map/dense/pallas_call | solution.py:127
  31.9 6.2 %tables.1 = (bf16[4,13,32,128]{3,2,1,0:T(8,128)(2,1)}, bf16[4,13,32,128]{3,2,1,0:T(8,128)(2,1)S(1)}) custom-call(s32[53]{0:T(128)S(1)} %pad_add_fusion.meta, bf16[256,256]{1,0:T(8,128)(2,1)S(1)} %get-tuple-element.10.hid_t, bf16[256,256]{1,0:T(8,128)(2,1)S(1)} %get-tuple-element.11.hgr_t, bf16[128,3456]{1,0:T(8,128)(2,1)S(1)} %copy-done.1, ...), custom_call_target="tpu_custom_call" | custom-call | tf_op jit(solution)/shard_map/tables/pallas_call | solution.py:149
  38.0 11.5 %all_to_all.60 = bf16[4,13,32,128]{3,2,1,0:T(8,128)(2,1)S(1)} all-to-all(bf16[4,13,32,128]{3,2,1,0:T(8,128)(2,1)S(1)} %get-tuple-element.13), channel_id=1, replica_groups=mesh['x'=4,'c'=2,'y'=4,'z'=8] {'y'}, dimensions={0} | all-to-all | bytes 851968 | tf_op jit(solution)/shard_map/table1/all_to_all | solution.py:167
  49.6 4.3 %all-to-all-start.6 = ((bf16[4,13,32,128]{3,2,1,0:T(8,128)(2,1)}), bf16[4,13,32,128]{3,2,1,0:T(8,128)(2,1)S(1)}, u32[]{:S(2)}, u32[]{:S(2)}) async-start(bf16[4,13,32,128]{3,2,1,0:T(8,128)(2,1)} %get-tuple-element.12), calls=%async_computation.6 | async-start | bytes 851968 | tf_op jit(solution)/shard_map/table1/all_to_all | solution.py:166
  53.9 0.1 reduce_sum.119
  53.9 0.7 copy.24
  54.6 7.0 %all-to-all-done.6 = bf16[4,13,32,128]{3,2,1,0:T(8,128)(2,1)S(1)} async-done(((bf16[4,13,32,128]{3,2,1,0:T(8,128)(2,1)}), bf16[4,13,32,128]{3,2,1,0:T(8,128)(2,1)S(1)}, u32[]{:S(2)}, u32[]{:S(2)}) %all-to-all-start.6) | async-done | bytes 426016 | tf_op jit(solution)/shard_map/table1/all_to_all | solution.py:166
  61.6 3.3 %all-to-all-start.9 = ((bf16[4,13,8,128]{3,2,1,0:T(8,128)(2,1)}), bf16[4,13,8,128]{3,2,1,0:T(8,128)(2,1)S(1)}, u32[]{:S(2)}, u32[]{:S(2)}) async-start(bf16[4,13,8,128]{3,2,1,0:T(8,128)(2,1)} %copy.24), calls=%async_computation.9 | async-start | bytes 212992 | tf_op jit(solution)/shard_map/table2/all_to_all | solution.py:179
  64.9 0.1 reduce_sum.117
  65.0 0.7 copy.23
  65.6 5.1 %all-to-all-done.9 = bf16[4,13,8,128]{3,2,1,0:T(8,128)(2,1)S(1)} async-done(((bf16[4,13,8,128]{3,2,1,0:T(8,128)(2,1)}), bf16[4,13,8,128]{3,2,1,0:T(8,128)(2,1)S(1)}, u32[]{:S(2)}, u32[]{:S(2)}) %all-to-all-start.9) | async-done | bytes 106528 | tf_op jit(solution)/shard_map/table2/all_to_all | solution.py:179
  70.7 3.3 %all-to-all-start.7 = ((bf16[4,13,8,128]{3,2,1,0:T(8,128)(2,1)}), bf16[4,13,8,128]{3,2,1,0:T(8,128)(2,1)S(1)}, u32[]{:S(2)}, u32[]{:S(2)}) async-start(bf16[4,13,8,128]{3,2,1,0:T(8,128)(2,1)} %copy.23), calls=%async_computation.7 | async-start | bytes 212992 | tf_op jit(solution)/shard_map/table2/all_to_all | solution.py:178
  74.1 5.8 %all-to-all-done.7 = bf16[4,13,8,128]{3,2,1,0:T(8,128)(2,1)S(1)} async-done(((bf16[4,13,8,128]{3,2,1,0:T(8,128)(2,1)}), bf16[4,13,8,128]{3,2,1,0:T(8,128)(2,1)S(1)}, u32[]{:S(2)}, u32[]{:S(2)}) %all-to-all-start.7) | async-done | bytes 106528 | tf_op jit(solution)/shard_map/table2/all_to_all | solution.py:178
  79.9 0.2 fusion
  80.1 11.2 %all_to_all.61 = bf16[8,8,8,128]{3,1,2,0:T(8,128)(2,1)S(1)} all-to-all(bf16[8,8,8,128]{3,1,2,0:T(8,128)(2,1)S(1)} %fusion), channel_id=1, replica_groups=mesh['x'=4,'c'=2,'y'=4,'z'=8] {'z'}, dimensions={0} | all-to-all | bytes 262144 | tf_op jit(solution)/shard_map/table3/all_to_all | solution.py:193
  91.3 12.4 %all_to_all.62 = bf16[4,32,3456]{2,1,0:T(8,128)(2,1)S(1)} all-to-all(bf16[4,32,3456]{2,1,0:T(8,128)(2,1)S(1)} %get-tuple-element.9), channel_id=1, replica_groups=mesh['x'=4,'c'=2,'y'=4,'z'=8] {'y'}, dimensions={0} | all-to-all | bytes 1769472 | tf_op jit(solution)/shard_map/cross1/all_to_all | solution.py:147
  103.7 3.5 %all-to-all-start = ((bf16[4,32,3456]{2,1,0:T(8,128)(2,1)}), bf16[4,32,3456]{2,1,0:T(8,128)(2,1)S(1)}, u32[]{:S(2)}, u32[]{:S(2)}) async-start(bf16[4,32,3456]{2,1,0:T(8,128)(2,1)} %get-tuple-element.8), calls=%async_computation | async-start | bytes 1769472 | tf_op jit(solution)/shard_map/cross1/all_to_all | solution.py:146
  107.2 0.8 reduce_sum.114
  108.0 9.5 %all-to-all-done = bf16[4,32,3456]{2,1,0:T(8,128)(2,1)S(1)} async-done(((bf16[4,32,3456]{2,1,0:T(8,128)(2,1)}), bf16[4,32,3456]{2,1,0:T(8,128)(2,1)S(1)}, u32[]{:S(2)}, u32[]{:S(2)}) %all-to-all-start) | async-done | bytes 884768 | tf_op jit(solution)/shard_map/cross1/all_to_all | solution.py:146
  117.5 3.4 %all-to-all-start.3 = ((bf16[4,8,3456]{2,1,0:T(8,128)(2,1)}), bf16[4,8,3456]{2,1,0:T(8,128)(2,1)S(1)}, u32[]{:S(2)}, u32[]{:S(2)}) async-start(bf16[4,8,3456]{2,1,0:T(8,128)(2,1)} %bitcast.2), calls=%async_computation.3 | async-start | bytes 442368 | tf_op jit(solution)/shard_map/cross2/all_to_all | solution.py:173
  120.9 0.8 reduce_sum.112
  121.7 5.6 %all-to-all-done.3 = bf16[4,8,3456]{2,1,0:T(8,128)(2,1)S(1)} async-done(((bf16[4,8,3456]{2,1,0:T(8,128)(2,1)}), bf16[4,8,3456]{2,1,0:T(8,128)(2,1)S(1)}, u32[]{:S(2)}, u32[]{:S(2)}) %all-to-all-start.3) | async-done | bytes 221216 | tf_op jit(solution)/shard_map/cross2/all_to_all | solution.py:173
  127.3 3.4 %all-to-all-start.1 = ((bf16[4,8,3456]{2,1,0:T(8,128)(2,1)}), bf16[4,8,3456]{2,1,0:T(8,128)(2,1)S(1)}, u32[]{:S(2)}, u32[]{:S(2)}) async-start(bf16[4,8,3456]{2,1,0:T(8,128)(2,1)} %bitcast.1), calls=%async_computation.1 | async-start | bytes 442368 | tf_op jit(solution)/shard_map/cross2/all_to_all | solution.py:172
  130.7 0.6 copy.25
  131.4 5.7 %all-to-all-done.1 = bf16[4,8,3456]{2,1,0:T(8,128)(2,1)S(1)} async-done(((bf16[4,8,3456]{2,1,0:T(8,128)(2,1)}), bf16[4,8,3456]{2,1,0:T(8,128)(2,1)S(1)}, u32[]{:S(2)}, u32[]{:S(2)}) %all-to-all-start.1) | async-done | bytes 221216 | tf_op jit(solution)/shard_map/cross2/all_to_all | solution.py:172
  137.1 3.3 %all-to-all-start.11 = ((f32[4,2,8,128]{3,2,1,0:T(8,128)}), f32[4,2,8,128]{3,2,1,0:T(8,128)S(1)}, u32[]{:S(2)}, u32[]{:S(2)}) async-start(f32[4,2,8,128]{3,2,1,0:T(8,128)} %bitcast.12), calls=%async_computation.11 | async-start | bytes 65536 | tf_op jit(solution)/shard_map/table4/all_to_all | solution.py:197
  140.5 0.7 copy.21
  141.2 4.6 %all-to-all-done.11 = f32[4,2,8,128]{3,2,1,0:T(8,128)S(1)} async-done(((f32[4,2,8,128]{3,2,1,0:T(8,128)}), f32[4,2,8,128]{3,2,1,0:T(8,128)S(1)}, u32[]{:S(2)}, u32[]{:S(2)}) %all-to-all-start.11) | async-done | bytes 32800 | tf_op jit(solution)/shard_map/table4/all_to_all | solution.py:197
  145.8 4.8 %all-to-all-start.4 = ((f32[8,54,128]{2,1,0:T(8,128)}), f32[8,54,128]{2,1,0:T(8,128)S(1)}, u32[]{:S(2)}, u32[]{:S(2)}) async-start(f32[8,54,128]{2,1,0:T(8,128)} %copy.21), calls=%async_computation.4 | async-start | bytes 458752 | tf_op jit(solution)/shard_map/cross3/all_to_all | solution.py:184
  150.6 0.6 copy_bitcast_fusion.1
  151.2 7.8 %all-to-all-done.4 = f32[8,54,128]{2,1,0:T(8,128)S(1)} async-done(((f32[8,54,128]{2,1,0:T(8,128)}), f32[8,54,128]{2,1,0:T(8,128)S(1)}, u32[]{:S(2)}, u32[]{:S(2)}) %all-to-all-start.4) | async-done | bytes 221216 | tf_op jit(solution)/shard_map/cross3/all_to_all | solution.py:184
  159.0 0.6 copy.33
  (20 shorter events, 0.3 us)
Async XLA Ops:
  0.6 24.0 %collective-permute-start = (bf16[128,3456]{1,0:T(8,128)(2,1)}, bf16[128,3456]{1,0:T(8,128)(2,1)S(1)}, u32[]{:S(2)}, u32[]{:S(2)}) collective-permute-start(bf16[128,3456]{1,0:T(8,128)(2,1)} %x.1), channel_id=1, source_target_pairs={{0,32},{32,0},{1,33},{33,1},{2,34},{34,2},{3,35},{35,3},{4,36},{36... | collective-permute-start | bytes 2654216 | tf_op jit(solution)/shard_map/swap/ppermute | solution.py:124
  0.7 23.9 %collective-permute-start.1 = (bf16[128,3456]{1,0:T(8,128)(2,1)}, bf16[128,3456]{1,0:T(8,128)(2,1)S(1)}, u32[]{:S(2)}, u32[]{:S(2)}) collective-permute-start(bf16[128,3456]{1,0:T(8,128)(2,1)} %up.3), channel_id=1, source_target_pairs={{0,32},{32,0},{1,33},{33,1},{2,34},{34,2},{3,35},{35,3},{4,36},{36... | collective-permute-start | bytes 2654216 | tf_op jit(solution)/shard_map/swap/ppermute | solution.py:125
  2.9 20.5 %all-to-all-start.5 = ((s16[32,8,128]{2,1,0:T(8,128)(2,1)}), s16[32,8,128]{2,1,0:T(8,128)(2,1)S(1)}, u32[]{:S(2)}, u32[]{:S(2)}) async-start(s16[32,8,128]{2,1,0:T(8,128)(2,1)} %bitcast.33), calls=%async_computation.5 | async-start | bytes 131072 | tf_op jit(solution)/shard_map/ids/all_to_all | solution.py:113
  23.4 1.3 collective-permute-start.2
  24.7 7.2 %copy-start = (bf16[256,3456]{1,0:T(8,128)(2,1)S(1)}, bf16[256,3456]{1,0:T(8,128)(2,1)}, u32[]{:S(2)}) copy-start(bf16[256,3456]{1,0:T(8,128)(2,1)} %u.3) | copy-start | bytes 5308420
  24.7 1.3 copy-start.1
  26.0 1.2 copy-start.2
  38.0 36.0 %copy-start.3 = (s32[26]{0:T(128)S(1)}, s32[26]{0:T(128)}, u32[]{:S(2)}) copy-start(s32[26]{0:T(128)} %param.12) | copy-start | bytes 316
  49.6 12.0 %all-to-all-start.6 = ((bf16[4,13,32,128]{3,2,1,0:T(8,128)(2,1)}), bf16[4,13,32,128]{3,2,1,0:T(8,128)(2,1)S(1)}, u32[]{:S(2)}, u32[]{:S(2)}) async-start(bf16[4,13,32,128]{3,2,1,0:T(8,128)(2,1)} %get-tuple-element.12), calls=%async_computation.6 | async-start | bytes 851968 | tf_op jit(solution)/shard_map/table1/all_to_all | solution.py:166
  61.6 9.1 %all-to-all-start.9 = ((bf16[4,13,8,128]{3,2,1,0:T(8,128)(2,1)}), bf16[4,13,8,128]{3,2,1,0:T(8,128)(2,1)S(1)}, u32[]{:S(2)}, u32[]{:S(2)}) async-start(bf16[4,13,8,128]{3,2,1,0:T(8,128)(2,1)} %copy.24), calls=%async_computation.9 | async-start | bytes 212992 | tf_op jit(solution)/shard_map/table2/all_to_all | solution.py:179
  70.7 9.1 %all-to-all-start.7 = ((bf16[4,13,8,128]{3,2,1,0:T(8,128)(2,1)}), bf16[4,13,8,128]{3,2,1,0:T(8,128)(2,1)S(1)}, u32[]{:S(2)}, u32[]{:S(2)}) async-start(bf16[4,13,8,128]{3,2,1,0:T(8,128)(2,1)} %copy.23), calls=%async_computation.7 | async-start | bytes 212992 | tf_op jit(solution)/shard_map/table2/all_to_all | solution.py:178
  103.7 13.8 %all-to-all-start = ((bf16[4,32,3456]{2,1,0:T(8,128)(2,1)}), bf16[4,32,3456]{2,1,0:T(8,128)(2,1)S(1)}, u32[]{:S(2)}, u32[]{:S(2)}) async-start(bf16[4,32,3456]{2,1,0:T(8,128)(2,1)} %get-tuple-element.8), calls=%async_computation | async-start | bytes 1769472 | tf_op jit(solution)/shard_map/cross1/all_to_all | solution.py:146
  117.5 9.8 %all-to-all-start.3 = ((bf16[4,8,3456]{2,1,0:T(8,128)(2,1)}), bf16[4,8,3456]{2,1,0:T(8,128)(2,1)S(1)}, u32[]{:S(2)}, u32[]{:S(2)}) async-start(bf16[4,8,3456]{2,1,0:T(8,128)(2,1)} %bitcast.2), calls=%async_computation.3 | async-start | bytes 442368 | tf_op jit(solution)/shard_map/cross2/all_to_all | solution.py:173
  127.3 9.8 %all-to-all-start.1 = ((bf16[4,8,3456]{2,1,0:T(8,128)(2,1)}), bf16[4,8,3456]{2,1,0:T(8,128)(2,1)S(1)}, u32[]{:S(2)}, u32[]{:S(2)}) async-start(bf16[4,8,3456]{2,1,0:T(8,128)(2,1)} %bitcast.1), calls=%async_computation.1 | async-start | bytes 442368 | tf_op jit(solution)/shard_map/cross2/all_to_all | solution.py:172
  137.1 8.7 %all-to-all-start.11 = ((f32[4,2,8,128]{3,2,1,0:T(8,128)}), f32[4,2,8,128]{3,2,1,0:T(8,128)S(1)}, u32[]{:S(2)}, u32[]{:S(2)}) async-start(f32[4,2,8,128]{3,2,1,0:T(8,128)} %bitcast.12), calls=%async_computation.11 | async-start | bytes 65536 | tf_op jit(solution)/shard_map/table4/all_to_all | solution.py:197
  145.8 13.2 %all-to-all-start.4 = ((f32[8,54,128]{2,1,0:T(8,128)}), f32[8,54,128]{2,1,0:T(8,128)S(1)}, u32[]{:S(2)}, u32[]{:S(2)}) async-start(f32[8,54,128]{2,1,0:T(8,128)} %copy.21), calls=%async_computation.4 | async-start | bytes 458752 | tf_op jit(solution)/shard_map/cross3/all_to_all | solution.py:184

commit v2 on v0

v2 whole, which is shorter than its diff:
```python
import math

import jax
import jax.numpy as jnp
from jax import lax
from jax.experimental import pallas as pl
from jax.experimental.pallas import tpu as pltpu
from jax.sharding import Mesh
from jax.sharding import PartitionSpec as P

EMB = 128
TABLES = 26
RANK = 256
NX, NY, NZ = 4, 4, 8
NJ = NY * NZ
BF = jnp.bfloat16
F32 = jnp.float32
I32 = jnp.int32
I16 = jnp.int16

CORE, ME, OWNER, SLOT, TABLE_AT = 0, 1, 2, 2 + TABLES, 2 + 2 * TABLES
VMEM = pl.BlockSpec(memory_space=pltpu.VMEM)
SMEM = pl.BlockSpec(memory_space=pltpu.SMEM)
HBM = pl.BlockSpec(memory_space=pltpu.HBM)


def nt(left, right):
    return lax.dot_general(left, right, (((1,), (1,)), ((), ())), preferred_element_type=F32)


def mm(left, right):
    return jnp.dot(left, right, preferred_element_type=F32)


def call(kernel, name, outs, *args, specs=None, out_specs=None, scratch=(), flops=0, size=0, vmem=24 << 20):
    return pl.pallas_call(
        kernel,
        out_shape=tuple(jax.ShapeDtypeStruct(shape, dtype) for shape, dtype in outs),
        in_specs=specs or [SMEM] + [VMEM] * (len(args) - 1),
        out_specs=tuple(out_specs or [VMEM] * len(outs)),
        scratch_shapes=list(scratch),
        compiler_params=pltpu.CompilerParams(vmem_limit_bytes=vmem),
        cost_estimate=pl.CostEstimate(flops=flops, bytes_accessed=size, transcendentals=0),
        name=name,
    )(*args)


def half_of(bit):
    return [p for p in range(NJ) if p >> bit & 1]


def ids_start(meta, ids, pids, state, sent, *, bit):
    for p in range(NJ):
        start = pl.multiple_of(jnp.bitwise_xor(meta[ME], p) * EMB, EMB)
        parts = [ref[s, :, pl.ds(start, EMB)] for ref in (ids, pids) for s in range(2)]
        state[p] = jnp.concatenate(parts, axis=0).astype(I16)
    for k, p in enumerate(half_of(bit)):
        sent[k] = state[p]


def ids_step(old, came, state, sent, *, last, bit):
    for p in range(NJ):
        if not p >> last & 1:
            state[p] = old[p]
    for k, p in enumerate(half_of(last)):
        state[p] = came[k]
    for k, p in enumerate(half_of(bit)):
        sent[k] = state[p]


def own_rows(full, core):
    picks = [
        jnp.where(core == 0, full[i * 64 : i * 64 + 32], full[i * 64 + 32 : i * 64 + 64])
        for i in range(NX)
    ]
    return jnp.concatenate(picks, axis=0)


def loads_of(pairs, sems):
    loads = [
        pltpu.make_async_copy(source, target, sems.at[k])
        for k, (source, target) in enumerate(pairs)
    ]
    for load in loads:
        load.start()
    return loads


def dense_kernel(meta, x, px, up, pup, v, u, hid_out, hgr_out, out, *scratch):
    both, ups, vv, uu, prod, hid, hgr, held, in_sems, out_sems = scratch
    n, width = x.shape
    loads = loads_of(
        (
            (x, both.at[:n]),
            (px, both.at[n:]),
            (v, vv),
            (up, ups.at[:n]),
            (pup, ups.at[n:]),
            (u, uu),
        ),
        in_sems,
    )
    for load in loads[:3]:
        load.wait()
    hid[...] = nt(vv[...], both[...]).astype(BF)
    loads[3].wait()
    loads[4].wait()
    prod[...] = (both[...].astype(F32) * ups[...].astype(F32)).astype(BF)
    loads[5].wait()
    hgr[...] = nt(uu[...], prod[...]).astype(BF)
    copies = loads_of(((hid, hid_out), (hgr, hgr_out)), out_sems)
    hid_own = own_rows(hid[...].astype(F32), meta[CORE]).astype(BF)
    hgr_own = own_rows(hgr[...].astype(F32), meta[CORE]).astype(BF)
    step = 1152
    for side, (left, right) in enumerate(((hid_own, prod), (hgr_own, both))):
        for k in range(width // step):
            total = mm(left, right[:, k * step : (k + 1) * step])
            cols = slice(side * width + k * step, side * width + (k + 1) * step)
            for i in range(NX):
                held[i, :, cols] = total[i * 32 : (i + 1) * 32].astype(BF)
            copies.append(
                pltpu.make_async_copy(
                    held.at[:, :, cols], out.at[:, :, cols], out_sems.at[len(copies)]
                )
            )
            copies[-1].start()
    for copy in copies:
        copy.wait()


def table_kernel(meta, hid_in, hgr_in, up_in, pup_in, u_in, v_in, bias, ids, came, out, *scratch, last):
    state, counts, hid, hgr, ups, u, v, held, in_sems, out_sem = scratch
    n = up_in.shape[0]
    loads = loads_of(
        (
            (hid_in, hid),
            (hgr_in, hgr),
            (u_in, u),
            (v_in, v),
            (up_in, ups.at[:n]),
            (pup_in, ups.at[n:]),
        ),
        in_sems,
    )
    for p in range(NJ):
        if not p >> last & 1:
            state[p] = ids[p].astype(I32)
    for k, p in enumerate(half_of(last)):
        state[p] = came[k].astype(I32)
    at = lax.broadcasted_iota(I32, (RANK // 2, n), 0)
    row = (at // 32) * 64 + meta[CORE] * 32 + at % 32
    for table in range(TABLES):
        slot = meta[SLOT + table]
        looked = state[jnp.bitwise_xor(meta[ME], meta[OWNER + table])]
        for half in range(2):
            eight = looked[half * 8 : half * 8 + 8]
            four = jnp.where(slot == 0, eight[:4], eight[4:])
            count = jnp.where(four[0:1] == row, 1.0, 0.0)
            for k in range(1, 4):
                count = count + jnp.where(four[k : k + 1] == row, 1.0, 0.0)
            counts[table, :, half * n : (half + 1) * n] = count.astype(BF)
    for load in loads:
        load.wait()
    hid_s = hid[...].astype(F32).T.astype(BF)
    hgr_s = hgr[...].astype(F32).T.astype(BF)
    for pair in range(TABLES // 2):
        cols = slice(EMB + pair * 256, EMB + pair * 256 + 256)
        mixed = mm(hid_s, u[:, cols]) + bias[:, cols]
        back = mm(hgr_s, v[:, cols])
        pooled = (ups[:, cols].astype(F32) * (1.0 + mixed) + back).astype(BF)
        for which in range(2):
            table = 2 * pair + which
            total = mm(counts[table], pooled[:, which * EMB : (which + 1) * EMB])
            for k in range(NX * NY):
                held[k, table] = total[k * 8 : (k + 1) * 8].astype(BF)
    copy = pltpu.make_async_copy(held, out, out_sem.at[0])
    copy.start()
    copy.wait()


def cross_kernel(came, out, sums):
    blocks = came.shape[2] // EMB
    for k in range(blocks):
        cols = slice(k * EMB, (k + 1) * EMB)
        total = came[0, :, cols].astype(F32)
        for i in range(1, NX):
            total = total + came[i, :, cols].astype(F32)
        sums[:, k] = total
    for j in range(NJ):
        out[j] = sums[j].astype(BF)


def route_kernel(meta, came, cross, out, held):
    held[0] = jnp.zeros((8, EMB), F32)
    total = came[0].astype(F32)
    for k in range(1, NX * NY):
        total = total + came[k].astype(F32)
    held[1:] = total
    for j in range(NJ):
        slots = [held[meta[TABLE_AT + 2 * j + s]] for s in range(2)]
        out[j, :16] = jnp.concatenate(slots, axis=0).astype(BF)
        out[j, 16:] = cross[j]


def last_kernel(came, cross, table):
    blocks = cross.shape[1] // EMB
    scale = 1.0 / math.sqrt(EMB * 256)
    total = came[0, 16:].astype(F32)
    for j in range(1, NJ):
        total = total + came[j, 16:].astype(F32)
    for k in range(blocks):
        cross[:, k * EMB : (k + 1) * EMB] = total[k : k + 1] * scale
    for y in range(NY):
        rows = came[y * NZ, :16].astype(F32)
        for z in range(1, NZ):
            rows = rows + came[y * NZ + z, :16].astype(F32)
        for s in range(2):
            table[s, y * 8 : (y + 1) * 8] = rows[s * 8 : (s + 1) * 8]


def on_device(cross_input, upstream, v_weight, u_weight, bias, placement, owned_ids):
    samples, width = cross_input.shape
    swap = [(0, 1), (1, 0)]
    pids = lax.ppermute(owned_ids, "c", swap)
    px = lax.ppermute(cross_input, "c", swap)
    pup = lax.ppermute(upstream, "c", swap)

    same = placement[:, None] == placement[None, :]
    earlier = jnp.arange(TABLES)[None, :] < jnp.arange(TABLES)[:, None]
    slot = jnp.sum((same & earlier).astype(I32), axis=1)
    target = placement * 2 + slot
    table_at = jnp.sum(
        jnp.where(
            jnp.arange(2 * NJ, dtype=I32)[:, None] == target[None, :],
            jnp.arange(1, TABLES + 1, dtype=I32)[None, :],
            0,
        ),
        axis=1,
    )
    position = jnp.stack([lax.axis_index("c"), lax.axis_index(("y", "z"))]).astype(I32)
    meta = jnp.concatenate([position, placement, slot, table_at])

    bits = [4, 3, 2, 1, 0]
    pieces = [((NJ, 16, EMB), I16), ((NJ // 2, 16, EMB), I16)]

    def swap_bit(sent, bit):
        return lax.ppermute(sent, ("y", "z"), [(j, j ^ 1 << bit) for j in range(NJ)])

    def start(*refs):
        ids_start(*refs, bit=bits[0])

    state, sent = call(start, "ids_start", pieces, meta, owned_ids, pids, size=400000)
    came = swap_bit(sent, bits[0])
    px, came = lax.optimization_barrier((px, came))
    for last, bit in zip(bits[:-1], bits[1:]):

        def step(*refs, last=last, bit=bit):
            ids_step(*refs, last=last, bit=bit)

        state, sent = call(
            step, f"ids_bit{bit}", pieces, state, came, specs=[VMEM] * 2, size=400000
        )
        came = swap_bit(sent, bit)

    hid2, hgr2, cross = call(
        dense_kernel,
        "dense",
        [((RANK, 2 * samples), BF)] * 2 + [((NX, NJ, 2 * width), BF)],
        meta,
        cross_input,
        px,
        upstream,
        pup,
        v_weight,
        u_weight,
        specs=[SMEM] + [HBM] * 6,
        out_specs=[HBM] * 3,
        scratch=[pltpu.VMEM((256, width), BF)] * 5
        + [pltpu.VMEM((RANK, 2 * samples), BF)] * 2
        + [
            pltpu.VMEM((NX, NJ, 2 * width), BF),
            pltpu.SemaphoreType.DMA((6,)),
            pltpu.SemaphoreType.DMA((8,)),
        ],
        vmem=56 << 20,
        flops=6 * 256 * 256 * width,
        size=6 << 20,
    )
    cross = lax.all_to_all(cross, "x", 0, 0, tiled=True)

    def tables_of(*refs):
        table_kernel(*refs, last=bits[-1])

    (tables,) = call(
        tables_of,
        "tables",
        [((NX * NY, TABLES, 8, EMB), BF)],
        meta,
        hid2,
        hgr2,
        upstream,
        pup,
        u_weight,
        v_weight,
        bias[None],
        state,
        came,
        specs=[SMEM] + [HBM] * 6 + [VMEM] * 3,
        out_specs=[HBM],
        scratch=[
            pltpu.VMEM((NJ, 16, EMB), I32),
            pltpu.VMEM((TABLES, RANK // 2, 2 * samples), BF),
        ]
        + [pltpu.VMEM((RANK, 2 * samples), BF)] * 2
        + [pltpu.VMEM((256, width), BF)] * 3
        + [
            pltpu.VMEM((NX * NY, TABLES, 8, EMB), BF),
            pltpu.SemaphoreType.DMA((6,)),
            pltpu.SemaphoreType.DMA((1,)),
        ],
        vmem=56 << 20,
        flops=6 * 256 * 256 * width,
        size=9 << 20,
    )
    tables = lax.all_to_all(tables, ("x", "y"), 0, 0, tiled=True)

    blocks = 2 * width // EMB
    (cross,) = call(
        cross_kernel,
        "cross_sum",
        [((NJ, blocks, EMB), BF)],
        cross,
        specs=[VMEM],
        scratch=[pltpu.VMEM((NJ, blocks, EMB), F32)],
        size=3 << 20,
    )
    (routed,) = call(
        route_kernel,
        "route",
        [((NJ, 16 + blocks, EMB), BF)],
        meta,
        tables,
        cross,
        scratch=[pltpu.VMEM((TABLES + 1, 8, EMB), F32)],
        size=3 << 20,
    )
    routed = lax.all_to_all(routed, ("y", "z"), 0, 0, tiled=True)
    return call(
        last_kernel,
        "last",
        [((1, 2 * width), F32), ((2, NJ, EMB), F32)],
        routed,
        specs=[VMEM],
        size=1 << 20,
    )


def solution(mesh):
    fine = Mesh(mesh.devices.reshape(NX, 2, NY, NZ), ("x", "c", "y", "z"))
    grp, tbl = ("x", "c"), ("y", "z")
    in_specs = (
        P(grp + tbl, None),
        P(grp + tbl, None),
        P(),
        P(),
        P(),
        P(),
        P(tbl, None, grp),
    )
    out_specs = (P(grp + tbl, None), P(tbl, grp, None))
    return jax.shard_map(
        on_device, mesh=fine, in_specs=in_specs, out_specs=out_specs, check_vma=False
    )
```

time: 144 us -> 103 us (0.72)
  waiting for transfers between devices: 70.2 us -> 24.1 us
  blocking collectives: 0 us -> 24.4 us
  Pallas kernels: 0 us -> 17.4 us
  between operations: 14.3 us -> 0.74 us
  other arithmetic: 12.7 us -> 1.67 us
  local copies, waits for them, and re-layouts: 15.7 us -> 5.34 us
  matrix products: 7.52 us -> 0 us
  starting transfers between devices: 23 us -> 28.6 us
    all_to_all x3 -> x2, waiting for transfers between devices: 70.2 us -> 11.2 us  [the longest x1 11.2 us: on_device(): tables = lax.all_to_all(tables, ('x', 'y'), 0, 0, tiled=True)]
    all_to_all x0 -> x1, blocking collectives: none -> 24.4 us  [on_device(): routed = lax.all_to_all(routed, ('y', 'z'), 0, 0, tiled=True)]
    pallas_call x0 -> x10, Pallas kernels: none -> 17.4 us  [call(): pl.pallas_call(kernel, out_shape=tuple((jax.ShapeDtypeStruct(shape, dtype...]
    ppermute x0 -> x8, starting transfers between devices: none -> 17 us  [the longest x5 16.3 us: swap_bit(): lax.ppermute(sent, ('y', 'z'), [(j, j ^ 1 << bit) for j in range(NJ)])]
    ppermute x0 -> x8, waiting for transfers between devices: none -> 12.9 us  [the longest x5 11.8 us: swap_bit(): lax.ppermute(sent, ('y', 'z'), [(j, j ^ 1 << bit) for j in range(NJ)])]
    all_to_all x3 -> x2, starting transfers between devices: 23 us -> 11.6 us  [the longest x1 7.3 us: on_device(): tables = lax.all_to_all(tables, ('x', 'y'), 0, 0, tiled=True)]
    reshape x4 -> x0, local copies, waits for them, and re-layouts: 9.13 us -> none  [the longest x2 3.73 us: in_blocks(): shard.reshape(*shape[:dim], length, shape[dim] // length, *shape[dim + 1:])]
    reduce_sum x4 -> x2, other arithmetic: 8.9 us -> 1 us  [the longest x1 0.91 us: on_device(): slot = jnp.sum((same & earlier).astype(I32), axis=1)]
  transfers between devices with their start and end apart: 4 -> 10, of which waited for: 3 -> 7; matrix products, arithmetic and copies ran while one was open for 17% -> 3% of each run, Pallas kernels for 0% -> 9%
where the time goes in v2:
time: 103 us; the launch traced here: 102 us
  starting transfers between devices  28.6 us (28%)
  blocking collectives  24.4 us (24%)
  waiting for transfers between devices  24.1 us (23%)
  Pallas kernels  17.4 us (17%)
  local copies, waits for them, and re-layouts  5.34 us (5%)
  other arithmetic  1.67 us (2%)
    all_to_all x1, blocking collectives, on_device(): routed = lax.all_to_all(routed, ('y', 'z'), 0, 0, tiled=True)  24.4 us
    pallas_call x10, Pallas kernels, call(): pl.pallas_call(kernel, out_shape=tuple((jax.ShapeDtypeStruct(shape, dtype...  17.4 us
    ppermute x5, starting transfers between devices, swap_bit(): lax.ppermute(sent, ('y', 'z'), [(j, j ^ 1 << bit) for j in range(NJ)])  16.3 us
    ppermute x5, waiting for transfers between devices, swap_bit(): lax.ppermute(sent, ('y', 'z'), [(j, j ^ 1 << bit) for j in range(NJ)])  11.8 us
    all_to_all x1, waiting for transfers between devices, on_device(): tables = lax.all_to_all(tables, ('x', 'y'), 0, 0, tiled=True)  11.2 us
    all_to_all x1, starting transfers between devices, on_device(): tables = lax.all_to_all(tables, ('x', 'y'), 0, 0, tiled=True)  7.3 us
    all_to_all x1, starting transfers between devices, on_device(): cross = lax.all_to_all(cross, 'x', 0, 0, tiled=True)  4.3 us
    unnamed x16, local copies, waits for them, and re-layouts  4 us
  transfers between devices with their start and end apart: 10, of which 7 were waited for; matrix products, arithmetic and copies ran while one was open for 3% of the time, Pallas kernels for 9%

profile of v2, /device:TPU:32, one launch (start us, length us, event | category | flops | bytes accessed | tf_op | source)
XLA Modules:
  0.0 102.3 jit_solution(1301551478401133891)
XLA Ops:
  0.6 0.1 collective-permute-start
  0.7 0.5 collective-permute-start.3
  1.2 0.1 collective-permute-start.1
  1.3 0.9 convert_reduce_fusion
  2.2 0.7 iota_add_fusion
  2.9 0.1 select_reduce_fusion
  3.0 0.7 concatenate.3.refs_0_.meta
  3.7 0.0 copy-start.2
  3.7 1.1 %collective-permute-done.1.refs_2_ = s32[2,4,4096]{2,1,0:T(4,128)S(1)} collective-permute-done((s32[2,4,4096]{2,1,0:T(4,128)}, s32[2,4,4096]{2,1,0:T(4,128)S(1)}, u32[]{:S(2)}, u32[]{:S(2)}) %collective-permute-start.1) | collective-permute-done | bytes 131104 | tf_op jit(solution)/shard_map/ppermute | solution.py:224
  4.8 0.0 copy-start.1
  4.8 0.9 copy-done.1
  5.7 0.6 ids_start.1
  6.3 3.3 %collective-permute-start.2 = (s16[16,16,128]{2,1,0:T(8,128)(2,1)S(1)}, s16[16,16,128]{2,1,0:T(8,128)(2,1)S(1)}, u32[]{:S(2)}, u32[]{:S(2)}) collective-permute-start(s16[16,16,128]{2,1,0:T(8,128)(2,1)S(1)} %get-tuple-element.17), channel_id=1, source_target_pairs={{0,16},{1,17},{2,18},{3,19},{4,20},{5,21},{6,22},{7,23},{8,24},{9,... | collective-permute-start | bytes 196616 | tf_op jit(solution)/shard_map/ppermute | solution.py:247
  9.6 2.6 %collective-permute-done.2.refs_1_ = s16[16,16,128]{2,1,0:T(8,128)(2,1)S(1)} collective-permute-done((s16[16,16,128]{2,1,0:T(8,128)(2,1)S(1)}, s16[16,16,128]{2,1,0:T(8,128)(2,1)S(1)}, u32[]{:S(2)}, u32[]{:S(2)}) %collective-permute-start.2) | collective-permute-done | bytes 65568 | tf_op jit(solution)/shard_map/ppermute | solution.py:247
  12.2 0.0 collective-permute-done.px
  12.2 0.0 copy-start.5
  12.2 0.0 collective-permute-done.3.pup.refs_4_
  12.2 0.0 copy-done.2
  12.2 0.9 copy-done.5
  13.1 0.0 copy-start.4
  13.1 0.9 copy-done.4
  14.0 6.8 %dense.1 = (bf16[256,256]{1,0:T(8,128)(2,1)}, bf16[256,256]{1,0:T(8,128)(2,1)}, bf16[4,32,6912]{2,1,0:T(8,128)(2,1)}) custom-call(s32[118]{0:T(128)} %copy-done.2, bf16[128,3456]{1,0:T(8,128)(2,1)} %x.1, bf16[128,3456]{1,0:T(8,128)(2,1)} %copy-done.5, bf16[128,3456]{1,0:T(8,128)(2,1)} %refs_3_.1, bf16[128,3456]{1,0:T(8,128)(2,1)} %copy-done.4, ...), custom_call_target="tpu_custom_call" | custom-call | flops 1358954496 | bytes 6291456 | tf_op jit(solution)/shard_map/dense/pallas_call | solution.py:36
  20.8 0.0 copy-start.7
  20.8 4.3 %all-to-all-start.1 = ((bf16[4,32,6912]{2,1,0:T(8,128)(2,1)}), bf16[4,32,6912]{2,1,0:T(8,128)(2,1)S(1)}, u32[]{:S(2)}, u32[]{:S(2)}) async-start(bf16[4,32,6912]{2,1,0:T(8,128)(2,1)} %get-tuple-element.31), calls=%async_computation.1 | async-start | bytes 3538944 | tf_op jit(solution)/shard_map/all_to_all | solution.py:289
  25.2 1.7 %collective-permute-start.4 = (s16[16,16,128]{2,1,0:T(8,128)(2,1)S(1)}, s16[16,16,128]{2,1,0:T(8,128)(2,1)S(1)}, u32[]{:S(2)}, u32[]{:S(2)}) collective-permute-start(s16[16,16,128]{2,1,0:T(8,128)(2,1)S(1)} %get-tuple-element.24), channel_id=1, source_target_pairs={{0,8},{1,9},{2,10},{3,11},{4,12},{5,13},{6,14},{7,15},{8,0},{9,1},... | collective-permute-start | bytes 196616 | tf_op jit(solution)/shard_map/ppermute | solution.py:247
  26.8 2.7 %collective-permute-done.4.refs_1_ = s16[16,16,128]{2,1,0:T(8,128)(2,1)S(1)} collective-permute-done((s16[16,16,128]{2,1,0:T(8,128)(2,1)S(1)}, s16[16,16,128]{2,1,0:T(8,128)(2,1)S(1)}, u32[]{:S(2)}, u32[]{:S(2)}) %collective-permute-start.4) | collective-permute-done | bytes 65568 | tf_op jit(solution)/shard_map/ppermute | solution.py:247
  29.5 6.4 %collective-permute-start.5 = (s16[16,16,128]{2,1,0:T(8,128)(2,1)S(1)}, s16[16,16,128]{2,1,0:T(8,128)(2,1)S(1)}, u32[]{:S(2)}, u32[]{:S(2)}) collective-permute-start(s16[16,16,128]{2,1,0:T(8,128)(2,1)S(1)} %get-tuple-element.26), channel_id=1, source_target_pairs={{0,4},{1,5},{2,6},{3,7},{4,0},{5,1},{6,2},{7,3},{8,12},{9,13},{10,... | collective-permute-start | bytes 196616 | tf_op jit(solution)/shard_map/ppermute | solution.py:247
  35.9 2.3 %collective-permute-done.5.refs_1_ = s16[16,16,128]{2,1,0:T(8,128)(2,1)S(1)} collective-permute-done((s16[16,16,128]{2,1,0:T(8,128)(2,1)S(1)}, s16[16,16,128]{2,1,0:T(8,128)(2,1)S(1)}, u32[]{:S(2)}, u32[]{:S(2)}) %collective-permute-start.5) | collective-permute-done | bytes 65568 | tf_op jit(solution)/shard_map/ppermute | solution.py:247
  38.2 3.3 %collective-permute-start.6 = (s16[16,16,128]{2,1,0:T(8,128)(2,1)S(1)}, s16[16,16,128]{2,1,0:T(8,128)(2,1)S(1)}, u32[]{:S(2)}, u32[]{:S(2)}) collective-permute-start(s16[16,16,128]{2,1,0:T(8,128)(2,1)S(1)} %get-tuple-element.28), channel_id=1, source_target_pairs={{0,2},{1,3},{2,0},{3,1},{4,6},{5,7},{6,4},{7,5},{8,10},{9,11},{10,... | collective-permute-start | bytes 196616 | tf_op jit(solution)/shard_map/ppermute | solution.py:247
  41.5 2.3 %collective-permute-done.6.refs_1_ = s16[16,16,128]{2,1,0:T(8,128)(2,1)S(1)} collective-permute-done((s16[16,16,128]{2,1,0:T(8,128)(2,1)S(1)}, s16[16,16,128]{2,1,0:T(8,128)(2,1)S(1)}, u32[]{:S(2)}, u32[]{:S(2)}) %collective-permute-start.6) | collective-permute-done | bytes 65568 | tf_op jit(solution)/shard_map/ppermute | solution.py:247
  43.8 0.0 copy-start
  43.8 0.6 copy-done
  44.5 1.7 %collective-permute-start.7 = (s16[16,16,128]{2,1,0:T(8,128)(2,1)S(1)}, s16[16,16,128]{2,1,0:T(8,128)(2,1)S(1)}, u32[]{:S(2)}, u32[]{:S(2)}) collective-permute-start(s16[16,16,128]{2,1,0:T(8,128)(2,1)S(1)} %get-tuple-element.30), channel_id=1, source_target_pairs={{0,1},{1,0},{2,3},{3,2},{4,5},{5,4},{6,7},{7,6},{8,9},{9,8},{10,11... | collective-permute-start | bytes 196616 | tf_op jit(solution)/shard_map/ppermute | solution.py:247
  46.2 0.0 copy-done.7
  46.2 0.6 broadcast_in_dim.24.refs_7_
  46.8 1.9 %collective-permute-done.7.refs_9_ = s16[16,16,128]{2,1,0:T(8,128)(2,1)S(1)} collective-permute-done((s16[16,16,128]{2,1,0:T(8,128)(2,1)S(1)}, s16[16,16,128]{2,1,0:T(8,128)(2,1)S(1)}, u32[]{:S(2)}, u32[]{:S(2)}) %collective-permute-start.7) | collective-permute-done | bytes 65568 | tf_op jit(solution)/shard_map/ppermute | solution.py:247
  48.8 0.0 copy-start.6
  48.8 0.6 copy-done.6
  49.4 7.9 %tables.1 = bf16[16,26,8,128]{3,2,1,0:T(8,128)(2,1)} custom-call(s32[118]{0:T(128)} %copy-done.2, bf16[256,256]{1,0:T(8,128)(2,1)} %get-tuple-element.19.refs_1_, bf16[256,256]{1,0:T(8,128)(2,1)} %get-tuple-element.20.refs_2_, bf16[128,3456]{1,0:T(8,128)(2,1)} %refs_3_.1, bf16[128,3456]{1,0:T(8,128)(2,1)} %copy-done.4, bf16[256,3456]{1,0:T(8,128)(2,1)} %refs_5_.1, ...), custom_call_target="tpu_custom_call" | custom-call | flops 1358954496 | bytes 9437184 | tf_op jit(solution)/shard_map/tables/pallas_call | solution.py:36
  57.2 0.0 copy-start.3
  57.3 0.0 all-to-all-done.1.came
  57.3 7.3 %all-to-all-start = ((bf16[16,26,8,128]{3,2,1,0:T(8,128)(2,1)}), bf16[16,26,8,128]{3,2,1,0:T(8,128)(2,1)S(1)}, u32[]{:S(2)}, u32[]{:S(2)}) async-start(bf16[16,26,8,128]{3,2,1,0:T(8,128)(2,1)} %tables.1), calls=%async_computation | async-start | bytes 1703936 | tf_op jit(solution)/shard_map/all_to_all | solution.py:325
  64.6 0.7 cross_sum.1.cross
  65.2 11.2 %all-to-all-done.came = bf16[16,26,8,128]{3,2,1,0:T(8,128)(2,1)S(1)} async-done(((bf16[16,26,8,128]{3,2,1,0:T(8,128)(2,1)}), bf16[16,26,8,128]{3,2,1,0:T(8,128)(2,1)S(1)}, u32[]{:S(2)}, u32[]{:S(2)}) %all-to-all-start) | async-done | bytes 852000 | tf_op jit(solution)/shard_map/all_to_all | solution.py:325
  76.4 0.0 copy-done.3
  76.4 0.7 route.1
  77.1 24.4 %all_to_all.15.came = bf16[32,70,128]{2,1,0:T(8,128)(2,1)S(1)} all-to-all(bf16[32,70,128]{2,1,0:T(8,128)(2,1)S(1)} %route.1), channel_id=1, replica_groups=mesh['x'=4,'c'=2,'y'=4,'z'=8] {'y','z'}, dimensions={0} | all-to-all | bytes 1146880 | tf_op jit(solution)/shard_map/all_to_all | solution.py:347
  101.6 0.7 last.1
  (4 shorter events, 0.1 us)
Async XLA Ops:
  0.6 11.6 %collective-permute-start = (bf16[128,3456]{1,0:T(8,128)(2,1)}, bf16[128,3456]{1,0:T(8,128)(2,1)S(1)}, u32[]{:S(2)}, u32[]{:S(2)}) collective-permute-start(bf16[128,3456]{1,0:T(8,128)(2,1)} %x.1), channel_id=1, source_target_pairs={{0,32},{32,0},{1,33},{33,1},{2,34},{34,2},{3,35},{35,3},{4,36},{36... | collective-permute-start | bytes 2654216 | tf_op jit(solution)/shard_map/ppermute | solution.py:225
  0.7 11.5 %collective-permute-start.3 = (bf16[128,3456]{1,0:T(8,128)(2,1)}, bf16[128,3456]{1,0:T(8,128)(2,1)S(1)}, u32[]{:S(2)}, u32[]{:S(2)}) collective-permute-start(bf16[128,3456]{1,0:T(8,128)(2,1)} %refs_3_.1), channel_id=1, source_target_pairs={{0,32},{32,0},{1,33},{33,1},{2,34},{34,2},{3,35},{35,3},{4,36},{36... | collective-permute-start | bytes 2654216 | tf_op jit(solution)/shard_map/ppermute | solution.py:226
  1.2 3.6 %collective-permute-start.1 = (s32[2,4,4096]{2,1,0:T(4,128)}, s32[2,4,4096]{2,1,0:T(4,128)S(1)}, u32[]{:S(2)}, u32[]{:S(2)}) collective-permute-start(s32[2,4,4096]{2,1,0:T(4,128)} %refs_1_.1), channel_id=1, source_target_pairs={{0,32},{32,0},{1,33},{33,1},{2,34},{34,2},{3,35},{35,3},{4,36},{36... | collective-permute-start | bytes 393224 | tf_op jit(solution)/shard_map/ppermute | solution.py:224
  3.7 8.5 %copy-start.2 = (s32[118]{0:T(128)}, s32[118]{0:T(128)S(1)}, u32[]{:S(2)}) copy-start(s32[118]{0:T(128)S(1)} %concatenate.3.refs_0_.meta) | copy-start | bytes 1420
  4.8 0.9 copy-start.1
  6.3 5.9 %collective-permute-start.2 = (s16[16,16,128]{2,1,0:T(8,128)(2,1)S(1)}, s16[16,16,128]{2,1,0:T(8,128)(2,1)S(1)}, u32[]{:S(2)}, u32[]{:S(2)}) collective-permute-start(s16[16,16,128]{2,1,0:T(8,128)(2,1)S(1)} %get-tuple-element.17), channel_id=1, source_target_pairs={{0,16},{1,17},{2,18},{3,19},{4,20},{5,21},{6,22},{7,23},{8,24},{9,... | collective-permute-start | bytes 196616 | tf_op jit(solution)/shard_map/ppermute | solution.py:247
  12.2 0.9 copy-start.5
  13.1 0.9 copy-start.4
  20.8 25.4 %copy-start.7 = (f32[3456]{0:T(1024)S(1)}, f32[3456]{0:T(1024)}, u32[]{:S(2)}) copy-start(f32[3456]{0:T(1024)} %param.11) | copy-start | bytes 41476
  20.8 36.4 %all-to-all-start.1 = ((bf16[4,32,6912]{2,1,0:T(8,128)(2,1)}), bf16[4,32,6912]{2,1,0:T(8,128)(2,1)S(1)}, u32[]{:S(2)}, u32[]{:S(2)}) async-start(bf16[4,32,6912]{2,1,0:T(8,128)(2,1)} %get-tuple-element.31), calls=%async_computation.1 | async-start | bytes 3538944 | tf_op jit(solution)/shard_map/all_to_all | solution.py:289
  25.2 4.4 %collective-permute-start.4 = (s16[16,16,128]{2,1,0:T(8,128)(2,1)S(1)}, s16[16,16,128]{2,1,0:T(8,128)(2,1)S(1)}, u32[]{:S(2)}, u32[]{:S(2)}) collective-permute-start(s16[16,16,128]{2,1,0:T(8,128)(2,1)S(1)} %get-tuple-element.24), channel_id=1, source_target_pairs={{0,8},{1,9},{2,10},{3,11},{4,12},{5,13},{6,14},{7,15},{8,0},{9,1},... | collective-permute-start | bytes 196616 | tf_op jit(solution)/shard_map/ppermute | solution.py:247
  29.5 8.6 %collective-permute-start.5 = (s16[16,16,128]{2,1,0:T(8,128)(2,1)S(1)}, s16[16,16,128]{2,1,0:T(8,128)(2,1)S(1)}, u32[]{:S(2)}, u32[]{:S(2)}) collective-permute-start(s16[16,16,128]{2,1,0:T(8,128)(2,1)S(1)} %get-tuple-element.26), channel_id=1, source_target_pairs={{0,4},{1,5},{2,6},{3,7},{4,0},{5,1},{6,2},{7,3},{8,12},{9,13},{10,... | collective-permute-start | bytes 196616 | tf_op jit(solution)/shard_map/ppermute | solution.py:247
  38.2 5.6 %collective-permute-start.6 = (s16[16,16,128]{2,1,0:T(8,128)(2,1)S(1)}, s16[16,16,128]{2,1,0:T(8,128)(2,1)S(1)}, u32[]{:S(2)}, u32[]{:S(2)}) collective-permute-start(s16[16,16,128]{2,1,0:T(8,128)(2,1)S(1)} %get-tuple-element.28), channel_id=1, source_target_pairs={{0,2},{1,3},{2,0},{3,1},{4,6},{5,7},{6,4},{7,5},{8,10},{9,11},{10,... | collective-permute-start | bytes 196616 | tf_op jit(solution)/shard_map/ppermute | solution.py:247
  43.8 0.7 copy-start
  44.5 4.3 %collective-permute-start.7 = (s16[16,16,128]{2,1,0:T(8,128)(2,1)S(1)}, s16[16,16,128]{2,1,0:T(8,128)(2,1)S(1)}, u32[]{:S(2)}, u32[]{:S(2)}) collective-permute-start(s16[16,16,128]{2,1,0:T(8,128)(2,1)S(1)} %get-tuple-element.30), channel_id=1, source_target_pairs={{0,1},{1,0},{2,3},{3,2},{4,5},{5,4},{6,7},{7,6},{8,9},{9,8},{10,11... | collective-permute-start | bytes 196616 | tf_op jit(solution)/shard_map/ppermute | solution.py:247
  48.8 0.6 copy-start.6
  57.2 19.2 %copy-start.3 = (s32[118]{0:T(128)S(1)}, s32[118]{0:T(128)}, u32[]{:S(2)}) copy-start(s32[118]{0:T(128)} %copy-done.2) | copy-start | bytes 1420
  57.3 19.2 %all-to-all-start = ((bf16[16,26,8,128]{3,2,1,0:T(8,128)(2,1)}), bf16[16,26,8,128]{3,2,1,0:T(8,128)(2,1)S(1)}, u32[]{:S(2)}, u32[]{:S(2)}) async-start(bf16[16,26,8,128]{3,2,1,0:T(8,128)(2,1)} %tables.1), calls=%async_computation | async-start | bytes 1703936 | tf_op jit(solution)/shard_map/all_to_all | solution.py:325

commit v3 on v2

v3 whole, which is shorter than its diff:
```python
import math

import jax
import jax.numpy as jnp
from jax import lax
from jax.experimental import pallas as pl
from jax.experimental.pallas import tpu as pltpu
from jax.sharding import Mesh
from jax.sharding import PartitionSpec as P

EMB = 128
TABLES = 26
RANK = 256
NX, NY, NZ = 4, 4, 8
NJ = NY * NZ
BF = jnp.bfloat16
F32 = jnp.float32
I32 = jnp.int32
I16 = jnp.int16

CORE, XX, YY, OWNER, SLOT, TABLE_AT = 0, 1, 2, 3, 3 + TABLES, 3 + 2 * TABLES
VMEM = pl.BlockSpec(memory_space=pltpu.VMEM)
SMEM = pl.BlockSpec(memory_space=pltpu.SMEM)
HBM = pl.BlockSpec(memory_space=pltpu.HBM)


def nt(left, right):
    return lax.dot_general(left, right, (((1,), (1,)), ((), ())), preferred_element_type=F32)


def mm(left, right):
    return jnp.dot(left, right, preferred_element_type=F32)


def call(kernel, name, outs, *args, specs=None, out_specs=None, scratch=(), flops=0, size=0, vmem=24 << 20):
    return pl.pallas_call(
        kernel,
        out_shape=tuple(jax.ShapeDtypeStruct(shape, dtype) for shape, dtype in outs),
        in_specs=specs or [SMEM] + [VMEM] * (len(args) - 1),
        out_specs=tuple(out_specs or [VMEM] * len(outs)),
        scratch_shapes=list(scratch),
        compiler_params=pltpu.CompilerParams(vmem_limit_bytes=vmem),
        cost_estimate=pl.CostEstimate(flops=flops, bytes_accessed=size, transcendentals=0),
        name=name,
    )(*args)


def ids_kernel(ids, out):
    for j in range(NJ):
        parts = [ids[s, :, j * EMB : (j + 1) * EMB] for s in range(2)]
        out[j] = jnp.concatenate(parts, axis=0).astype(I16)


def own_rows(full, core):
    picks = [
        jnp.where(core == 0, full[i * 64 : i * 64 + 32], full[i * 64 + 32 : i * 64 + 64])
        for i in range(NX)
    ]
    return jnp.concatenate(picks, axis=0)


def loads_of(pairs, sems):
    loads = [
        pltpu.make_async_copy(source, target, sems.at[k])
        for k, (source, target) in enumerate(pairs)
    ]
    for load in loads:
        load.start()
    return loads


def dense_kernel(meta, x, px, up, pup, v, u, hid_out, hgr_out, out, *scratch):
    both, ups, vv, uu, prod, hid, hgr, held, in_sems, out_sems = scratch
    n, width = x.shape
    loads = loads_of(((x, both.at[:n]), (v, vv), (up, ups), (u, uu)), in_sems)
    both[n:] = px[...]
    prod[n:] = (px[...].astype(F32) * pup[...].astype(F32)).astype(BF)
    loads[0].wait()
    loads[1].wait()
    hid[...] = nt(vv[...], both[...]).astype(BF)
    loads[2].wait()
    prod[:n] = (both[:n].astype(F32) * ups[...].astype(F32)).astype(BF)
    loads[3].wait()
    hgr[...] = nt(uu[...], prod[...]).astype(BF)
    copies = loads_of(((hid, hid_out), (hgr, hgr_out)), out_sems)
    hid_own = own_rows(hid[...].astype(F32), meta[CORE]).astype(BF)
    hgr_own = own_rows(hgr[...].astype(F32), meta[CORE]).astype(BF)
    step = 1152
    for side, (left, right) in enumerate(((hid_own, prod), (hgr_own, both))):
        for k in range(width // step):
            total = mm(left, right[:, k * step : (k + 1) * step])
            cols = slice(side * width + k * step, side * width + (k + 1) * step)
            for i in range(NX * NY):
                held[i, :, cols] = total[i * 8 : (i + 1) * 8].astype(BF)
            copies.append(
                pltpu.make_async_copy(
                    held.at[:, :, cols], out.at[:, :, cols], out_sems.at[len(copies)]
                )
            )
            copies[-1].start()
    for copy in copies:
        copy.wait()


def table_kernel(meta, hid_in, hgr_in, up_in, u_in, v_in, pup, bias, ids, pids, *refs):
    outs, (state, counts, hid, hgr, up, u, v) = refs[:4], refs[4:11]
    held, in_sems, out_sems = refs[11:15], refs[15], refs[16]
    n = up_in.shape[0]
    loads = loads_of(((hid_in, hid), (hgr_in, hgr), (u_in, u), (v_in, v), (up_in, up)), in_sems)
    for p in range(NJ):
        state[p, :8] = ids[p].astype(I32)
        state[p, 8:] = pids[p].astype(I32)
    at = lax.broadcasted_iota(I32, (RANK // 2, n), 0)
    row = lax.rem(meta[XX] + (at // 8) % 4, NX) * 64 + lax.rem(meta[YY] + at // 32, NY) * 8
    row = row + meta[CORE] * 32 + at % 8
    for table in range(TABLES):
        slot = meta[SLOT + table]
        looked = state[meta[OWNER + table]]
        for half in range(2):
            eight = looked[half * 8 : half * 8 + 8]
            four = jnp.where(slot == 0, eight[:4], eight[4:])
            count = jnp.where(four[0:1] == row, 1.0, 0.0)
            for k in range(1, 4):
                count = count + jnp.where(four[k : k + 1] == row, 1.0, 0.0)
            counts[table, :, half * n : (half + 1) * n] = count.astype(BF)
    for load in loads:
        load.wait()
    hid_s = hid[...].astype(F32).T.astype(BF)
    hgr_s = hgr[...].astype(F32).T.astype(BF)
    for pair in range(TABLES // 2):
        cols = slice(EMB + pair * 256, EMB + pair * 256 + 256)
        mixed = mm(hid_s, u[:, cols]) + bias[:, cols]
        back = mm(hgr_s, v[:, cols])
        up_float = jnp.concatenate([up[:, cols], pup[:, cols]], axis=0).astype(F32)
        pooled = (up_float * (1.0 + mixed) + back).astype(BF)
        for which in range(2):
            table = 2 * pair + which
            total = mm(counts[table], pooled[:, which * EMB : (which + 1) * EMB])
            for d in range(NY):
                held[d][table] = total[d * 32 : (d + 1) * 32].astype(held[d].dtype)
    for copy in loads_of(tuple(zip(held, outs)), out_sems):
        copy.wait()


def total_of(refs):
    total = refs[0][...].astype(F32)
    for ref in refs[1:]:
        total = total + ref[...].astype(F32)
    return total


def table_second(*refs):
    total = total_of(refs[:NY])
    for d in range(NX):
        refs[NY + d][...] = total[:, d * 8 : (d + 1) * 8].astype(refs[NY + d].dtype)


def cross_kernel(came, out, sums):
    for k in range(came.shape[2] // EMB):
        cols = slice(k * EMB, (k + 1) * EMB)
        total = came[0, :, cols].astype(F32)
        for i in range(1, NX * NY):
            total = total + came[i, :, cols].astype(F32)
        sums[:, k] = total
    out[...] = sums[...].astype(BF)


def cross_last(came, out):
    scale = 1.0 / math.sqrt(EMB * 256)
    total = came[0].astype(F32)
    for z in range(1, NZ):
        total = total + came[z].astype(F32)
    for k in range(total.shape[0]):
        out[:, k * EMB : (k + 1) * EMB] = total[k : k + 1] * scale


def route_kernel(meta, *refs):
    came, out, held = refs[:NX], refs[NX], refs[NX + 1]
    held[0] = jnp.zeros((8, EMB), F32)
    held[1:] = total_of(came)
    for j in range(NJ):
        slots = [held[meta[TABLE_AT + 2 * j + s]] for s in range(2)]
        out[j] = jnp.concatenate(slots, axis=0).astype(BF)


def table_last(came, table):
    for y in range(NY):
        rows = came[y * NZ].astype(F32)
        for z in range(1, NZ):
            rows = rows + came[y * NZ + z].astype(F32)
        for s in range(2):
            table[s, y * 8 : (y + 1) * 8] = rows[s * 8 : (s + 1) * 8]


def shift(chunks, axis):
    n = len(chunks)
    return [chunks[0]] + [
        lax.ppermute(chunks[d], axis, [(i, (i + d) % n) for i in range(n)]) for d in range(1, n)
    ]


def on_device(cross_input, upstream, v_weight, u_weight, bias, placement, owned_ids):
    samples, width = cross_input.shape
    blocks = 2 * width // EMB
    swap = [(0, 1), (1, 0)]
    px = lax.ppermute(cross_input, "c", swap)
    pup = lax.ppermute(upstream, "c", swap)

    (ids,) = call(ids_kernel, "ids", [((NJ, 8, EMB), I16)], owned_ids, specs=[VMEM], size=200000)
    ids = lax.all_to_all(ids, ("y", "z"), 0, 0, tiled=True)

    same = placement[:, None] == placement[None, :]
    earlier = jnp.arange(TABLES)[None, :] < jnp.arange(TABLES)[:, None]
    slot = jnp.sum((same & earlier).astype(I32), axis=1)
    target = placement * 2 + slot
    table_at = jnp.sum(
        jnp.where(
            jnp.arange(2 * NJ, dtype=I32)[:, None] == target[None, :],
            jnp.arange(1, TABLES + 1, dtype=I32)[None, :],
            0,
        ),
        axis=1,
    )
    position = jnp.stack([lax.axis_index(axis) for axis in ("c", "x", "y")]).astype(I32)
    meta = jnp.concatenate([position, placement, slot, table_at])

    wide = pltpu.VMEM((256, width), BF)
    half = pltpu.VMEM((samples, width), BF)
    square = pltpu.VMEM((RANK, 2 * samples), BF)
    hid, hgr, cross = call(
        dense_kernel,
        "dense",
        [((RANK, 2 * samples), BF)] * 2 + [((NX * NY, NZ, 2 * width), BF)],
        meta,
        cross_input,
        px,
        upstream,
        pup,
        v_weight,
        u_weight,
        specs=[SMEM, HBM, VMEM, HBM, VMEM, HBM, HBM],
        out_specs=[HBM] * 3,
        scratch=[wide, half, wide, wide, wide, square, square]
        + [
            pltpu.VMEM((NX * NY, NZ, 2 * width), BF),
            pltpu.SemaphoreType.DMA((4,)),
            pltpu.SemaphoreType.DMA((8,)),
        ],
        vmem=56 << 20,
        flops=6 * 256 * 256 * width,
        size=6 << 20,
    )
    ids, cross = lax.optimization_barrier((ids, cross))
    cross = lax.all_to_all(cross, ("x", "y"), 0, 0, tiled=True)
    pids = lax.ppermute(ids, "c", swap)

    sent = [((TABLES, 32, EMB), F32)] + [((TABLES, 32, EMB), BF)] * 3
    tables = call(
        table_kernel,
        "tables",
        sent,
        meta,
        hid,
        hgr,
        upstream,
        u_weight,
        v_weight,
        pup,
        bias[None],
        ids,
        pids,
        specs=[SMEM] + [HBM] * 5 + [VMEM] * 4,
        out_specs=[HBM] * 4,
        scratch=[
            pltpu.VMEM((NJ, 16, EMB), I32),
            pltpu.VMEM((TABLES, RANK // 2, 2 * samples), BF),
            square,
            square,
            half,
            wide,
            wide,
        ]
        + [pltpu.VMEM(shape, dtype) for shape, dtype in sent]
        + [pltpu.SemaphoreType.DMA((5,)), pltpu.SemaphoreType.DMA((4,))],
        vmem=56 << 20,
        flops=6 * 256 * 256 * width,
        size=9 << 20,
    )
    tables = shift(tables, "y")
    tables = call(
        table_second,
        "table_second",
        [((TABLES, 8, EMB), F32)] + [((TABLES, 8, EMB), BF)] * 3,
        *tables,
        specs=[VMEM] * 4,
        size=1 << 20,
    )
    (cross,) = call(
        cross_kernel,
        "cross_sum",
        [((NZ, blocks, EMB), BF)],
        cross,
        specs=[VMEM],
        scratch=[pltpu.VMEM((NZ, blocks, EMB), F32)],
        size=3 << 20,
    )
    cross = lax.all_to_all(cross, "z", 0, 0, tiled=True)
    tables = shift(tables, "x")
    (routed,) = call(
        route_kernel,
        "route",
        [((NJ, 16, EMB), BF)],
        meta,
        *tables,
        scratch=[pltpu.VMEM((TABLES + 1, 8, EMB), F32)],
        size=1 << 20,
    )
    cross, routed = lax.optimization_barrier((cross, routed))
    routed = lax.all_to_all(routed, ("y", "z"), 0, 0, tiled=True)
    (cross_grad,) = call(
        cross_last, "cross_last", [((1, 2 * width), F32)], cross, specs=[VMEM], size=200000
    )
    (table_grad,) = call(
        table_last, "table_last", [((2, 32, EMB), F32)], routed, specs=[VMEM], size=200000
    )
    return (cross_grad, table_grad)


def solution(mesh):
    fine = Mesh(mesh.devices.reshape(NX, 2, NY, NZ), ("x", "c", "y", "z"))
    grp, tbl = ("x", "c"), ("y", "z")
    in_specs = (
        P(grp + tbl, None),
        P(grp + tbl, None),
        P(),
        P(),
        P(),
        P(),
        P(tbl, None, grp),
    )
    out_specs = (P(grp + tbl, None), P(tbl, grp, None))
    return jax.shard_map(
        on_device, mesh=fine, in_specs=in_specs, out_specs=out_specs, check_vma=False
    )
```

time: 103 us -> 95.3 us (0.925)
  blocking collectives: 24.4 us -> 0 us
  starting transfers between devices: 28.6 us -> 44.9 us
  waiting for transfers between devices: 24.1 us -> 22 us
  Pallas kernels: 17.4 us -> 19.3 us
    all_to_all x1 -> x0, blocking collectives: 24.4 us -> none  [on_device(): routed = lax.all_to_all(routed, ('y', 'z'), 0, 0, tiled=True)]
    all_to_all x2 -> x4, starting transfers between devices: 11.6 us -> 33.9 us  [the longest x1 11.4 us: on_device(): ids = lax.all_to_all(ids, ('y', 'z'), 0, 0, tiled=True)]
    ppermute x6 -> x7, waiting for transfers between devices: 12.9 us -> 3.23 us  [the longest x6 2.61 us: shift(): lax.ppermute(chunks[d], axis, [(i, (i + d) % n) for i in range(n)])]
    all_to_all x2 -> x4, waiting for transfers between devices: 11.2 us -> 18.8 us  [the longest x1 9.77 us: on_device(): cross = lax.all_to_all(cross, ('x', 'y'), 0, 0, tiled=True)]
    ppermute x6 -> x7, starting transfers between devices: 16.4 us -> 10.5 us  [the longest x6 10.4 us: shift(): lax.ppermute(chunks[d], axis, [(i, (i + d) % n) for i in range(n)])]
    pallas_call x10 -> x8, Pallas kernels: 17.4 us -> 19.3 us  [call(): pl.pallas_call(kernel, out_shape=tuple((jax.ShapeDtypeStruct(shape, dtype...]
  transfers between devices with their start and end apart: 10 -> 13, of which waited for: 7 -> 5; matrix products, arithmetic and copies ran while one was open for 3% -> 4% of each run, Pallas kernels for 9% -> 20%
where the time goes in v3:
time: 95.3 us; the launch traced here: 94 us
  starting transfers between devices  44.9 us (47%)
  waiting for transfers between devices  22 us (23%)
  Pallas kernels  19.3 us (20%)
  local copies, waits for them, and re-layouts  5.24 us (5%)
  other arithmetic  1.67 us (2%)
    pallas_call x8, Pallas kernels, call(): pl.pallas_call(kernel, out_shape=tuple((jax.ShapeDtypeStruct(shape, dtype...  19.3 us
    all_to_all x1, starting transfers between devices, on_device(): ids = lax.all_to_all(ids, ('y', 'z'), 0, 0, tiled=True)  11.4 us
    ppermute x6, starting transfers between devices, shift(): lax.ppermute(chunks[d], axis, [(i, (i + d) % n) for i in range(n)])  10.4 us
    all_to_all x1, waiting for transfers between devices, on_device(): cross = lax.all_to_all(cross, ('x', 'y'), 0, 0, tiled=True)  9.77 us
    all_to_all x1, waiting for transfers between devices, on_device(): routed = lax.all_to_all(routed, ('y', 'z'), 0, 0, tiled=True)  9.03 us
    all_to_all x1, starting transfers between devices, on_device(): routed = lax.all_to_all(routed, ('y', 'z'), 0, 0, tiled=True)  8.35 us
    all_to_all x1, starting transfers between devices, on_device(): cross = lax.all_to_all(cross, 'z', 0, 0, tiled=True)  7.22 us
    all_to_all x1, starting transfers between devices, on_device(): cross = lax.all_to_all(cross, ('x', 'y'), 0, 0, tiled=True)  6.96 us
  transfers between devices with their start and end apart: 13, of which 5 were waited for; matrix products, arithmetic and copies ran while one was open for 4% of the time, Pallas kernels for 20%

profile of v3, /device:TPU:32, one launch (start us, length us, event | category | flops | bytes accessed | tf_op | source)
XLA Modules:
  0.0 94.0 jit_solution(16285865495699128644)
XLA Ops:
  0.6 0.1 collective-permute-start.1
  0.7 0.5 collective-permute-start
  1.2 0.9 copy-done.1
  2.1 0.6 ids.2
  2.8 11.4 %all-to-all-start = ((s16[32,8,128]{2,1,0:T(8,128)(2,1)}), s16[32,8,128]{2,1,0:T(8,128)(2,1)S(1)}, u32[]{:S(2)}, u32[]{:S(2)}) async-start(s16[32,8,128]{2,1,0:T(8,128)(2,1)} %ids.2), calls=%async_computation | async-start | bytes 131072 | tf_op jit(solution)/shard_map/all_to_all | solution.py:210
  14.1 0.9 convert_reduce_fusion
  15.0 0.7 iota_add_fusion
  15.7 0.1 select_reduce_fusion
  15.8 1.3 %concatenate.3.meta = s32[119]{0:T(128)} concatenate(s32[1]{0:T(128)} %bitcast, s32[1]{0:T(128)} %bitcast.1, s32[1]{0:T(128)} %bitcast.2, s32[26]{0:T(128)} %param.12, s32[26]{0:T(128)S(1)} %convert_reduce_fusion, s32[64]{0:T(128)S(1)} %select_reduce_fusion), dimensions={0} | concatenate | bytes 952 | tf_op jit(solution)/shard_map/concatenate | solution.py:225
  17.1 0.0 collective-permute-done.1.pup
  17.1 0.0 collective-permute-done.px
  17.1 0.9 copy-done.3
  18.0 0.9 copy-done.4
  18.9 7.1 %dense.1 = (bf16[256,256]{1,0:T(8,128)(2,1)}, bf16[256,256]{1,0:T(8,128)(2,1)}, bf16[16,8,6912]{2,1,0:T(8,128)(2,1)}) custom-call(s32[119]{0:T(128)} %concatenate.3.meta, bf16[128,3456]{1,0:T(8,128)(2,1)} %x.1, bf16[128,3456]{1,0:T(8,128)(2,1)} %copy-done.4, bf16[128,3456]{1,0:T(8,128)(2,1)} %up_in.1, bf16[128,3456]{1,0:T(8,128)(2,1)} %copy-done.3, ...), custom_call_target="tpu_custom_call" | custom-call | flops 1358954496 | bytes 6291456 | tf_op jit(solution)/shard_map/dense/pallas_call | solution.py:36
  26.0 0.0 all-to-all-done.ids
  26.0 0.0 copy-start.5
  26.0 0.0 copy-start.7
  26.0 7.0 %all-to-all-start.1 = ((bf16[16,8,6912]{2,1,0:T(8,128)(2,1)}), bf16[16,8,6912]{2,1,0:T(8,128)(2,1)S(1)}, u32[]{:S(2)}, u32[]{:S(2)}) async-start(bf16[16,8,6912]{2,1,0:T(8,128)(2,1)} %get-tuple-element.18), calls=%async_computation.1 | async-start | bytes 3538944 | tf_op jit(solution)/shard_map/all_to_all | solution.py:254
  33.0 0.0 copy-done.5
  33.0 0.1 collective-permute-start.2
  33.1 0.0 copy-done.7
  33.1 0.6 broadcast_in_dim.24.bias
  33.7 0.6 collective-permute-done.2.pids
  34.4 0.6 copy-done.6
  35.0 7.9 %tables.1 = (f32[26,32,128]{2,1,0:T(8,128)}, bf16[26,32,128]{2,1,0:T(8,128)(2,1)}, bf16[26,32,128]{2,1,0:T(8,128)(2,1)}, bf16[26,32,128]{2,1,0:T(8,128)(2,1)}) custom-call(s32[119]{0:T(128)} %concatenate.3.meta, bf16[256,256]{1,0:T(8,128)(2,1)} %get-tuple-element.19.hid_in, bf16[256,256]{1,0:T(8,128)(2,1)} %get-tuple-element.20.hgr_in, ...), custom_call_target="tpu_custom_call" | custom-call | flops 1358954496 | bytes 9437184 | tf_op jit(solution)/shard_map/tables/pallas_call | solution.py:36
  42.9 2.0 %collective-permute-start.3 = (bf16[26,32,128]{2,1,0:T(8,128)(2,1)}, bf16[26,32,128]{2,1,0:T(8,128)(2,1)S(1)}, u32[]{:S(2)}, u32[]{:S(2)}) collective-permute-start(bf16[26,32,128]{2,1,0:T(8,128)(2,1)} %get-tuple-element.23), channel_id=1, source_target_pairs={{0,8},{8,16},{16,24},{24,0},{1,9},{9,17},{17,25},{25,1},{2,10},{10... | collective-permute-start | bytes 638984 | tf_op jit(solution)/shard_map/ppermute | solution.py:198
  44.9 2.7 %collective-permute-start.4 = (bf16[26,32,128]{2,1,0:T(8,128)(2,1)}, bf16[26,32,128]{2,1,0:T(8,128)(2,1)S(1)}, u32[]{:S(2)}, u32[]{:S(2)}) collective-permute-start(bf16[26,32,128]{2,1,0:T(8,128)(2,1)} %get-tuple-element.24), channel_id=1, source_target_pairs={{0,16},{8,24},{16,0},{24,8},{1,17},{9,25},{17,1},{25,9},{2,18},{10... | collective-permute-start | bytes 638984 | tf_op jit(solution)/shard_map/ppermute | solution.py:198
  47.6 1.5 %collective-permute-start.5 = (bf16[26,32,128]{2,1,0:T(8,128)(2,1)}, bf16[26,32,128]{2,1,0:T(8,128)(2,1)S(1)}, u32[]{:S(2)}, u32[]{:S(2)}) collective-permute-start(bf16[26,32,128]{2,1,0:T(8,128)(2,1)} %get-tuple-element.25), channel_id=1, source_target_pairs={{0,24},{8,0},{16,8},{24,16},{1,25},{9,1},{17,9},{25,17},{2,26},{10... | collective-permute-start | bytes 638984 | tf_op jit(solution)/shard_map/ppermute | solution.py:198
  49.1 9.8 %all-to-all-done.1.came = bf16[16,8,6912]{2,1,0:T(8,128)(2,1)S(1)} async-done(((bf16[16,8,6912]{2,1,0:T(8,128)(2,1)}), bf16[16,8,6912]{2,1,0:T(8,128)(2,1)S(1)}, u32[]{:S(2)}, u32[]{:S(2)}) %all-to-all-start.1) | async-done | bytes 1769504 | tf_op jit(solution)/shard_map/all_to_all | solution.py:254
  58.8 1.0 %cross_sum.1 = bf16[8,54,128]{2,1,0:T(8,128)(2,1)} custom-call(bf16[16,8,6912]{2,1,0:T(8,128)(2,1)S(1)} %all-to-all-done.1.came), custom_call_target="tpu_custom_call" | custom-call | bytes 3145728 | tf_op jit(solution)/shard_map/cross_sum/pallas_call | solution.py:36
  59.8 7.2 %all-to-all-start.2 = ((bf16[8,54,128]{2,1,0:T(8,128)(2,1)}), bf16[8,54,128]{2,1,0:T(8,128)(2,1)S(1)}, u32[]{:S(2)}, u32[]{:S(2)}) async-start(bf16[8,54,128]{2,1,0:T(8,128)(2,1)} %cross_sum.1), calls=%async_computation.2 | async-start | bytes 229376 | tf_op jit(solution)/shard_map/all_to_all | solution.py:307
  67.0 0.0 collective-permute-done.3.refs_1_
  67.0 0.0 collective-permute-done.4.refs_2_
  67.0 0.0 collective-permute-done.5.refs_3_
  67.1 0.0 copy-done
  67.1 0.1 table_second.1
  67.2 0.1 collective-permute-start.6
  67.3 2.3 %collective-permute-start.7 = (bf16[26,8,128]{2,1,0:T(8,128)(2,1)S(1)}, bf16[26,8,128]{2,1,0:T(8,128)(2,1)S(1)}, u32[]{:S(2)}, u32[]{:S(2)}) collective-permute-start(bf16[26,8,128]{2,1,0:T(8,128)(2,1)S(1)} %get-tuple-element.28), channel_id=1, source_target_pairs={{0,128},{64,192},{128,0},{192,64},{1,129},{65,193},{129,1},{193,65... | collective-permute-start | bytes 159752 | tf_op jit(solution)/shard_map/ppermute | solution.py:198
  69.6 1.8 %collective-permute-start.8 = (bf16[26,8,128]{2,1,0:T(8,128)(2,1)S(1)}, bf16[26,8,128]{2,1,0:T(8,128)(2,1)S(1)}, u32[]{:S(2)}, u32[]{:S(2)}) collective-permute-start(bf16[26,8,128]{2,1,0:T(8,128)(2,1)S(1)} %get-tuple-element.29), channel_id=1, source_target_pairs={{0,192},{64,0},{128,64},{192,128},{1,193},{65,1},{129,65},{193,129... | collective-permute-start | bytes 159752 | tf_op jit(solution)/shard_map/ppermute | solution.py:198
  71.4 1.7 %collective-permute-done.6.refs_1_ = bf16[26,8,128]{2,1,0:T(8,128)(2,1)S(1)} collective-permute-done((bf16[26,8,128]{2,1,0:T(8,128)(2,1)S(1)}, bf16[26,8,128]{2,1,0:T(8,128)(2,1)S(1)}, u32[]{:S(2)}, u32[]{:S(2)}) %collective-permute-start.6) | collective-permute-done | bytes 53280 | tf_op jit(solution)/shard_map/ppermute | solution.py:198
  73.2 0.0 collective-permute-done.7.refs_2_
  73.2 0.9 collective-permute-done.8.refs_3_
  74.0 1.3 %route.1 = bf16[32,16,128]{2,1,0:T(8,128)(2,1)} custom-call(s32[119]{0:T(128)S(1)} %copy-done.2, f32[26,8,128]{2,1,0:T(8,128)S(1)} %get-tuple-element.26.refs_0_, bf16[26,8,128]{2,1,0:T(8,128)(2,1)S(1)} %collective-permute-done.6.refs_1_, bf16[26,8,128]{2,1,0:T(8,128)(2,1)S(1)} %collective-permute-done.7.refs_2_, ...), custom_call_target="tpu_custom_call" | custom-call | bytes 1048576 | tf_op jit(solution)/shard_map/route/pallas_call | solution.py:36
  75.3 0.0 all-to-all-done.2.came
  75.3 8.3 %all-to-all-start.3 = ((bf16[32,16,128]{2,1,0:T(8,128)(2,1)}), bf16[32,16,128]{2,1,0:T(8,128)(2,1)S(1)}, u32[]{:S(2)}, u32[]{:S(2)}) async-start(bf16[32,16,128]{2,1,0:T(8,128)(2,1)} %route.1), calls=%async_computation.3 | async-start | bytes 262144 | tf_op jit(solution)/shard_map/all_to_all | solution.py:319
  83.7 0.6 cross_last.1
  84.3 9.0 %all-to-all-done.3.came = bf16[32,16,128]{2,1,0:T(8,128)(2,1)S(1)} async-done(((bf16[32,16,128]{2,1,0:T(8,128)(2,1)}), bf16[32,16,128]{2,1,0:T(8,128)(2,1)S(1)}, u32[]{:S(2)}, u32[]{:S(2)}) %all-to-all-start.3) | async-done | bytes 131104 | tf_op jit(solution)/shard_map/all_to_all | solution.py:319
  93.3 0.6 table_last.1
  (7 shorter events, 0.0 us)
Async XLA Ops:
  0.6 16.4 %collective-permute-start.1 = (bf16[128,3456]{1,0:T(8,128)(2,1)}, bf16[128,3456]{1,0:T(8,128)(2,1)S(1)}, u32[]{:S(2)}, u32[]{:S(2)}) collective-permute-start(bf16[128,3456]{1,0:T(8,128)(2,1)} %up_in.1), channel_id=1, source_target_pairs={{0,32},{32,0},{1,33},{33,1},{2,34},{34,2},{3,35},{35,3},{4,36},{36... | collective-permute-start | bytes 2654216 | tf_op jit(solution)/shard_map/ppermute | solution.py:207
  0.7 16.3 %collective-permute-start = (bf16[128,3456]{1,0:T(8,128)(2,1)}, bf16[128,3456]{1,0:T(8,128)(2,1)S(1)}, u32[]{:S(2)}, u32[]{:S(2)}) collective-permute-start(bf16[128,3456]{1,0:T(8,128)(2,1)} %x.1), channel_id=1, source_target_pairs={{0,32},{32,0},{1,33},{33,1},{2,34},{34,2},{3,35},{35,3},{4,36},{36... | collective-permute-start | bytes 2654216 | tf_op jit(solution)/shard_map/ppermute | solution.py:206
  1.2 0.9 copy-start.1
  2.8 23.2 %all-to-all-start = ((s16[32,8,128]{2,1,0:T(8,128)(2,1)}), s16[32,8,128]{2,1,0:T(8,128)(2,1)S(1)}, u32[]{:S(2)}, u32[]{:S(2)}) async-start(s16[32,8,128]{2,1,0:T(8,128)(2,1)} %ids.2), calls=%async_computation | async-start | bytes 131072 | tf_op jit(solution)/shard_map/all_to_all | solution.py:210
  17.1 0.9 copy-start.3
  18.0 0.9 copy-start.4
  26.0 7.0 %copy-start.5 = (s16[32,8,128]{2,1,0:T(8,128)(2,1)}, s16[32,8,128]{2,1,0:T(8,128)(2,1)S(1)}, u32[]{:S(2)}) copy-start(s16[32,8,128]{2,1,0:T(8,128)(2,1)S(1)} %all-to-all-done.ids) | copy-start | bytes 196612
  26.0 7.1 %copy-start.7 = (f32[3456]{0:T(1024)S(1)}, f32[3456]{0:T(1024)}, u32[]{:S(2)}) copy-start(f32[3456]{0:T(1024)} %param.11) | copy-start | bytes 41476
  26.0 32.8 %all-to-all-start.1 = ((bf16[16,8,6912]{2,1,0:T(8,128)(2,1)}), bf16[16,8,6912]{2,1,0:T(8,128)(2,1)S(1)}, u32[]{:S(2)}, u32[]{:S(2)}) async-start(bf16[16,8,6912]{2,1,0:T(8,128)(2,1)} %get-tuple-element.18), calls=%async_computation.1 | async-start | bytes 3538944 | tf_op jit(solution)/shard_map/all_to_all | solution.py:254
  33.0 1.3 %collective-permute-start.2 = (s16[32,8,128]{2,1,0:T(8,128)(2,1)S(1)}, s16[32,8,128]{2,1,0:T(8,128)(2,1)S(1)}, u32[]{:S(2)}, u32[]{:S(2)}) collective-permute-start(s16[32,8,128]{2,1,0:T(8,128)(2,1)S(1)} %all-to-all-done.ids), channel_id=1, source_target_pairs={{0,32},{32,0},{1,33},{33,1},{2,34},{34,2},{3,35},{35,3},{4,36},{36... | collective-permute-start | bytes 196616 | tf_op jit(solution)/shard_map/ppermute | solution.py:255
  34.4 0.6 copy-start.6
  42.9 24.1 %copy-start = (f32[26,32,128]{2,1,0:T(8,128)S(1)}, f32[26,32,128]{2,1,0:T(8,128)}, u32[]{:S(2)}) copy-start(f32[26,32,128]{2,1,0:T(8,128)} %get-tuple-element.22.refs_0_) | copy-start | bytes 1277956
  42.9 31.1 %copy-start.2 = (s32[119]{0:T(128)S(1)}, s32[119]{0:T(128)}, u32[]{:S(2)}) copy-start(s32[119]{0:T(128)} %concatenate.3.meta) | copy-start | bytes 1432
  42.9 24.1 %collective-permute-start.3 = (bf16[26,32,128]{2,1,0:T(8,128)(2,1)}, bf16[26,32,128]{2,1,0:T(8,128)(2,1)S(1)}, u32[]{:S(2)}, u32[]{:S(2)}) collective-permute-start(bf16[26,32,128]{2,1,0:T(8,128)(2,1)} %get-tuple-element.23), channel_id=1, source_target_pairs={{0,8},{8,16},{16,24},{24,0},{1,9},{9,17},{17,25},{25,1},{2,10},{10... | collective-permute-start | bytes 638984 | tf_op jit(solution)/shard_map/ppermute | solution.py:198
  44.9 22.1 %collective-permute-start.4 = (bf16[26,32,128]{2,1,0:T(8,128)(2,1)}, bf16[26,32,128]{2,1,0:T(8,128)(2,1)S(1)}, u32[]{:S(2)}, u32[]{:S(2)}) collective-permute-start(bf16[26,32,128]{2,1,0:T(8,128)(2,1)} %get-tuple-element.24), channel_id=1, source_target_pairs={{0,16},{8,24},{16,0},{24,8},{1,17},{9,25},{17,1},{25,9},{2,18},{10... | collective-permute-start | bytes 638984 | tf_op jit(solution)/shard_map/ppermute | solution.py:198
  47.6 19.4 %collective-permute-start.5 = (bf16[26,32,128]{2,1,0:T(8,128)(2,1)}, bf16[26,32,128]{2,1,0:T(8,128)(2,1)S(1)}, u32[]{:S(2)}, u32[]{:S(2)}) collective-permute-start(bf16[26,32,128]{2,1,0:T(8,128)(2,1)} %get-tuple-element.25), channel_id=1, source_target_pairs={{0,24},{8,0},{16,8},{24,16},{1,25},{9,1},{17,9},{25,17},{2,26},{10... | collective-permute-start | bytes 638984 | tf_op jit(solution)/shard_map/ppermute | solution.py:198
  59.8 15.5 %all-to-all-start.2 = ((bf16[8,54,128]{2,1,0:T(8,128)(2,1)}), bf16[8,54,128]{2,1,0:T(8,128)(2,1)S(1)}, u32[]{:S(2)}, u32[]{:S(2)}) async-start(bf16[8,54,128]{2,1,0:T(8,128)(2,1)} %cross_sum.1), calls=%async_computation.2 | async-start | bytes 229376 | tf_op jit(solution)/shard_map/all_to_all | solution.py:307
  67.2 6.0 %collective-permute-start.6 = (bf16[26,8,128]{2,1,0:T(8,128)(2,1)S(1)}, bf16[26,8,128]{2,1,0:T(8,128)(2,1)S(1)}, u32[]{:S(2)}, u32[]{:S(2)}) collective-permute-start(bf16[26,8,128]{2,1,0:T(8,128)(2,1)S(1)} %get-tuple-element.27), channel_id=1, source_target_pairs={{0,64},{64,128},{128,192},{192,0},{1,65},{65,129},{129,193},{193,1... | collective-permute-start | bytes 159752 | tf_op jit(solution)/shard_map/ppermute | solution.py:198
  67.3 5.9 %collective-permute-start.7 = (bf16[26,8,128]{2,1,0:T(8,128)(2,1)S(1)}, bf16[26,8,128]{2,1,0:T(8,128)(2,1)S(1)}, u32[]{:S(2)}, u32[]{:S(2)}) collective-permute-start(bf16[26,8,128]{2,1,0:T(8,128)(2,1)S(1)} %get-tuple-element.28), channel_id=1, source_target_pairs={{0,128},{64,192},{128,0},{192,64},{1,129},{65,193},{129,1},{193,65... | collective-permute-start | bytes 159752 | tf_op jit(solution)/shard_map/ppermute | solution.py:198
  69.6 4.4 %collective-permute-start.8 = (bf16[26,8,128]{2,1,0:T(8,128)(2,1)S(1)}, bf16[26,8,128]{2,1,0:T(8,128)(2,1)S(1)}, u32[]{:S(2)}, u32[]{:S(2)}) collective-permute-start(bf16[26,8,128]{2,1,0:T(8,128)(2,1)S(1)} %get-tuple-element.29), channel_id=1, source_target_pairs={{0,192},{64,0},{128,64},{192,128},{1,193},{65,1},{129,65},{193,129... | collective-permute-start | bytes 159752 | tf_op jit(solution)/shard_map/ppermute | solution.py:198
  75.3 18.0 %all-to-all-start.3 = ((bf16[32,16,128]{2,1,0:T(8,128)(2,1)}), bf16[32,16,128]{2,1,0:T(8,128)(2,1)S(1)}, u32[]{:S(2)}, u32[]{:S(2)}) async-start(bf16[32,16,128]{2,1,0:T(8,128)(2,1)} %route.1), calls=%async_computation.3 | async-start | bytes 262144 | tf_op jit(solution)/shard_map/all_to_all | solution.py:319

commit v4 on v3

v4 whole, which is shorter than its diff:
```python
import math

import jax
import jax.numpy as jnp
from jax import lax
from jax.experimental import pallas as pl
from jax.experimental.pallas import tpu as pltpu
from jax.sharding import Mesh
from jax.sharding import PartitionSpec as P

EMB = 128
TABLES = 26
RANK = 256
NX, NY, NZ = 4, 4, 8
NJ = NY * NZ
BF = jnp.bfloat16
F32 = jnp.float32
I32 = jnp.int32
I16 = jnp.int16

VMEM = pl.BlockSpec(memory_space=pltpu.VMEM)
SMEM = pl.BlockSpec(memory_space=pltpu.SMEM)
HBM = pl.BlockSpec(memory_space=pltpu.HBM)


def nt(left, right):
    return lax.dot_general(left, right, (((1,), (1,)), ((), ())), preferred_element_type=F32)


def mm(left, right):
    return jnp.dot(left, right, preferred_element_type=F32)


def call(kernel, name, outs, *args, specs=None, out_specs=None, scratch=(), flops=0, size=0, vmem=24 << 20):
    return pl.pallas_call(
        kernel,
        out_shape=tuple(jax.ShapeDtypeStruct(shape, dtype) for shape, dtype in outs),
        in_specs=specs or [SMEM] + [VMEM] * (len(args) - 1),
        out_specs=tuple(out_specs or [VMEM] * len(outs)),
        scratch_shapes=list(scratch),
        compiler_params=pltpu.CompilerParams(vmem_limit_bytes=vmem),
        cost_estimate=pl.CostEstimate(flops=flops, bytes_accessed=size, transcendentals=0),
        name=name,
    )(*args)


def ids_kernel(ids, out):
    for j in range(NJ):
        parts = [ids[s, :, j * EMB : (j + 1) * EMB] for s in range(2)]
        out[j] = jnp.concatenate(parts, axis=0).astype(I16)


def own_rows(full, core):
    picks = [
        jnp.where(core == 0, full[i * 64 : i * 64 + 32], full[i * 64 + 32 : i * 64 + 64])
        for i in range(NX)
    ]
    return jnp.concatenate(picks, axis=0)


def dense_kernel(x, px, up, pup, v_in, u_in, hid, hgr, out, both, prod, v, u, held, in_sems, sems):
    n, width = x.shape
    core = lax.axis_index("c")
    loads = []
    for source, target in ((v_in, v), (u_in, u)):
        for k in range(2):
            rows = slice(k * 128, (k + 1) * 128)
            loads.append(
                pltpu.make_async_copy(source.at[rows], target.at[rows], in_sems.at[len(loads)])
            )
            loads[-1].start()
    both[:n] = x[...]
    both[n:] = px[...]
    prod[:n] = (x[...].astype(F32) * up[...].astype(F32)).astype(BF)
    prod[n:] = (px[...].astype(F32) * pup[...].astype(F32)).astype(BF)
    loads[0].wait()
    loads[1].wait()
    hid[...] = nt(v[...], both[...]).astype(BF)
    loads[2].wait()
    loads[3].wait()
    hgr[...] = nt(u[...], prod[...]).astype(BF)
    hid_own = own_rows(hid[...].astype(F32), core).astype(BF)
    hgr_own = own_rows(hgr[...].astype(F32), core).astype(BF)
    step = 1152
    copies = []
    for side, (left, right) in enumerate(((hid_own, prod), (hgr_own, both))):
        for k in range(width // step):
            total = mm(left, right[:, k * step : (k + 1) * step])
            cols = slice(side * width + k * step, side * width + (k + 1) * step)
            for i in range(NX * NY):
                held[i, :, cols] = total[i * 8 : (i + 1) * 8].astype(BF)
            copies.append(
                pltpu.make_async_copy(
                    held.at[:, :, cols], out.at[:, :, cols], sems.at[len(copies)]
                )
            )
            copies[-1].start()
    for copy in copies:
        copy.wait()


def slots_of(placement, used, visit):
    for j in range(NJ):
        used[j] = 0
    for table in range(TABLES):
        owner = placement[table]
        slot = used[owner]
        used[owner] = slot + 1
        visit(table, owner, slot)


def table_kernel(placement, hid, hgr, up, u, v, pup, bias, ids, pids, *refs):
    outs, (state, counts, used) = refs[:4], refs[4:]
    n = up.shape[0]
    for p in range(NJ):
        state[p, :8] = ids[p].astype(I32)
        state[p, 8:] = pids[p].astype(I32)
    at = lax.broadcasted_iota(I32, (RANK // 2, n), 0)
    row = lax.rem(lax.axis_index("x") + (at // 8) % 4, NX) * 64 + at % 8
    row = row + lax.rem(lax.axis_index("y") + at // 32, NY) * 8 + lax.axis_index("c") * 32

    def count_rows(table, owner, slot):
        looked = state[owner]
        for half in range(2):
            eight = looked[half * 8 : half * 8 + 8]
            four = jnp.where(slot == 0, eight[:4], eight[4:])
            count = jnp.where(four[0:1] == row, 1.0, 0.0)
            for k in range(1, 4):
                count = count + jnp.where(four[k : k + 1] == row, 1.0, 0.0)
            counts[table, :, half * n : (half + 1) * n] = count.astype(BF)

    slots_of(placement, used, count_rows)
    hid_s = hid[...].astype(F32).T.astype(BF)
    hgr_s = hgr[...].astype(F32).T.astype(BF)
    for pair in range(TABLES // 2):
        cols = slice(EMB + pair * 256, EMB + pair * 256 + 256)
        mixed = mm(hid_s, u[:, cols]) + bias[:, cols]
        back = mm(hgr_s, v[:, cols])
        up_float = jnp.concatenate([up[:, cols], pup[:, cols]], axis=0).astype(F32)
        pooled = (up_float * (1.0 + mixed) + back).astype(BF)
        for which in range(2):
            table = 2 * pair + which
            total = mm(counts[table], pooled[:, which * EMB : (which + 1) * EMB])
            for d in range(NY):
                outs[d][table] = total[d * 32 : (d + 1) * 32].astype(outs[d].dtype)


def total_of(refs):
    total = refs[0][...].astype(F32)
    for ref in refs[1:]:
        total = total + ref[...].astype(F32)
    return total


def table_second(*refs):
    total = total_of(refs[:NY])
    for d in range(NX):
        refs[NY + d][...] = total[:, d * 8 : (d + 1) * 8].astype(refs[NY + d].dtype)


def route_kernel(placement, *refs):
    came, outs, (held, used, at) = refs[:NX], refs[NX : NX + NY], refs[NX + NY :]
    for k in range(2 * NJ):
        at[k] = 0

    def note(table, owner, slot):
        at[2 * owner + slot] = table + 1

    slots_of(placement, used, note)
    held[0] = jnp.zeros((8, EMB), F32)
    held[1:] = total_of(came)
    for d in range(NY):
        first = lax.rem(lax.axis_index("y") + d, NY) * NZ
        for z in range(NZ):
            slots = [held[at[2 * (first + z) + s]] for s in range(2)]
            outs[d][z] = jnp.concatenate(slots, axis=0).astype(BF)


def to_z_kernel(cross, *refs):
    routed, out, sums = refs[:NY], refs[NY], refs[NY + 1]
    for k in range(cross.shape[2] // EMB):
        cols = slice(k * EMB, (k + 1) * EMB)
        total = cross[0, :, cols].astype(F32)
        for i in range(1, NX * NY):
            total = total + cross[i, :, cols].astype(F32)
        sums[:, k] = total
    for z in range(NZ):
        for d in range(NY):
            out[z, d * 16 : (d + 1) * 16] = routed[d][z]
        out[z, 64:] = sums[z].astype(BF)


def last_kernel(came, cross, table):
    scale = 1.0 / math.sqrt(EMB * 256)
    total = came[0].astype(F32)
    for z in range(1, NZ):
        total = total + came[z].astype(F32)
    for k in range(cross.shape[1] // EMB):
        cross[:, k * EMB : (k + 1) * EMB] = total[64 + k : 65 + k] * scale
    for d in range(NY):
        start = pl.multiple_of(lax.rem(lax.axis_index("y") + NY - d, NY) * 8, 8)
        for s in range(2):
            table[s, pl.ds(start, 8)] = total[d * 16 + s * 8 : d * 16 + s * 8 + 8]


def shift(chunks, axis):
    n = len(chunks)
    return [chunks[0]] + [
        lax.ppermute(chunks[d], axis, [(i, (i + d) % n) for i in range(n)]) for d in range(1, n)
    ]


def on_device(cross_input, upstream, v_weight, u_weight, bias, placement, owned_ids):
    samples, width = cross_input.shape
    blocks = 2 * width // EMB
    swap = [(0, 1), (1, 0)]
    px = lax.ppermute(cross_input, "c", swap)
    pup = lax.ppermute(upstream, "c", swap)

    (ids,) = call(ids_kernel, "ids", [((NJ, 8, EMB), I16)], owned_ids, specs=[VMEM], flops=40 << 30, size=60 << 20, vmem=4 << 20)
    ids = lax.all_to_all(ids, ("y", "z"), 0, 0, tiled=True)

    hid, hgr, cross = call(
        dense_kernel,
        "dense",
        [((RANK, 2 * samples), BF)] * 2 + [((NX * NY, NZ, 2 * width), BF)],
        cross_input,
        px,
        upstream,
        pup,
        v_weight,
        u_weight,
        specs=[VMEM] * 4 + [HBM] * 2,
        out_specs=[VMEM] * 2 + [HBM],
        scratch=[pltpu.VMEM((2 * samples, width), BF)] * 2
        + [pltpu.VMEM((RANK, width), BF)] * 2
        + [
            pltpu.VMEM((NX * NY, NZ, 2 * width), BF),
            pltpu.SemaphoreType.DMA((4,)),
            pltpu.SemaphoreType.DMA((6,)),
        ],
        vmem=50 << 20,
        flops=6 * 256 * 256 * width,
        size=6 << 20,
    )
    ids, cross = lax.optimization_barrier((ids, cross))
    cross = lax.all_to_all(cross, ("x", "y"), 0, 0, tiled=True)
    pids = lax.ppermute(ids, "c", swap)

    tables = call(
        table_kernel,
        "tables",
        [((TABLES, 32, EMB), F32)] + [((TABLES, 32, EMB), BF)] * 3,
        placement,
        hid,
        hgr,
        upstream,
        u_weight,
        v_weight,
        pup,
        bias[None],
        ids,
        pids,
        scratch=[
            pltpu.VMEM((NJ, 16, EMB), I32),
            pltpu.VMEM((TABLES, RANK // 2, 2 * samples), BF),
            pltpu.SMEM((NJ,), I32),
        ],
        vmem=40 << 20,
        flops=6 * 256 * 256 * width,
        size=9 << 20,
    )
    tables = shift(tables, "y")
    tables = call(
        table_second,
        "table_second",
        [((TABLES, 8, EMB), F32)] + [((TABLES, 8, EMB), BF)] * 3,
        *tables,
        specs=[VMEM] * 4,
        size=1 << 20,
    )
    tables = shift(tables, "x")
    routed = call(
        route_kernel,
        "route",
        [((NZ, 16, EMB), BF)] * NY,
        placement,
        *tables,
        scratch=[
            pltpu.VMEM((TABLES + 1, 8, EMB), F32),
            pltpu.SMEM((NJ,), I32),
            pltpu.SMEM((2 * NJ,), I32),
        ],
        size=1 << 20,
    )
    routed = shift(routed, "y")
    (both,) = call(
        to_z_kernel,
        "to_z",
        [((NZ, 64 + blocks, EMB), BF)],
        cross,
        *routed,
        specs=[VMEM] * (1 + NY),
        scratch=[pltpu.VMEM((NZ, blocks, EMB), F32)],
        size=3 << 20,
    )
    both = lax.all_to_all(both, "z", 0, 0, tiled=True)
    return call(
        last_kernel,
        "last",
        [((1, 2 * width), F32), ((2, NJ, EMB), F32)],
        both,
        specs=[VMEM],
        size=300000,
    )


def solution(mesh):
    fine = Mesh(mesh.devices.reshape(NX, 2, NY, NZ), ("x", "c", "y", "z"))
    grp, tbl = ("x", "c"), ("y", "z")
    in_specs = (
        P(grp + tbl, None),
        P(grp + tbl, None),
        P(),
        P(),
        P(),
        P(),
        P(tbl, None, grp),
    )
    out_specs = (P(grp + tbl, None), P(tbl, grp, None))
    return jax.shard_map(
        on_device, mesh=fine, in_specs=in_specs, out_specs=out_specs, check_vma=False
    )
```

time: 95.3 us -> 97 us (1.018)
  the two profiles are of different devices: /device:TPU:32 before, /device:TPU:2 now
where the time goes in v4:
time: 97 us; the launch traced here: 96.5 us
  starting transfers between devices  32.7 us (34%)
  waiting for transfers between devices  25.7 us (26%)
  blocking collectives  15.7 us (16%)
  Pallas kernels  13.9 us (14%)
  local copies, waits for them, and re-layouts  7.71 us (8%)
    ppermute x9, waiting for transfers between devices, shift(): lax.ppermute(chunks[d], axis, [(i, (i + d) % n) for i in range(n)])  21.8 us
    all_to_all x1, blocking collectives, on_device(): both = lax.all_to_all(both, 'z', 0, 0, tiled=True)  15.7 us
    ppermute x9, starting transfers between devices, shift(): lax.ppermute(chunks[d], axis, [(i, (i + d) % n) for i in range(n)])  14.6 us
    pallas_call x7, Pallas kernels, call(): pl.pallas_call(kernel, out_shape=tuple((jax.ShapeDtypeStruct(shape, dtype...  13.9 us
    all_to_all x1, starting transfers between devices, on_device(): ids = lax.all_to_all(ids, ('y', 'z'), 0, 0, tiled=True)  11.6 us
    unnamed x28, local copies, waits for them, and re-layouts  6.98 us
    all_to_all x1, starting transfers between devices, on_device(): cross = lax.all_to_all(cross, ('x', 'y'), 0, 0, tiled=True)  5.88 us
    all_to_all x1, waiting for transfers between devices, on_device(): ids = lax.all_to_all(ids, ('y', 'z'), 0, 0, tiled=True)  3.21 us
  transfers between devices with their start and end apart: 14, of which 9 were waited for; matrix products, arithmetic and copies ran while one was open for 1% of the time, Pallas kernels for 12%

profile of v4, /device:TPU:2, one launch (start us, length us, event | category | flops | bytes accessed | tf_op | source)
XLA Modules:
  0.0 96.5 jit_solution(11731841476822031238)
XLA Ops:
  0.6 0.0 copy-start.2
  0.6 0.0 copy-start.6
  0.7 0.1 collective-permute-start.1
  0.8 0.5 collective-permute-start
  1.3 0.9 copy-done.13
  2.2 0.6 copy-done.11
  2.8 11.6 %all-to-all-start = ((s16[32,8,128]{2,1,0:T(8,128)(2,1)}), s16[32,8,128]{2,1,0:T(8,128)(2,1)}, u32[]{:S(2)}, u32[]{:S(2)}) async-start(s16[32,8,128]{2,1,0:T(8,128)(2,1)} %copy-done.11), calls=%async_computation | async-start | bytes 131072 | tf_op jit(solution)/shard_map/all_to_all | solution.py:221
  14.4 0.0 collective-permute-done.1.pup
  14.4 0.0 copy-start.4
  14.4 0.0 collective-permute-done.px
  14.5 5.4 %dense.1 = (bf16[256,256]{1,0:T(8,128)(2,1)S(1)}, bf16[256,256]{1,0:T(8,128)(2,1)S(1)}, bf16[16,8,6912]{2,1,0:T(8,128)(2,1)}) custom-call(bf16[128,3456]{1,0:T(8,128)(2,1)S(1)} %copy-done.6, bf16[128,3456]{1,0:T(8,128)(2,1)S(1)} %collective-permute-done.px, bf16[128,3456]{1,0:T(8,128)(2,1)S(1)} %copy-done.2, ...), custom_call_target="tpu_custom_call" | custom-call | flops 1358954496 | bytes 6291456 | tf_op jit(solution)/shard_map/dense/pallas_call | solution.py:35
  19.9 0.6 copy-done.7
  20.6 0.7 copy-done.9
  21.2 3.2 %all-to-all-done.ids = s16[32,8,128]{2,1,0:T(8,128)(2,1)} async-done(((s16[32,8,128]{2,1,0:T(8,128)(2,1)}), s16[32,8,128]{2,1,0:T(8,128)(2,1)}, u32[]{:S(2)}, u32[]{:S(2)}) %all-to-all-start) | async-done | bytes 65568 | tf_op jit(solution)/shard_map/all_to_all | solution.py:221
  24.4 5.9 %all-to-all-start.1 = ((bf16[16,8,6912]{2,1,0:T(8,128)(2,1)}), bf16[16,8,6912]{2,1,0:T(8,128)(2,1)}, u32[]{:S(2)}, u32[]{:S(2)}) async-start(bf16[16,8,6912]{2,1,0:T(8,128)(2,1)} %get-tuple-element.20), calls=%async_computation.1 | async-start | bytes 3538944 | tf_op jit(solution)/shard_map/all_to_all | solution.py:247
  30.3 0.0 collective-permute-start.2
  30.3 0.7 broadcast_in_dim.3.bias
  31.0 0.7 collective-permute-done.2.pids
  31.8 0.0 copy-start.3
  31.8 1.2 %copy-done.3 = bf16[128,3456]{1,0:T(8,128)(2,1)S(1)} copy-done((bf16[128,3456]{1,0:T(8,128)(2,1)S(1)}, bf16[128,3456]{1,0:T(8,128)(2,1)}, u32[]{:S(2)}) %copy-start.3) | copy-done | bytes 884760
  32.9 1.2 %copy-done.5 = bf16[128,3456]{1,0:T(8,128)(2,1)S(1)} copy-done((bf16[128,3456]{1,0:T(8,128)(2,1)S(1)}, bf16[128,3456]{1,0:T(8,128)(2,1)}, u32[]{:S(2)}) %copy-start.5) | copy-done | bytes 884760
  34.1 0.9 copy-done.8
  35.0 0.9 copy-done.10
  35.9 5.1 %tables.1 = (f32[26,32,128]{2,1,0:T(8,128)S(1)}, bf16[26,32,128]{2,1,0:T(8,128)(2,1)S(1)}, bf16[26,32,128]{2,1,0:T(8,128)(2,1)S(1)}, bf16[26,32,128]{2,1,0:T(8,128)(2,1)S(1)}) custom-call(s32[26]{0:T(128)S(1)} %copy-done.12, bf16[256,256]{1,0:T(8,128)(2,1)S(1)} %copy-done.8, bf16[256,256]{1,0:T(8,128)(2,1)S(1)} %copy-done.10, ...), custom_call_target="tpu_custom_call" | custom-call | flops 1358954496 | bytes 9437184 | tf_op jit(solution)/shard_map/tables/pallas_call | solution.py:35
  41.0 1.5 %collective-permute-start.3 = (bf16[26,32,128]{2,1,0:T(8,128)(2,1)S(1)}, bf16[26,32,128]{2,1,0:T(8,128)(2,1)S(1)}, u32[]{:S(2)}, u32[]{:S(2)}) collective-permute-start(bf16[26,32,128]{2,1,0:T(8,128)(2,1)S(1)} %get-tuple-element.25), channel_id=1, source_target_pairs={{0,8},{8,16},{16,24},{24,0},{1,9},{9,17},{17,25},{25,1},{2,10},{10... | collective-permute-start | bytes 638984 | tf_op jit(solution)/shard_map/ppermute | solution.py:209
  42.6 2.7 %collective-permute-start.4 = (bf16[26,32,128]{2,1,0:T(8,128)(2,1)S(1)}, bf16[26,32,128]{2,1,0:T(8,128)(2,1)S(1)}, u32[]{:S(2)}, u32[]{:S(2)}) collective-permute-start(bf16[26,32,128]{2,1,0:T(8,128)(2,1)S(1)} %get-tuple-element.26), channel_id=1, source_target_pairs={{0,16},{8,24},{16,0},{24,8},{1,17},{9,25},{17,1},{25,9},{2,18},{10... | collective-permute-start | bytes 638984 | tf_op jit(solution)/shard_map/ppermute | solution.py:209
  45.2 1.5 %collective-permute-start.5 = (bf16[26,32,128]{2,1,0:T(8,128)(2,1)S(1)}, bf16[26,32,128]{2,1,0:T(8,128)(2,1)S(1)}, u32[]{:S(2)}, u32[]{:S(2)}) collective-permute-start(bf16[26,32,128]{2,1,0:T(8,128)(2,1)S(1)} %get-tuple-element.27), channel_id=1, source_target_pairs={{0,24},{8,0},{16,8},{24,16},{1,25},{9,1},{17,9},{25,17},{2,26},{10... | collective-permute-start | bytes 638984 | tf_op jit(solution)/shard_map/ppermute | solution.py:209
  46.7 9.2 %collective-permute-done.3.refs_1_ = bf16[26,32,128]{2,1,0:T(8,128)(2,1)S(1)} collective-permute-done((bf16[26,32,128]{2,1,0:T(8,128)(2,1)S(1)}, bf16[26,32,128]{2,1,0:T(8,128)(2,1)S(1)}, u32[]{:S(2)}, u32[]{:S(2)}) %collective-permute-start.3) | collective-permute-done | bytes 213024 | tf_op jit(solution)/shard_map/ppermute | solution.py:209
  56.0 5.7 %collective-permute-done.4.refs_2_ = bf16[26,32,128]{2,1,0:T(8,128)(2,1)S(1)} collective-permute-done((bf16[26,32,128]{2,1,0:T(8,128)(2,1)S(1)}, bf16[26,32,128]{2,1,0:T(8,128)(2,1)S(1)}, u32[]{:S(2)}, u32[]{:S(2)}) %collective-permute-start.4) | collective-permute-done | bytes 213024 | tf_op jit(solution)/shard_map/ppermute | solution.py:209
  61.7 0.0 collective-permute-done.5.refs_3_
  61.7 0.1 table_second.1
  61.8 1.8 %collective-permute-start.6 = (bf16[26,8,128]{2,1,0:T(8,128)(2,1)S(1)}, bf16[26,8,128]{2,1,0:T(8,128)(2,1)S(1)}, u32[]{:S(2)}, u32[]{:S(2)}) collective-permute-start(bf16[26,8,128]{2,1,0:T(8,128)(2,1)S(1)} %get-tuple-element.29), channel_id=1, source_target_pairs={{0,64},{64,128},{128,192},{192,0},{1,65},{65,129},{129,193},{193,1... | collective-permute-start | bytes 159752 | tf_op jit(solution)/shard_map/ppermute | solution.py:209
  63.7 2.4 %collective-permute-start.7 = (bf16[26,8,128]{2,1,0:T(8,128)(2,1)S(1)}, bf16[26,8,128]{2,1,0:T(8,128)(2,1)S(1)}, u32[]{:S(2)}, u32[]{:S(2)}) collective-permute-start(bf16[26,8,128]{2,1,0:T(8,128)(2,1)S(1)} %get-tuple-element.30), channel_id=1, source_target_pairs={{0,128},{64,192},{128,0},{192,64},{1,129},{65,193},{129,1},{193,65... | collective-permute-start | bytes 159752 | tf_op jit(solution)/shard_map/ppermute | solution.py:209
  66.1 0.5 collective-permute-start.8
  66.6 0.0 collective-permute-done.6.refs_1_
  66.6 2.7 %collective-permute-done.7.refs_2_ = bf16[26,8,128]{2,1,0:T(8,128)(2,1)S(1)} collective-permute-done((bf16[26,8,128]{2,1,0:T(8,128)(2,1)S(1)}, bf16[26,8,128]{2,1,0:T(8,128)(2,1)S(1)}, u32[]{:S(2)}, u32[]{:S(2)}) %collective-permute-start.7) | collective-permute-done | bytes 53280 | tf_op jit(solution)/shard_map/ppermute | solution.py:209
  69.3 0.9 collective-permute-done.8.refs_3_
  70.2 0.8 route.1
  71.0 2.2 %collective-permute-start.10 = (bf16[8,16,128]{2,1,0:T(8,128)(2,1)S(1)}, bf16[8,16,128]{2,1,0:T(8,128)(2,1)S(1)}, u32[]{:S(2)}, u32[]{:S(2)}) collective-permute-start(bf16[8,16,128]{2,1,0:T(8,128)(2,1)S(1)} %get-tuple-element.34), channel_id=1, source_target_pairs={{0,16},{8,24},{16,0},{24,8},{1,17},{9,25},{17,1},{25,9},{2,18},{10... | collective-permute-start | bytes 98312 | tf_op jit(solution)/shard_map/ppermute | solution.py:209
  73.2 0.0 collective-permute-start.11
  73.2 2.0 %collective-permute-start.9 = (bf16[8,16,128]{2,1,0:T(8,128)(2,1)S(1)}, bf16[8,16,128]{2,1,0:T(8,128)(2,1)S(1)}, u32[]{:S(2)}, u32[]{:S(2)}) collective-permute-start(bf16[8,16,128]{2,1,0:T(8,128)(2,1)S(1)} %get-tuple-element.33), channel_id=1, source_target_pairs={{0,8},{8,16},{16,24},{24,0},{1,9},{9,17},{17,25},{25,1},{2,10},{10... | collective-permute-start | bytes 98312 | tf_op jit(solution)/shard_map/ppermute | solution.py:209
  75.2 1.3 %collective-permute-done.10.refs_2_ = bf16[8,16,128]{2,1,0:T(8,128)(2,1)S(1)} collective-permute-done((bf16[8,16,128]{2,1,0:T(8,128)(2,1)S(1)}, bf16[8,16,128]{2,1,0:T(8,128)(2,1)S(1)}, u32[]{:S(2)}, u32[]{:S(2)}) %collective-permute-start.10) | collective-permute-done | bytes 32800 | tf_op jit(solution)/shard_map/ppermute | solution.py:209
  76.5 0.6 collective-permute-done.11.refs_3_
  77.1 1.2 %collective-permute-done.9.refs_1_ = bf16[8,16,128]{2,1,0:T(8,128)(2,1)S(1)} collective-permute-done((bf16[8,16,128]{2,1,0:T(8,128)(2,1)S(1)}, bf16[8,16,128]{2,1,0:T(8,128)(2,1)S(1)}, u32[]{:S(2)}, u32[]{:S(2)}) %collective-permute-start.9) | collective-permute-done | bytes 32800 | tf_op jit(solution)/shard_map/ppermute | solution.py:209
  78.3 0.0 all-to-all-done.1.cross
  78.3 1.8 %to_z.1 = bf16[8,118,128]{2,1,0:T(8,128)(2,1)S(1)} custom-call(bf16[16,8,6912]{2,1,0:T(8,128)(2,1)} %all-to-all-done.1.cross, bf16[8,16,128]{2,1,0:T(8,128)(2,1)S(1)} %get-tuple-element.32.refs_0_, bf16[8,16,128]{2,1,0:T(8,128)(2,1)S(1)} %collective-permute-done.9.refs_1_, bf16[8,16,128]{2,1,0:T(8,128)(2,1)S(1)} %collective-permute-done.10.refs_2_, ...), custom_call_target="tpu_custom_call" | custom-call | bytes 3145728 | tf_op jit(solution)/shard_map/to_z/pallas_call | solution.py:35
  80.1 15.7 %all_to_all.15.came = bf16[8,118,128]{2,1,0:T(8,128)(2,1)S(1)} all-to-all(bf16[8,118,128]{2,1,0:T(8,128)(2,1)S(1)} %to_z.1), channel_id=1, replica_groups=mesh['x'=4,'c'=2,'y'=4,'z'=8] {'z'}, dimensions={0} | all-to-all | bytes 483328 | tf_op jit(solution)/shard_map/all_to_all | solution.py:307
  95.8 0.7 last.1
  (17 shorter events, 0.0 us)
Async XLA Ops:
  0.6 13.8 %copy-start.2 = (bf16[128,3456]{1,0:T(8,128)(2,1)S(1)}, bf16[128,3456]{1,0:T(8,128)(2,1)}, u32[]{:S(2)}) copy-start(bf16[128,3456]{1,0:T(8,128)(2,1)} %up.3) | copy-start | bytes 2654212
  0.6 13.8 %copy-start.6 = (bf16[128,3456]{1,0:T(8,128)(2,1)S(1)}, bf16[128,3456]{1,0:T(8,128)(2,1)}, u32[]{:S(2)}) copy-start(bf16[128,3456]{1,0:T(8,128)(2,1)} %x.1) | copy-start | bytes 2654212
  0.7 13.8 %collective-permute-start.1 = (bf16[128,3456]{1,0:T(8,128)(2,1)}, bf16[128,3456]{1,0:T(8,128)(2,1)S(1)}, u32[]{:S(2)}, u32[]{:S(2)}) collective-permute-start(bf16[128,3456]{1,0:T(8,128)(2,1)} %up.3), channel_id=1, source_target_pairs={{0,32},{32,0},{1,33},{33,1},{2,34},{34,2},{3,35},{35,3},{4,36},{36... | collective-permute-start | bytes 2654216 | tf_op jit(solution)/shard_map/ppermute | solution.py:218
  0.8 13.7 %collective-permute-start = (bf16[128,3456]{1,0:T(8,128)(2,1)}, bf16[128,3456]{1,0:T(8,128)(2,1)S(1)}, u32[]{:S(2)}, u32[]{:S(2)}) collective-permute-start(bf16[128,3456]{1,0:T(8,128)(2,1)} %x.1), channel_id=1, source_target_pairs={{0,32},{32,0},{1,33},{33,1},{2,34},{34,2},{3,35},{35,3},{4,36},{36... | collective-permute-start | bytes 2654216 | tf_op jit(solution)/shard_map/ppermute | solution.py:217
  1.2 0.9 copy-start.13
  2.2 0.6 copy-start.11
  2.8 21.6 %all-to-all-start = ((s16[32,8,128]{2,1,0:T(8,128)(2,1)}), s16[32,8,128]{2,1,0:T(8,128)(2,1)}, u32[]{:S(2)}, u32[]{:S(2)}) async-start(s16[32,8,128]{2,1,0:T(8,128)(2,1)} %copy-done.11), calls=%async_computation | async-start | bytes 131072 | tf_op jit(solution)/shard_map/all_to_all | solution.py:221
  14.4 5.5 %copy-start.4 = (bf16[128,3456]{1,0:T(8,128)(2,1)}, bf16[128,3456]{1,0:T(8,128)(2,1)S(1)}, u32[]{:S(2)}) copy-start(bf16[128,3456]{1,0:T(8,128)(2,1)S(1)} %collective-permute-done.1.pup) | copy-start | bytes 2654212
  19.9 0.7 copy-start.7
  20.6 0.7 copy-start.9
  24.4 7.4 %copy-start = (bf16[256,3456]{1,0:T(8,128)(2,1)S(1)}, bf16[256,3456]{1,0:T(8,128)(2,1)}, u32[]{:S(2)}) copy-start(bf16[256,3456]{1,0:T(8,128)(2,1)} %v.1) | copy-start | bytes 5308420
  24.4 7.4 %copy-start.1 = (bf16[256,3456]{1,0:T(8,128)(2,1)S(1)}, bf16[256,3456]{1,0:T(8,128)(2,1)}, u32[]{:S(2)}) copy-start(bf16[256,3456]{1,0:T(8,128)(2,1)} %u.1) | copy-start | bytes 5308420
  24.4 7.4 %copy-start.12 = (s32[26]{0:T(128)S(1)}, s32[26]{0:T(128)}, u32[]{:S(2)}) copy-start(s32[26]{0:T(128)} %placement.3) | copy-start | bytes 316
  24.4 53.9 %all-to-all-start.1 = ((bf16[16,8,6912]{2,1,0:T(8,128)(2,1)}), bf16[16,8,6912]{2,1,0:T(8,128)(2,1)}, u32[]{:S(2)}, u32[]{:S(2)}) async-start(bf16[16,8,6912]{2,1,0:T(8,128)(2,1)} %get-tuple-element.20), calls=%async_computation.1 | async-start | bytes 3538944 | tf_op jit(solution)/shard_map/all_to_all | solution.py:247
  30.3 1.5 %collective-permute-start.2 = (s16[32,8,128]{2,1,0:T(8,128)(2,1)}, s16[32,8,128]{2,1,0:T(8,128)(2,1)S(1)}, u32[]{:S(2)}, u32[]{:S(2)}) collective-permute-start(s16[32,8,128]{2,1,0:T(8,128)(2,1)} %all-to-all-done.ids), channel_id=1, source_target_pairs={{0,32},{32,0},{1,33},{33,1},{2,34},{34,2},{3,35},{35,3},{4,36},{36... | collective-permute-start | bytes 196616 | tf_op jit(solution)/shard_map/ppermute | solution.py:248
  31.8 1.2 %copy-start.3 = (bf16[128,3456]{1,0:T(8,128)(2,1)S(1)}, bf16[128,3456]{1,0:T(8,128)(2,1)}, u32[]{:S(2)}) copy-start(bf16[128,3456]{1,0:T(8,128)(2,1)} %up.3) | copy-start | bytes 2654212
  32.9 1.2 %copy-start.5 = (bf16[128,3456]{1,0:T(8,128)(2,1)S(1)}, bf16[128,3456]{1,0:T(8,128)(2,1)}, u32[]{:S(2)}) copy-start(bf16[128,3456]{1,0:T(8,128)(2,1)} %copy-done.4) | copy-start | bytes 2654212
  34.1 0.9 copy-start.8
  35.0 0.9 copy-start.10
  41.0 14.9 %collective-permute-start.3 = (bf16[26,32,128]{2,1,0:T(8,128)(2,1)S(1)}, bf16[26,32,128]{2,1,0:T(8,128)(2,1)S(1)}, u32[]{:S(2)}, u32[]{:S(2)}) collective-permute-start(bf16[26,32,128]{2,1,0:T(8,128)(2,1)S(1)} %get-tuple-element.25), channel_id=1, source_target_pairs={{0,8},{8,16},{16,24},{24,0},{1,9},{9,17},{17,25},{25,1},{2,10},{10... | collective-permute-start | bytes 638984 | tf_op jit(solution)/shard_map/ppermute | solution.py:209
  42.6 19.1 %collective-permute-start.4 = (bf16[26,32,128]{2,1,0:T(8,128)(2,1)S(1)}, bf16[26,32,128]{2,1,0:T(8,128)(2,1)S(1)}, u32[]{:S(2)}, u32[]{:S(2)}) collective-permute-start(bf16[26,32,128]{2,1,0:T(8,128)(2,1)S(1)} %get-tuple-element.26), channel_id=1, source_target_pairs={{0,16},{8,24},{16,0},{24,8},{1,17},{9,25},{17,1},{25,9},{2,18},{10... | collective-permute-start | bytes 638984 | tf_op jit(solution)/shard_map/ppermute | solution.py:209
  45.2 16.5 %collective-permute-start.5 = (bf16[26,32,128]{2,1,0:T(8,128)(2,1)S(1)}, bf16[26,32,128]{2,1,0:T(8,128)(2,1)S(1)}, u32[]{:S(2)}, u32[]{:S(2)}) collective-permute-start(bf16[26,32,128]{2,1,0:T(8,128)(2,1)S(1)} %get-tuple-element.27), channel_id=1, source_target_pairs={{0,24},{8,0},{16,8},{24,16},{1,25},{9,1},{17,9},{25,17},{2,26},{10... | collective-permute-start | bytes 638984 | tf_op jit(solution)/shard_map/ppermute | solution.py:209
  61.8 4.7 %collective-permute-start.6 = (bf16[26,8,128]{2,1,0:T(8,128)(2,1)S(1)}, bf16[26,8,128]{2,1,0:T(8,128)(2,1)S(1)}, u32[]{:S(2)}, u32[]{:S(2)}) collective-permute-start(bf16[26,8,128]{2,1,0:T(8,128)(2,1)S(1)} %get-tuple-element.29), channel_id=1, source_target_pairs={{0,64},{64,128},{128,192},{192,0},{1,65},{65,129},{129,193},{193,1... | collective-permute-start | bytes 159752 | tf_op jit(solution)/shard_map/ppermute | solution.py:209
  63.7 5.6 %collective-permute-start.7 = (bf16[26,8,128]{2,1,0:T(8,128)(2,1)S(1)}, bf16[26,8,128]{2,1,0:T(8,128)(2,1)S(1)}, u32[]{:S(2)}, u32[]{:S(2)}) collective-permute-start(bf16[26,8,128]{2,1,0:T(8,128)(2,1)S(1)} %get-tuple-element.30), channel_id=1, source_target_pairs={{0,128},{64,192},{128,0},{192,64},{1,129},{65,193},{129,1},{193,65... | collective-permute-start | bytes 159752 | tf_op jit(solution)/shard_map/ppermute | solution.py:209
  66.1 4.1 %collective-permute-start.8 = (bf16[26,8,128]{2,1,0:T(8,128)(2,1)S(1)}, bf16[26,8,128]{2,1,0:T(8,128)(2,1)S(1)}, u32[]{:S(2)}, u32[]{:S(2)}) collective-permute-start(bf16[26,8,128]{2,1,0:T(8,128)(2,1)S(1)} %get-tuple-element.31), channel_id=1, source_target_pairs={{0,192},{64,0},{128,64},{192,128},{1,193},{65,1},{129,65},{193,129... | collective-permute-start | bytes 159752 | tf_op jit(solution)/shard_map/ppermute | solution.py:209
  71.0 5.5 %collective-permute-start.10 = (bf16[8,16,128]{2,1,0:T(8,128)(2,1)S(1)}, bf16[8,16,128]{2,1,0:T(8,128)(2,1)S(1)}, u32[]{:S(2)}, u32[]{:S(2)}) collective-permute-start(bf16[8,16,128]{2,1,0:T(8,128)(2,1)S(1)} %get-tuple-element.34), channel_id=1, source_target_pairs={{0,16},{8,24},{16,0},{24,8},{1,17},{9,25},{17,1},{25,9},{2,18},{10... | collective-permute-start | bytes 98312 | tf_op jit(solution)/shard_map/ppermute | solution.py:209
  73.2 3.9 %collective-permute-start.11 = (bf16[8,16,128]{2,1,0:T(8,128)(2,1)S(1)}, bf16[8,16,128]{2,1,0:T(8,128)(2,1)S(1)}, u32[]{:S(2)}, u32[]{:S(2)}) collective-permute-start(bf16[8,16,128]{2,1,0:T(8,128)(2,1)S(1)} %get-tuple-element.35), channel_id=1, source_target_pairs={{0,24},{8,0},{16,8},{24,16},{1,25},{9,1},{17,9},{25,17},{2,26},{10... | collective-permute-start | bytes 98312 | tf_op jit(solution)/shard_map/ppermute | solution.py:209
  73.2 5.1 %collective-permute-start.9 = (bf16[8,16,128]{2,1,0:T(8,128)(2,1)S(1)}, bf16[8,16,128]{2,1,0:T(8,128)(2,1)S(1)}, u32[]{:S(2)}, u32[]{:S(2)}) collective-permute-start(bf16[8,16,128]{2,1,0:T(8,128)(2,1)S(1)} %get-tuple-element.33), channel_id=1, source_target_pairs={{0,8},{8,16},{16,24},{24,0},{1,9},{9,17},{17,25},{25,1},{2,10},{10... | collective-permute-start | bytes 98312 | tf_op jit(solution)/shard_map/ppermute | solution.py:209

commit v5 on v4

--- a/solution.py
+++ b/solution.py
@@ -50,17 +50,9 @@
         out[j] = jnp.concatenate(parts, axis=0).astype(I16)
 
 
-def own_rows(full, core):
-    picks = [
-        jnp.where(core == 0, full[i * 64 : i * 64 + 32], full[i * 64 + 32 : i * 64 + 64])
-        for i in range(NX)
-    ]
-    return jnp.concatenate(picks, axis=0)
-
-
-def dense_kernel(x, px, up, pup, v_in, u_in, hid, hgr, out, both, prod, v, u, held, in_sems, sems):
+def dense_kernel(x, px, up, pup, v_in, u_in, hid, hgr, by_x, *refs):
+    by_y, (both, prod, v, u, held, held_y, in_sems, sems) = refs[:4], refs[4:]
     n, width = x.shape
-    core = lax.axis_index("c")
     loads = []
     for source, target in ((v_in, v), (u_in, u)):
         for k in range(2):
@@ -79,22 +71,33 @@
     loads[2].wait()
     loads[3].wait()
     hgr[...] = nt(u[...], prod[...]).astype(BF)
-    hid_own = own_rows(hid[...].astype(F32), core).astype(BF)
-    hgr_own = own_rows(hgr[...].astype(F32), core).astype(BF)
+    at = lax.broadcasted_iota(I32, (RANK // 2, RANK), 0)
+    row = lax.broadcasted_iota(I32, (RANK // 2, RANK), 1)
+    base = lax.axis_index("c") * 32 + at % 8
+    to_x, to_y = lax.axis_index("x"), lax.axis_index("y")
+    row_x = base + (at // 32) * 64 + lax.rem(to_y + (at // 8) % 4, NY) * 8
+    row_y = base + lax.rem(to_x + (at // 8) % 4, NX) * 64 + lax.rem(to_y + at // 32, NY) * 8
+    hid_own = mm((row == row_x).astype(F32).astype(BF), hid[...]).astype(BF)
+    hgr_own = mm((row == row_y).astype(F32).astype(BF), hgr[...]).astype(BF)
     step = 1152
     copies = []
-    for side, (left, right) in enumerate(((hid_own, prod), (hgr_own, both))):
-        for k in range(width // step):
-            total = mm(left, right[:, k * step : (k + 1) * step])
-            cols = slice(side * width + k * step, side * width + (k + 1) * step)
-            for i in range(NX * NY):
-                held[i, :, cols] = total[i * 8 : (i + 1) * 8].astype(BF)
-            copies.append(
-                pltpu.make_async_copy(
-                    held.at[:, :, cols], out.at[:, :, cols], sems.at[len(copies)]
-                )
-            )
-            copies[-1].start()
+    for k in range(width // step):
+        cols = slice(k * step, (k + 1) * step)
+        total = mm(hgr_own, both[:, cols])
+        for d in range(4):
+            held_y[d, :, cols] = total[d * 32 : (d + 1) * 32].astype(BF)
+    for d in range(4):
+        copies.append(pltpu.make_async_copy(held_y.at[d], by_y[d], sems.at[d]))
+        copies[-1].start()
+    for k in range(width // step):
+        cols = slice(k * step, (k + 1) * step)
+        total = mm(hid_own, prod[:, cols])
+        for i in range(NX):
+            held[i, :, cols] = total[i * 32 : (i + 1) * 32].astype(BF)
+        copies.append(
+            pltpu.make_async_copy(held.at[:, :, cols], by_x.at[:, :, cols], sems.at[4 + k])
+        )
+        copies[-1].start()
     for copy in copies:
         copy.wait()
 
@@ -110,14 +113,13 @@
 
 
 def table_kernel(placement, hid, hgr, up, u, v, pup, bias, ids, pids, *refs):
-    outs, (state, counts, used) = refs[:4], refs[4:]
+    out, state, counts, used = refs
     n = up.shape[0]
     for p in range(NJ):
         state[p, :8] = ids[p].astype(I32)
         state[p, 8:] = pids[p].astype(I32)
     at = lax.broadcasted_iota(I32, (RANK // 2, n), 0)
-    row = lax.rem(lax.axis_index("x") + (at // 8) % 4, NX) * 64 + at % 8
-    row = row + lax.rem(lax.axis_index("y") + at // 32, NY) * 8 + lax.axis_index("c") * 32
+    row = (at // 32) * 64 + lax.axis_index("c") * 32 + at % 32
 
     def count_rows(table, owner, slot):
         looked = state[owner]
@@ -141,8 +143,8 @@
         for which in range(2):
             table = 2 * pair + which
             total = mm(counts[table], pooled[:, which * EMB : (which + 1) * EMB])
-            for d in range(NY):
-                outs[d][table] = total[d * 32 : (d + 1) * 32].astype(outs[d].dtype)
+            for k in range(NX * NY):
+                out[k, table] = total[k * 8 : (k + 1) * 8].astype(BF)
 
 
 def total_of(refs):
@@ -152,14 +154,20 @@
     return total
 
 
-def table_second(*refs):
-    total = total_of(refs[:NY])
-    for d in range(NX):
-        refs[NY + d][...] = total[:, d * 8 : (d + 1) * 8].astype(refs[NY + d].dtype)
+def cross_second(*refs):
+    came_x, came_y, outs = refs[0], refs[1:5], refs[5:]
+    total = came_x[0].astype(F32)
+    for i in range(1, NX):
+        total = total + came_x[i].astype(F32)
+    for d in range(4):
+        outs[d][...] = total[d * 8 : (d + 1) * 8].astype(outs[d].dtype)
+    total = total_of(came_y)
+    for d in range(4):
+        outs[4 + d][...] = total[d * 8 : (d + 1) * 8].astype(outs[4 + d].dtype)
 
 
 def route_kernel(placement, *refs):
-    came, outs, (held, used, at) = refs[:NX], refs[NX : NX + NY], refs[NX + NY :]
+    came, outs, (held, used, at) = refs[0], refs[1 : 1 + NY], refs[1 + NY :]
     for k in range(2 * NJ):
         at[k] = 0
 
@@ -168,7 +176,10 @@
 
     slots_of(placement, used, note)
     held[0] = jnp.zeros((8, EMB), F32)
-    held[1:] = total_of(came)
+    total = came[0].astype(F32)
+    for k in range(1, NX * NY):
+        total = total + came[k].astype(F32)
+    held[1:] = total
     for d in range(NY):
         first = lax.rem(lax.axis_index("y") + d, NY) * NZ
         for z in range(NZ):
@@ -176,14 +187,13 @@
             outs[d][z] = jnp.concatenate(slots, axis=0).astype(BF)
 
 
-def to_z_kernel(cross, *refs):
-    routed, out, sums = refs[:NY], refs[NY], refs[NY + 1]
-    for k in range(cross.shape[2] // EMB):
-        cols = slice(k * EMB, (k + 1) * EMB)
-        total = cross[0, :, cols].astype(F32)
-        for i in range(1, NX * NY):
-            total = total + cross[i, :, cols].astype(F32)
-        sums[:, k] = total
+def to_z_kernel(*refs):
+    cross, routed, out, sums = refs[:8], refs[8 : 8 + NY], refs[8 + NY], refs[9 + NY]
+    blocks = cross[0].shape[1] // EMB
+    for side in range(2):
+        total = total_of(cross[4 * side : 4 * side + 4])
+        for k in range(blocks):
+            sums[:, side * blocks + k] = total[:, k * EMB : (k + 1) * EMB]
     for z in range(NZ):
         for d in range(NY):
             out[z, d * 16 : (d + 1) * 16] = routed[d][z]
@@ -220,10 +230,11 @@
     (ids,) = call(ids_kernel, "ids", [((NJ, 8, EMB), I16)], owned_ids, specs=[VMEM], flops=40 << 30, size=60 << 20, vmem=4 << 20)
     ids = lax.all_to_all(ids, ("y", "z"), 0, 0, tiled=True)
 
-    hid, hgr, cross = call(
+    sent = [((NJ, width), BF)] * 4
+    hid, hgr, by_x, *by_y = call(
         dense_kernel,
         "dense",
-        [((RANK, 2 * samples), BF)] * 2 + [((NX * NY, NZ, 2 * width), BF)],
+        [((RANK, 2 * samples), BF)] * 2 + [((NX, NJ, width), BF)] + sent,
         cross_input,
         px,
         upstream,
@@ -231,26 +242,29 @@
         v_weight,
         u_weight,
         specs=[VMEM] * 4 + [HBM] * 2,
-        out_specs=[VMEM] * 2 + [HBM],
+        out_specs=[VMEM] * 2 + [HBM] * 5,
         scratch=[pltpu.VMEM((2 * samples, width), BF)] * 2
         + [pltpu.VMEM((RANK, width), BF)] * 2
         + [
-            pltpu.VMEM((NX * NY, NZ, 2 * width), BF),
+            pltpu.VMEM((NX, NJ, width), BF),
+            pltpu.VMEM((NY, NJ, width), BF),
             pltpu.SemaphoreType.DMA((4,)),
-            pltpu.SemaphoreType.DMA((6,)),
+            pltpu.SemaphoreType.DMA((7,)),
         ],
-        vmem=50 << 20,
+        vmem=57 << 20,
         flops=6 * 256 * 256 * width,
         size=6 << 20,
     )
-    ids, cross = lax.optimization_barrier((ids, cross))
-    cross = lax.all_to_all(cross, ("x", "y"), 0, 0, tiled=True)
+    by_y = shift(by_y, "y")
+    ids, by_x = lax.optimization_barrier((ids, by_x))
+    by_x = lax.all_to_all(by_x, "x", 0, 0, tiled=True)
+    hid, *by_y = lax.optimization_barrier((hid, *by_y))
     pids = lax.ppermute(ids, "c", swap)
 
-    tables = call(
+    (tables,) = call(
         table_kernel,
         "tables",
-        [((TABLES, 32, EMB), F32)] + [((TABLES, 32, EMB), BF)] * 3,
+        [((NX * NY, TABLES, 8, EMB), BF)],
         placement,
         hid,
         hgr,
@@ -270,22 +284,25 @@
         flops=6 * 256 * 256 * width,
         size=9 << 20,
     )
-    tables = shift(tables, "y")
-    tables = call(
-        table_second,
-        "table_second",
-        [((TABLES, 8, EMB), F32)] + [((TABLES, 8, EMB), BF)] * 3,
-        *tables,
-        specs=[VMEM] * 4,
-        size=1 << 20,
-    )
-    tables = shift(tables, "x")
+    by_x, tables = lax.optimization_barrier((by_x, tables))
+    tables = lax.all_to_all(tables, ("x", "y"), 0, 0, tiled=True)
+    sent = [((NZ, width), F32)] + [((NZ, width), BF)] * 3
+    cross = call(
+        cross_second,
+        "cross_second",
+        sent * 2,
+        by_x,
+        *by_y,
+        specs=[VMEM] * 5,
+        size=3 << 20,
+    )
+    cross = shift(cross[:4], "y") + shift(cross[4:], "x")
     routed = call(
         route_kernel,
         "route",
         [((NZ, 16, EMB), BF)] * NY,
         placement,
-        *tables,
+        tables,
         scratch=[
             pltpu.VMEM((TABLES + 1, 8, EMB), F32),
             pltpu.SMEM((NJ,), I32),
@@ -298,9 +315,9 @@
         to_z_kernel,
         "to_z",
         [((NZ, 64 + blocks, EMB), BF)],
-        cross,
+        *cross,
         *routed,
-        specs=[VMEM] * (1 + NY),
+        specs=[VMEM] * (8 + NY),
         scratch=[pltpu.VMEM((NZ, blocks, EMB), F32)],
         size=3 << 20,
     )

time: 97 us -> 102 us (1.052)
  the two profiles are of different devices: /device:TPU:2 before, /device:TPU:32 now
where the time goes in v5:
time: 102 us; the launch traced here: 100 us
  starting transfers between devices  45.2 us (44%)
  Pallas kernels  17.1 us (17%)
  blocking collectives  15.5 us (15%)
  waiting for transfers between devices  11 us (11%)
  local copies, waits for them, and re-layouts  10.6 us (10%)
    ppermute x12, starting transfers between devices, shift(): lax.ppermute(chunks[d], axis, [(i, (i + d) % n) for i in range(n)])  22.7 us
    pallas_call x7, Pallas kernels, call(): pl.pallas_call(kernel, out_shape=tuple((jax.ShapeDtypeStruct(shape, dtype...  17.1 us
    all_to_all x1, blocking collectives, on_device(): both = lax.all_to_all(both, 'z', 0, 0, tiled=True)  15.5 us
    all_to_all x1, starting transfers between devices, on_device(): ids = lax.all_to_all(ids, ('y', 'z'), 0, 0, tiled=True)  11.4 us
    ppermute x12, waiting for transfers between devices, shift(): lax.ppermute(chunks[d], axis, [(i, (i + d) % n) for i in range(n)])  10.9 us
    unnamed x36, local copies, waits for them, and re-layouts  9.86 us
    all_to_all x1, starting transfers between devices, on_device(): tables = lax.all_to_all(tables, ('x', 'y'), 0, 0, tiled=True)  6.04 us
    all_to_all x1, starting transfers between devices, on_device(): by_x = lax.all_to_all(by_x, 'x', 0, 0, tiled=True)  4.43 us
  transfers between devices with their start and end apart: 18, of which 6 were waited for; matrix products, arithmetic and copies ran while one was open for 1% of the time, Pallas kernels for 16%

profile of v5, /device:TPU:32, one launch (start us, length us, event | category | flops | bytes accessed | tf_op | source)
XLA Modules:
  0.0 100.2 jit_solution(2337327375787976996)
XLA Ops:
  0.6 0.1 collective-permute-start
  0.7 0.5 collective-permute-start.1
  1.2 0.9 copy-done.16
  2.1 0.6 ids.2
  2.8 11.4 %all-to-all-start = ((s16[32,8,128]{2,1,0:T(8,128)(2,1)}), s16[32,8,128]{2,1,0:T(8,128)(2,1)}, u32[]{:S(2)}, u32[]{:S(2)}) async-start(s16[32,8,128]{2,1,0:T(8,128)(2,1)} %ids.2), calls=%async_computation | async-start | bytes 131072 | tf_op jit(solution)/shard_map/all_to_all | solution.py:231
  14.2 0.0 collective-permute-done.px
  14.2 0.9 copy-done.17
  15.1 0.9 copy-done.3
  16.1 8.3 %dense.1 = (bf16[256,256]{1,0:T(8,128)(2,1)}, bf16[256,256]{1,0:T(8,128)(2,1)}, bf16[4,32,3456]{2,1,0:T(8,128)(2,1)}, bf16[32,3456]{1,0:T(8,128)(2,1)}, bf16[32,...) custom-call(bf16[128,3456]{1,0:T(8,128)(2,1)} %x.1, bf16[128,3456]{1,0:T(8,128)(2,1)} %copy-done.17, ...), custom_call_target="tpu_custom_call" | custom-call | flops 1358954496 | bytes 6291456 | tf_op jit(solution)/shard_map/dense/pallas_call | solution.py:35
  24.4 0.0 copy-start
  24.4 0.0 copy-start.15
  24.4 4.4 %all-to-all-start.1 = ((bf16[4,32,3456]{2,1,0:T(8,128)(2,1)}), bf16[4,32,3456]{2,1,0:T(8,128)(2,1)}, u32[]{:S(2)}, u32[]{:S(2)}) async-start(bf16[4,32,3456]{2,1,0:T(8,128)(2,1)} %get-tuple-element.31), calls=%async_computation.1 | async-start | bytes 1769472 | tf_op jit(solution)/shard_map/all_to_all | solution.py:260
  28.9 1.5 %collective-permute-start.2 = (bf16[32,3456]{1,0:T(8,128)(2,1)}, bf16[32,3456]{1,0:T(8,128)(2,1)S(1)}, u32[]{:S(2)}, u32[]{:S(2)}) collective-permute-start(bf16[32,3456]{1,0:T(8,128)(2,1)} %get-tuple-element.34), channel_id=1, source_target_pairs={{0,8},{8,16},{16,24},{24,0},{1,9},{9,17},{17,25},{25,1},{2,10},{10... | collective-permute-start | bytes 663560 | tf_op jit(solution)/shard_map/ppermute | solution.py:219
  30.4 2.7 %collective-permute-start.3 = (bf16[32,3456]{1,0:T(8,128)(2,1)}, bf16[32,3456]{1,0:T(8,128)(2,1)S(1)}, u32[]{:S(2)}, u32[]{:S(2)}) collective-permute-start(bf16[32,3456]{1,0:T(8,128)(2,1)} %get-tuple-element.35), channel_id=1, source_target_pairs={{0,16},{8,24},{16,0},{24,8},{1,17},{9,25},{17,1},{25,9},{2,18},{10... | collective-permute-start | bytes 663560 | tf_op jit(solution)/shard_map/ppermute | solution.py:219
  33.1 1.4 %collective-permute-start.4 = (bf16[32,3456]{1,0:T(8,128)(2,1)}, bf16[32,3456]{1,0:T(8,128)(2,1)S(1)}, u32[]{:S(2)}, u32[]{:S(2)}) collective-permute-start(bf16[32,3456]{1,0:T(8,128)(2,1)} %get-tuple-element.36), channel_id=1, source_target_pairs={{0,24},{8,0},{16,8},{24,16},{1,25},{9,1},{17,9},{25,17},{2,26},{10... | collective-permute-start | bytes 663560 | tf_op jit(solution)/shard_map/ppermute | solution.py:219
  34.5 0.0 collective-permute-start.5
  34.5 0.7 broadcast_in_dim.3.bias
  35.2 2.5 %collective-permute-done.2.refs_2_ = bf16[32,3456]{1,0:T(8,128)(2,1)S(1)} collective-permute-done((bf16[32,3456]{1,0:T(8,128)(2,1)}, bf16[32,3456]{1,0:T(8,128)(2,1)S(1)}, u32[]{:S(2)}, u32[]{:S(2)}) %collective-permute-start.2) | collective-permute-done | bytes 221216 | tf_op jit(solution)/shard_map/ppermute | solution.py:219
  37.7 0.7 copy-done.7
  38.4 4.5 %collective-permute-done.3.refs_3_ = bf16[32,3456]{1,0:T(8,128)(2,1)S(1)} collective-permute-done((bf16[32,3456]{1,0:T(8,128)(2,1)}, bf16[32,3456]{1,0:T(8,128)(2,1)S(1)}, u32[]{:S(2)}, u32[]{:S(2)}) %collective-permute-start.3) | collective-permute-done | bytes 221216 | tf_op jit(solution)/shard_map/ppermute | solution.py:219
  42.9 0.7 copy-done.9
  43.6 0.7 copy-done.11
  44.3 0.0 copy-start.2
  44.3 1.2 %copy-done.2 = bf16[128,3456]{1,0:T(8,128)(2,1)S(1)} copy-done((bf16[128,3456]{1,0:T(8,128)(2,1)S(1)}, bf16[128,3456]{1,0:T(8,128)(2,1)}, u32[]{:S(2)}) %copy-start.2) | copy-done | bytes 884760
  45.4 1.2 %copy-done.4 = bf16[128,3456]{1,0:T(8,128)(2,1)S(1)} copy-done((bf16[128,3456]{1,0:T(8,128)(2,1)S(1)}, bf16[128,3456]{1,0:T(8,128)(2,1)}, u32[]{:S(2)}) %copy-start.4) | copy-done | bytes 884760
  46.6 0.9 copy-done.13
  47.5 0.9 copy-done.14
  48.4 5.1 %tables.1 = bf16[16,26,8,128]{3,2,1,0:T(8,128)(2,1)S(1)} custom-call(s32[26]{0:T(128)S(1)} %copy-done.15, bf16[256,256]{1,0:T(8,128)(2,1)S(1)} %copy-done.13, bf16[256,256]{1,0:T(8,128)(2,1)S(1)} %copy-done.14, bf16[128,3456]{1,0:T(8,128)(2,1)S(1)} %copy-done.2, bf16[256,3456]{1,0:T(8,128)(2,1)S(1)} %copy-done.1, bf16[256,3456]{1,0:T(8,128)(2,1)S(1)} %copy-done, ...), custom_call_target="tpu_custom_call" | custom-call | flops 1358954496 | bytes 9437184 | tf_op jit(solution)/shard_map/tables/pallas_call | solution.py:35
  53.5 0.9 copy-done.5
  54.4 6.0 %all-to-all-start.2 = ((bf16[16,26,8,128]{3,2,1,0:T(8,128)(2,1)}), bf16[16,26,8,128]{3,2,1,0:T(8,128)(2,1)S(1)}, u32[]{:S(2)}, u32[]{:S(2)}) async-start(bf16[16,26,8,128]{3,2,1,0:T(8,128)(2,1)} %copy-done.5), calls=%async_computation.2 | async-start | bytes 1703936 | tf_op jit(solution)/shard_map/all_to_all | solution.py:288
  60.5 1.4 %cross_second.1 = (f32[8,3456]{1,0:T(8,128)S(1)}, bf16[8,3456]{1,0:T(8,128)(2,1)S(1)}, bf16[8,3456]{1,0:T(8,128)(2,1)S(1)}, bf16[8,3456]{1,0:T(8,128)(2,1)S(1)},...) custom-call(bf16[4,32,3456]{2,1,0:T(8,128)(2,1)} %all-to-all-done.1., ...), custom_call_target="tpu_custom_call" | custom-call | bytes 3145728 | tf_op jit(solution)/shard_map/cross_second/pallas_call | solution.py:35
  61.9 2.0 %collective-permute-start.6 = (bf16[8,3456]{1,0:T(8,128)(2,1)S(1)}, bf16[8,3456]{1,0:T(8,128)(2,1)S(1)}, u32[]{:S(2)}, u32[]{:S(2)}) collective-permute-start(bf16[8,3456]{1,0:T(8,128)(2,1)S(1)} %get-tuple-element.46), channel_id=1, source_target_pairs={{0,8},{8,16},{16,24},{24,0},{1,9},{9,17},{17,25},{25,1},{2,10},{10... | collective-permute-start | bytes 165896 | tf_op jit(solution)/shard_map/ppermute | solution.py:219
  63.9 2.7 %collective-permute-start.7 = (bf16[8,3456]{1,0:T(8,128)(2,1)S(1)}, bf16[8,3456]{1,0:T(8,128)(2,1)S(1)}, u32[]{:S(2)}, u32[]{:S(2)}) collective-permute-start(bf16[8,3456]{1,0:T(8,128)(2,1)S(1)} %get-tuple-element.47), channel_id=1, source_target_pairs={{0,16},{8,24},{16,0},{24,8},{1,17},{9,25},{17,1},{25,9},{2,18},{10... | collective-permute-start | bytes 165896 | tf_op jit(solution)/shard_map/ppermute | solution.py:219
  66.6 1.5 %collective-permute-start.8 = (bf16[8,3456]{1,0:T(8,128)(2,1)S(1)}, bf16[8,3456]{1,0:T(8,128)(2,1)S(1)}, u32[]{:S(2)}, u32[]{:S(2)}) collective-permute-start(bf16[8,3456]{1,0:T(8,128)(2,1)S(1)} %get-tuple-element.48), channel_id=1, source_target_pairs={{0,24},{8,0},{16,8},{24,16},{1,25},{9,1},{17,9},{25,17},{2,26},{10... | collective-permute-start | bytes 165896 | tf_op jit(solution)/shard_map/ppermute | solution.py:219
  68.0 1.5 %collective-permute-start.9 = (bf16[8,3456]{1,0:T(8,128)(2,1)S(1)}, bf16[8,3456]{1,0:T(8,128)(2,1)S(1)}, u32[]{:S(2)}, u32[]{:S(2)}) collective-permute-start(bf16[8,3456]{1,0:T(8,128)(2,1)S(1)} %get-tuple-element.50), channel_id=1, source_target_pairs={{0,64},{64,128},{128,192},{192,0},{1,65},{65,129},{129,193},{193,1... | collective-permute-start | bytes 165896 | tf_op jit(solution)/shard_map/ppermute | solution.py:219
  69.5 2.7 %collective-permute-start.10 = (bf16[8,3456]{1,0:T(8,128)(2,1)S(1)}, bf16[8,3456]{1,0:T(8,128)(2,1)S(1)}, u32[]{:S(2)}, u32[]{:S(2)}) collective-permute-start(bf16[8,3456]{1,0:T(8,128)(2,1)S(1)} %get-tuple-element.51), channel_id=1, source_target_pairs={{0,128},{64,192},{128,0},{192,64},{1,129},{65,193},{129,1},{193,65... | collective-permute-start | bytes 165896 | tf_op jit(solution)/shard_map/ppermute | solution.py:219
  72.2 1.2 %collective-permute-done.6.refs_1_ = bf16[8,3456]{1,0:T(8,128)(2,1)S(1)} collective-permute-done((bf16[8,3456]{1,0:T(8,128)(2,1)S(1)}, bf16[8,3456]{1,0:T(8,128)(2,1)S(1)}, u32[]{:S(2)}, u32[]{:S(2)}) %collective-permute-start.6) | collective-permute-done | bytes 55328 | tf_op jit(solution)/shard_map/ppermute | solution.py:219
  73.4 2.6 %collective-permute-start.11 = (bf16[8,3456]{1,0:T(8,128)(2,1)S(1)}, bf16[8,3456]{1,0:T(8,128)(2,1)S(1)}, u32[]{:S(2)}, u32[]{:S(2)}) collective-permute-start(bf16[8,3456]{1,0:T(8,128)(2,1)S(1)} %get-tuple-element.52), channel_id=1, source_target_pairs={{0,192},{64,0},{128,64},{192,128},{1,193},{65,1},{129,65},{193,129... | collective-permute-start | bytes 165896 | tf_op jit(solution)/shard_map/ppermute | solution.py:219
  76.0 0.8 route.1
  76.8 0.4 collective-permute-start.12
  77.3 2.6 %collective-permute-start.13 = (bf16[8,16,128]{2,1,0:T(8,128)(2,1)S(1)}, bf16[8,16,128]{2,1,0:T(8,128)(2,1)S(1)}, u32[]{:S(2)}, u32[]{:S(2)}) collective-permute-start(bf16[8,16,128]{2,1,0:T(8,128)(2,1)S(1)} %get-tuple-element.56), channel_id=1, source_target_pairs={{0,16},{8,24},{16,0},{24,8},{1,17},{9,25},{17,1},{25,9},{2,18},{10... | collective-permute-start | bytes 98312 | tf_op jit(solution)/shard_map/ppermute | solution.py:219
  79.9 1.2 %collective-permute-start.14 = (bf16[8,16,128]{2,1,0:T(8,128)(2,1)S(1)}, bf16[8,16,128]{2,1,0:T(8,128)(2,1)S(1)}, u32[]{:S(2)}, u32[]{:S(2)}) collective-permute-start(bf16[8,16,128]{2,1,0:T(8,128)(2,1)S(1)} %get-tuple-element.57), channel_id=1, source_target_pairs={{0,24},{8,0},{16,8},{24,16},{1,25},{9,1},{17,9},{25,17},{2,26},{10... | collective-permute-start | bytes 98312 | tf_op jit(solution)/shard_map/ppermute | solution.py:219
  81.0 1.0 %collective-permute-done.12.refs_9_ = bf16[8,16,128]{2,1,0:T(8,128)(2,1)S(1)} collective-permute-done((bf16[8,16,128]{2,1,0:T(8,128)(2,1)S(1)}, bf16[8,16,128]{2,1,0:T(8,128)(2,1)S(1)}, u32[]{:S(2)}, u32[]{:S(2)}) %collective-permute-start.12) | collective-permute-done | bytes 32800 | tf_op jit(solution)/shard_map/ppermute | solution.py:219
  82.1 0.7 collective-permute-done.13.refs_10_
  82.7 1.1 %collective-permute-done.14.refs_11_ = bf16[8,16,128]{2,1,0:T(8,128)(2,1)S(1)} collective-permute-done((bf16[8,16,128]{2,1,0:T(8,128)(2,1)S(1)}, bf16[8,16,128]{2,1,0:T(8,128)(2,1)S(1)}, u32[]{:S(2)}, u32[]{:S(2)}) %collective-permute-start.14) | collective-permute-done | bytes 32800 | tf_op jit(solution)/shard_map/ppermute | solution.py:219
  83.8 0.2 to_z.1
  84.0 15.5 %all_to_all.20.came = bf16[8,118,128]{2,1,0:T(8,128)(2,1)S(1)} all-to-all(bf16[8,118,128]{2,1,0:T(8,128)(2,1)S(1)} %to_z.1), channel_id=1, replica_groups=mesh['x'=4,'c'=2,'y'=4,'z'=8] {'z'}, dimensions={0} | all-to-all | bytes 483328 | tf_op jit(solution)/shard_map/all_to_all | solution.py:324
  99.5 0.7 last.1
  (33 shorter events, 0.1 us)
Async XLA Ops:
  0.6 13.6 %collective-permute-start = (bf16[128,3456]{1,0:T(8,128)(2,1)}, bf16[128,3456]{1,0:T(8,128)(2,1)S(1)}, u32[]{:S(2)}, u32[]{:S(2)}) collective-permute-start(bf16[128,3456]{1,0:T(8,128)(2,1)} %x.1), channel_id=1, source_target_pairs={{0,32},{32,0},{1,33},{33,1},{2,34},{34,2},{3,35},{35,3},{4,36},{36... | collective-permute-start | bytes 2654216 | tf_op jit(solution)/shard_map/ppermute | solution.py:227
  0.7 13.5 %collective-permute-start.1 = (bf16[128,3456]{1,0:T(8,128)(2,1)}, bf16[128,3456]{1,0:T(8,128)(2,1)S(1)}, u32[]{:S(2)}, u32[]{:S(2)}) collective-permute-start(bf16[128,3456]{1,0:T(8,128)(2,1)} %up.3), channel_id=1, source_target_pairs={{0,32},{32,0},{1,33},{33,1},{2,34},{34,2},{3,35},{35,3},{4,36},{36... | collective-permute-start | bytes 2654216 | tf_op jit(solution)/shard_map/ppermute | solution.py:228
  1.2 0.9 copy-start.16
  2.8 21.7 %all-to-all-start = ((s16[32,8,128]{2,1,0:T(8,128)(2,1)}), s16[32,8,128]{2,1,0:T(8,128)(2,1)}, u32[]{:S(2)}, u32[]{:S(2)}) async-start(s16[32,8,128]{2,1,0:T(8,128)(2,1)} %ids.2), calls=%async_computation | async-start | bytes 131072 | tf_op jit(solution)/shard_map/all_to_all | solution.py:231
  14.2 0.9 copy-start.17
  15.1 0.9 copy-start.3
  16.1 28.2 %copy-start.1 = (bf16[256,3456]{1,0:T(8,128)(2,1)S(1)}, bf16[256,3456]{1,0:T(8,128)(2,1)}, u32[]{:S(2)}) copy-start(bf16[256,3456]{1,0:T(8,128)(2,1)} %u.1) | copy-start | bytes 5308420
  24.4 19.8 %copy-start = (bf16[256,3456]{1,0:T(8,128)(2,1)S(1)}, bf16[256,3456]{1,0:T(8,128)(2,1)}, u32[]{:S(2)}) copy-start(bf16[256,3456]{1,0:T(8,128)(2,1)} %v.1) | copy-start | bytes 5308420
  24.4 19.8 %copy-start.15 = (s32[26]{0:T(128)S(1)}, s32[26]{0:T(128)}, u32[]{:S(2)}) copy-start(s32[26]{0:T(128)} %placement.3) | copy-start | bytes 316
  24.4 30.0 %all-to-all-start.1 = ((bf16[4,32,3456]{2,1,0:T(8,128)(2,1)}), bf16[4,32,3456]{2,1,0:T(8,128)(2,1)}, u32[]{:S(2)}, u32[]{:S(2)}) async-start(bf16[4,32,3456]{2,1,0:T(8,128)(2,1)} %get-tuple-element.31), calls=%async_computation.1 | async-start | bytes 1769472 | tf_op jit(solution)/shard_map/all_to_all | solution.py:260
  28.9 8.8 %collective-permute-start.2 = (bf16[32,3456]{1,0:T(8,128)(2,1)}, bf16[32,3456]{1,0:T(8,128)(2,1)S(1)}, u32[]{:S(2)}, u32[]{:S(2)}) collective-permute-start(bf16[32,3456]{1,0:T(8,128)(2,1)} %get-tuple-element.34), channel_id=1, source_target_pairs={{0,8},{8,16},{16,24},{24,0},{1,9},{9,17},{17,25},{25,1},{2,10},{10... | collective-permute-start | bytes 663560 | tf_op jit(solution)/shard_map/ppermute | solution.py:219
  30.4 12.5 %collective-permute-start.3 = (bf16[32,3456]{1,0:T(8,128)(2,1)}, bf16[32,3456]{1,0:T(8,128)(2,1)S(1)}, u32[]{:S(2)}, u32[]{:S(2)}) collective-permute-start(bf16[32,3456]{1,0:T(8,128)(2,1)} %get-tuple-element.35), channel_id=1, source_target_pairs={{0,16},{8,24},{16,0},{24,8},{1,17},{9,25},{17,1},{25,9},{2,18},{10... | collective-permute-start | bytes 663560 | tf_op jit(solution)/shard_map/ppermute | solution.py:219
  33.1 10.5 %collective-permute-start.4 = (bf16[32,3456]{1,0:T(8,128)(2,1)}, bf16[32,3456]{1,0:T(8,128)(2,1)S(1)}, u32[]{:S(2)}, u32[]{:S(2)}) collective-permute-start(bf16[32,3456]{1,0:T(8,128)(2,1)} %get-tuple-element.36), channel_id=1, source_target_pairs={{0,24},{8,0},{16,8},{24,16},{1,25},{9,1},{17,9},{25,17},{2,26},{10... | collective-permute-start | bytes 663560 | tf_op jit(solution)/shard_map/ppermute | solution.py:219
  34.5 9.7 %collective-permute-start.5 = (s16[32,8,128]{2,1,0:T(8,128)(2,1)}, s16[32,8,128]{2,1,0:T(8,128)(2,1)S(1)}, u32[]{:S(2)}, u32[]{:S(2)}) collective-permute-start(s16[32,8,128]{2,1,0:T(8,128)(2,1)} %all-to-all-done.ids), channel_id=1, source_target_pairs={{0,32},{32,0},{1,33},{33,1},{2,34},{34,2},{3,35},{35,3},{4,36},{36... | collective-permute-start | bytes 196616 | tf_op jit(solution)/shard_map/ppermute | solution.py:262
  37.7 0.7 copy-start.7
  42.9 0.7 copy-start.9
  43.6 0.7 copy-start.11
  44.3 1.2 %copy-start.2 = (bf16[128,3456]{1,0:T(8,128)(2,1)S(1)}, bf16[128,3456]{1,0:T(8,128)(2,1)}, u32[]{:S(2)}) copy-start(bf16[128,3456]{1,0:T(8,128)(2,1)} %up.3) | copy-start | bytes 2654212
  45.4 1.2 %copy-start.4 = (bf16[128,3456]{1,0:T(8,128)(2,1)S(1)}, bf16[128,3456]{1,0:T(8,128)(2,1)}, u32[]{:S(2)}) copy-start(bf16[128,3456]{1,0:T(8,128)(2,1)} %copy-done.3) | copy-start | bytes 2654212
  46.6 0.9 copy-start.13
  47.5 0.9 copy-start.14
  53.5 0.9 copy-start.5
  54.4 6.1 %copy-start.6 = (bf16[32,3456]{1,0:T(8,128)(2,1)S(1)}, bf16[32,3456]{1,0:T(8,128)(2,1)}, u32[]{:S(2)}) copy-start(bf16[32,3456]{1,0:T(8,128)(2,1)} %get-tuple-element.41.refs_1_) | copy-start | bytes 663556
  54.4 6.1 %copy-start.8 = (bf16[32,3456]{1,0:T(8,128)(2,1)S(1)}, bf16[32,3456]{1,0:T(8,128)(2,1)}, u32[]{:S(2)}) copy-start(bf16[32,3456]{1,0:T(8,128)(2,1)} %copy-done.7) | copy-start | bytes 663556
  54.4 6.1 %copy-start.10 = (bf16[32,3456]{1,0:T(8,128)(2,1)S(1)}, bf16[32,3456]{1,0:T(8,128)(2,1)}, u32[]{:S(2)}) copy-start(bf16[32,3456]{1,0:T(8,128)(2,1)} %copy-done.9) | copy-start | bytes 663556
  54.4 6.1 %copy-start.12 = (bf16[32,3456]{1,0:T(8,128)(2,1)S(1)}, bf16[32,3456]{1,0:T(8,128)(2,1)}, u32[]{:S(2)}) copy-start(bf16[32,3456]{1,0:T(8,128)(2,1)} %copy-done.11) | copy-start | bytes 663556
  54.4 21.6 %all-to-all-start.2 = ((bf16[16,26,8,128]{3,2,1,0:T(8,128)(2,1)}), bf16[16,26,8,128]{3,2,1,0:T(8,128)(2,1)S(1)}, u32[]{:S(2)}, u32[]{:S(2)}) async-start(bf16[16,26,8,128]{3,2,1,0:T(8,128)(2,1)} %copy-done.5), calls=%async_computation.2 | async-start | bytes 1703936 | tf_op jit(solution)/shard_map/all_to_all | solution.py:288
  61.9 11.5 %collective-permute-start.6 = (bf16[8,3456]{1,0:T(8,128)(2,1)S(1)}, bf16[8,3456]{1,0:T(8,128)(2,1)S(1)}, u32[]{:S(2)}, u32[]{:S(2)}) collective-permute-start(bf16[8,3456]{1,0:T(8,128)(2,1)S(1)} %get-tuple-element.46), channel_id=1, source_target_pairs={{0,8},{8,16},{16,24},{24,0},{1,9},{9,17},{17,25},{25,1},{2,10},{10... | collective-permute-start | bytes 165896 | tf_op jit(solution)/shard_map/ppermute | solution.py:219
  63.9 12.9 %collective-permute-start.7 = (bf16[8,3456]{1,0:T(8,128)(2,1)S(1)}, bf16[8,3456]{1,0:T(8,128)(2,1)S(1)}, u32[]{:S(2)}, u32[]{:S(2)}) collective-permute-start(bf16[8,3456]{1,0:T(8,128)(2,1)S(1)} %get-tuple-element.47), channel_id=1, source_target_pairs={{0,16},{8,24},{16,0},{24,8},{1,17},{9,25},{17,1},{25,9},{2,18},{10... | collective-permute-start | bytes 165896 | tf_op jit(solution)/shard_map/ppermute | solution.py:219
  66.6 10.7 %collective-permute-start.8 = (bf16[8,3456]{1,0:T(8,128)(2,1)S(1)}, bf16[8,3456]{1,0:T(8,128)(2,1)S(1)}, u32[]{:S(2)}, u32[]{:S(2)}) collective-permute-start(bf16[8,3456]{1,0:T(8,128)(2,1)S(1)} %get-tuple-element.48), channel_id=1, source_target_pairs={{0,24},{8,0},{16,8},{24,16},{1,25},{9,1},{17,9},{25,17},{2,26},{10... | collective-permute-start | bytes 165896 | tf_op jit(solution)/shard_map/ppermute | solution.py:219
  68.0 11.8 %collective-permute-start.9 = (bf16[8,3456]{1,0:T(8,128)(2,1)S(1)}, bf16[8,3456]{1,0:T(8,128)(2,1)S(1)}, u32[]{:S(2)}, u32[]{:S(2)}) collective-permute-start(bf16[8,3456]{1,0:T(8,128)(2,1)S(1)} %get-tuple-element.50), channel_id=1, source_target_pairs={{0,64},{64,128},{128,192},{192,0},{1,65},{65,129},{129,193},{193,1... | collective-permute-start | bytes 165896 | tf_op jit(solution)/shard_map/ppermute | solution.py:219
  69.5 11.5 %collective-permute-start.10 = (bf16[8,3456]{1,0:T(8,128)(2,1)S(1)}, bf16[8,3456]{1,0:T(8,128)(2,1)S(1)}, u32[]{:S(2)}, u32[]{:S(2)}) collective-permute-start(bf16[8,3456]{1,0:T(8,128)(2,1)S(1)} %get-tuple-element.51), channel_id=1, source_target_pairs={{0,128},{64,192},{128,0},{192,64},{1,129},{65,193},{129,1},{193,65... | collective-permute-start | bytes 165896 | tf_op jit(solution)/shard_map/ppermute | solution.py:219
  73.4 7.6 %collective-permute-start.11 = (bf16[8,3456]{1,0:T(8,128)(2,1)S(1)}, bf16[8,3456]{1,0:T(8,128)(2,1)S(1)}, u32[]{:S(2)}, u32[]{:S(2)}) collective-permute-start(bf16[8,3456]{1,0:T(8,128)(2,1)S(1)} %get-tuple-element.52), channel_id=1, source_target_pairs={{0,192},{64,0},{128,64},{192,128},{1,193},{65,1},{129,65},{193,129... | collective-permute-start | bytes 165896 | tf_op jit(solution)/shard_map/ppermute | solution.py:219
  76.8 5.2 %collective-permute-start.12 = (bf16[8,16,128]{2,1,0:T(8,128)(2,1)S(1)}, bf16[8,16,128]{2,1,0:T(8,128)(2,1)S(1)}, u32[]{:S(2)}, u32[]{:S(2)}) collective-permute-start(bf16[8,16,128]{2,1,0:T(8,128)(2,1)S(1)} %get-tuple-element.55), channel_id=1, source_target_pairs={{0,8},{8,16},{16,24},{24,0},{1,9},{9,17},{17,25},{25,1},{2,10},{10... | collective-permute-start | bytes 98312 | tf_op jit(solution)/shard_map/ppermute | solution.py:219
  77.3 5.4 %collective-permute-start.13 = (bf16[8,16,128]{2,1,0:T(8,128)(2,1)S(1)}, bf16[8,16,128]{2,1,0:T(8,128)(2,1)S(1)}, u32[]{:S(2)}, u32[]{:S(2)}) collective-permute-start(bf16[8,16,128]{2,1,0:T(8,128)(2,1)S(1)} %get-tuple-element.56), channel_id=1, source_target_pairs={{0,16},{8,24},{16,0},{24,8},{1,17},{9,25},{17,1},{25,9},{2,18},{10... | collective-permute-start | bytes 98312 | tf_op jit(solution)/shard_map/ppermute | solution.py:219
  79.9 3.9 %collective-permute-start.14 = (bf16[8,16,128]{2,1,0:T(8,128)(2,1)S(1)}, bf16[8,16,128]{2,1,0:T(8,128)(2,1)S(1)}, u32[]{:S(2)}, u32[]{:S(2)}) collective-permute-start(bf16[8,16,128]{2,1,0:T(8,128)(2,1)S(1)} %get-tuple-element.57), channel_id=1, source_target_pairs={{0,24},{8,0},{16,8},{24,16},{1,25},{9,1},{17,9},{25,17},{2,26},{10... | collective-permute-start | bytes 98312 | tf_op jit(solution)/shard_map/ppermute | solution.py:219

commit v6 on v4

--- a/solution.py
+++ b/solution.py
@@ -87,8 +87,8 @@
         for k in range(width // step):
             total = mm(left, right[:, k * step : (k + 1) * step])
             cols = slice(side * width + k * step, side * width + (k + 1) * step)
-            for i in range(NX * NY):
-                held[i, :, cols] = total[i * 8 : (i + 1) * 8].astype(BF)
+            for i in range(NX):
+                held[i, :, cols] = total[i * NJ : (i + 1) * NJ].astype(BF)
             copies.append(
                 pltpu.make_async_copy(
                     held.at[:, :, cols], out.at[:, :, cols], sems.at[len(copies)]
@@ -158,8 +158,19 @@
         refs[NY + d][...] = total[:, d * 8 : (d + 1) * 8].astype(refs[NY + d].dtype)
 
 
-def route_kernel(placement, *refs):
-    came, outs, (held, used, at) = refs[:NX], refs[NX : NX + NY], refs[NX + NY :]
+def cross_kernel(came, out, sums):
+    for k in range(came.shape[2] // EMB):
+        cols = slice(k * EMB, (k + 1) * EMB)
+        total = came[0, :, cols].astype(F32)
+        for i in range(1, NX):
+            total = total + came[i, :, cols].astype(F32)
+        sums[:, k] = total
+    for j in range(NJ):
+        out[j] = sums[j].astype(BF)
+
+
+def route_kernel(placement, cross, *refs):
+    came, out, (held, used, at) = refs[:NX], refs[NX], refs[NX + 1 :]
     for k in range(2 * NJ):
         at[k] = 0
 
@@ -169,38 +180,25 @@
     slots_of(placement, used, note)
     held[0] = jnp.zeros((8, EMB), F32)
     held[1:] = total_of(came)
-    for d in range(NY):
-        first = lax.rem(lax.axis_index("y") + d, NY) * NZ
-        for z in range(NZ):
-            slots = [held[at[2 * (first + z) + s]] for s in range(2)]
-            outs[d][z] = jnp.concatenate(slots, axis=0).astype(BF)
-
-
-def to_z_kernel(cross, *refs):
-    routed, out, sums = refs[:NY], refs[NY], refs[NY + 1]
-    for k in range(cross.shape[2] // EMB):
-        cols = slice(k * EMB, (k + 1) * EMB)
-        total = cross[0, :, cols].astype(F32)
-        for i in range(1, NX * NY):
-            total = total + cross[i, :, cols].astype(F32)
-        sums[:, k] = total
-    for z in range(NZ):
-        for d in range(NY):
-            out[z, d * 16 : (d + 1) * 16] = routed[d][z]
-        out[z, 64:] = sums[z].astype(BF)
+    for j in range(NJ):
+        slots = [held[at[2 * j + s]] for s in range(2)]
+        out[j, :16] = jnp.concatenate(slots, axis=0).astype(BF)
+        out[j, 16:] = cross[j]
 
 
 def last_kernel(came, cross, table):
     scale = 1.0 / math.sqrt(EMB * 256)
-    total = came[0].astype(F32)
-    for z in range(1, NZ):
-        total = total + came[z].astype(F32)
+    total = came[0, 16:].astype(F32)
+    for j in range(1, NJ):
+        total = total + came[j, 16:].astype(F32)
     for k in range(cross.shape[1] // EMB):
-        cross[:, k * EMB : (k + 1) * EMB] = total[64 + k : 65 + k] * scale
-    for d in range(NY):
-        start = pl.multiple_of(lax.rem(lax.axis_index("y") + NY - d, NY) * 8, 8)
+        cross[:, k * EMB : (k + 1) * EMB] = total[k : k + 1] * scale
+    for y in range(NY):
+        rows = came[y * NZ, :16].astype(F32)
+        for z in range(1, NZ):
+            rows = rows + came[y * NZ + z, :16].astype(F32)
         for s in range(2):
-            table[s, pl.ds(start, 8)] = total[d * 16 + s * 8 : d * 16 + s * 8 + 8]
+            table[s, y * 8 : (y + 1) * 8] = rows[s * 8 : (s + 1) * 8]
 
 
 def shift(chunks, axis):
@@ -223,7 +221,7 @@
     hid, hgr, cross = call(
         dense_kernel,
         "dense",
-        [((RANK, 2 * samples), BF)] * 2 + [((NX * NY, NZ, 2 * width), BF)],
+        [((RANK, 2 * samples), BF)] * 2 + [((NX, NJ, 2 * width), BF)],
         cross_input,
         px,
         upstream,
@@ -235,7 +233,7 @@
         scratch=[pltpu.VMEM((2 * samples, width), BF)] * 2
         + [pltpu.VMEM((RANK, width), BF)] * 2
         + [
-            pltpu.VMEM((NX * NY, NZ, 2 * width), BF),
+            pltpu.VMEM((NX, NJ, 2 * width), BF),
             pltpu.SemaphoreType.DMA((4,)),
             pltpu.SemaphoreType.DMA((6,)),
         ],
@@ -244,7 +242,7 @@
         size=6 << 20,
     )
     ids, cross = lax.optimization_barrier((ids, cross))
-    cross = lax.all_to_all(cross, ("x", "y"), 0, 0, tiled=True)
+    cross = lax.all_to_all(cross, "x", 0, 0, tiled=True)
     pids = lax.ppermute(ids, "c", swap)
 
     tables = call(
@@ -280,38 +278,37 @@
         size=1 << 20,
     )
     tables = shift(tables, "x")
-    routed = call(
+    (cross,) = call(
+        cross_kernel,
+        "cross_sum",
+        [((NJ, blocks, EMB), BF)],
+        cross,
+        specs=[VMEM],
+        scratch=[pltpu.VMEM((NJ, blocks, EMB), F32)],
+        size=3 << 20,
+    )
+    (routed,) = call(
         route_kernel,
         "route",
-        [((NZ, 16, EMB), BF)] * NY,
+        [((NJ, 16 + blocks, EMB), BF)],
         placement,
+        cross,
         *tables,
         scratch=[
             pltpu.VMEM((TABLES + 1, 8, EMB), F32),
             pltpu.SMEM((NJ,), I32),
             pltpu.SMEM((2 * NJ,), I32),
         ],
-        size=1 << 20,
-    )
-    routed = shift(routed, "y")
-    (both,) = call(
-        to_z_kernel,
-        "to_z",
-        [((NZ, 64 + blocks, EMB), BF)],
-        cross,
-        *routed,
-        specs=[VMEM] * (1 + NY),
-        scratch=[pltpu.VMEM((NZ, blocks, EMB), F32)],
-        size=3 << 20,
-    )
-    both = lax.all_to_all(both, "z", 0, 0, tiled=True)
+        size=2 << 20,
+    )
+    routed = lax.all_to_all(routed, ("y", "z"), 0, 0, tiled=True)
     return call(
         last_kernel,
         "last",
         [((1, 2 * width), F32), ((2, NJ, EMB), F32)],
-        both,
+        routed,
         specs=[VMEM],
-        size=300000,
+        size=1 << 20,
     )
 
 

time: 97 us -> 88.2 us (0.909)
  the two profiles are of different devices: /device:TPU:2 before, /device:TPU:32 now
where the time goes in v6:
time: 88.2 us; the launch traced here: 87.7 us
  starting transfers between devices  26.8 us (30%)
  blocking collectives  24.7 us (28%)
  Pallas kernels  14.3 us (16%)
  waiting for transfers between devices  13.4 us (15%)
  local copies, waits for them, and re-layouts  7.71 us (9%)
    all_to_all x1, blocking collectives, on_device(): routed = lax.all_to_all(routed, ('y', 'z'), 0, 0, tiled=True)  24.7 us
    pallas_call x7, Pallas kernels, call(): pl.pallas_call(kernel, out_shape=tuple((jax.ShapeDtypeStruct(shape, dtype...  14.3 us
    all_to_all x1, starting transfers between devices, on_device(): ids = lax.all_to_all(ids, ('y', 'z'), 0, 0, tiled=True)  11.4 us
    ppermute x6, waiting for transfers between devices, shift(): lax.ppermute(chunks[d], axis, [(i, (i + d) % n) for i in range(n)])  10.3 us
    ppermute x6, starting transfers between devices, shift(): lax.ppermute(chunks[d], axis, [(i, (i + d) % n) for i in range(n)])  10.1 us
    unnamed x28, local copies, waits for them, and re-layouts  6.98 us
    all_to_all x1, starting transfers between devices, on_device(): cross = lax.all_to_all(cross, 'x', 0, 0, tiled=True)  4.64 us
    all_to_all x1, waiting for transfers between devices, on_device(): ids = lax.all_to_all(ids, ('y', 'z'), 0, 0, tiled=True)  2.36 us
  transfers between devices with their start and end apart: 11, of which 5 were waited for; matrix products, arithmetic and copies ran while one was open for 1% of the time, Pallas kernels for 15%

profile of v6, /device:TPU:32, one launch (start us, length us, event | category | flops | bytes accessed | tf_op | source)
XLA Modules:
  0.0 87.7 jit_solution(8839752379847793039)
XLA Ops:
  0.6 0.0 copy-start.2
  0.6 0.0 copy-start.6
  0.7 0.1 collective-permute-start.1
  0.8 0.5 collective-permute-start
  1.3 0.9 %copy-done.13 = s32[2,4,4096]{2,1,0:T(4,128)S(1)} copy-done((s32[2,4,4096]{2,1,0:T(4,128)S(1)}, s32[2,4,4096]{2,1,0:T(4,128)}, u32[]{:S(2)}) %copy-start.13) | copy-done | bytes 131096
  2.2 0.0 copy-start.11
  2.2 0.6 copy-done.11
  2.8 11.4 %all-to-all-start = ((s16[32,8,128]{2,1,0:T(8,128)(2,1)}), s16[32,8,128]{2,1,0:T(8,128)(2,1)}, u32[]{:S(2)}, u32[]{:S(2)}) async-start(s16[32,8,128]{2,1,0:T(8,128)(2,1)} %copy-done.11), calls=%async_computation | async-start | bytes 131072 | tf_op jit(solution)/shard_map/all_to_all | solution.py:219
  14.2 0.0 collective-permute-done.1.pup
  14.2 0.0 copy-start.4
  14.2 0.0 collective-permute-done.px
  14.3 0.0 copy-done.2
  14.3 0.0 copy-done.6
  14.3 5.4 %dense.1 = (bf16[256,256]{1,0:T(8,128)(2,1)S(1)}, bf16[256,256]{1,0:T(8,128)(2,1)S(1)}, bf16[4,32,6912]{2,1,0:T(8,128)(2,1)}) custom-call(bf16[128,3456]{1,0:T(8,128)(2,1)S(1)} %copy-done.6, bf16[128,3456]{1,0:T(8,128)(2,1)S(1)} %collective-permute-done.px, bf16[128,3456]{1,0:T(8,128)(2,1)S(1)} %copy-done.2, ...), custom_call_target="tpu_custom_call" | custom-call | flops 1358954496 | bytes 6291456 | tf_op jit(solution)/shard_map/dense/pallas_call | solution.py:35
  19.7 0.0 copy-done.4
  19.7 0.0 copy-start.7
  19.7 0.6 copy-done.7
  20.4 0.6 copy-done.9
  21.0 2.4 %all-to-all-done.ids = s16[32,8,128]{2,1,0:T(8,128)(2,1)} async-done(((s16[32,8,128]{2,1,0:T(8,128)(2,1)}), s16[32,8,128]{2,1,0:T(8,128)(2,1)}, u32[]{:S(2)}, u32[]{:S(2)}) %all-to-all-start) | async-done | bytes 65568 | tf_op jit(solution)/shard_map/all_to_all | solution.py:219
  23.4 4.6 %all-to-all-start.1 = ((bf16[4,32,6912]{2,1,0:T(8,128)(2,1)}), bf16[4,32,6912]{2,1,0:T(8,128)(2,1)}, u32[]{:S(2)}, u32[]{:S(2)}) async-start(bf16[4,32,6912]{2,1,0:T(8,128)(2,1)} %get-tuple-element.16), calls=%async_computation.1 | async-start | bytes 3538944 | tf_op jit(solution)/shard_map/all_to_all | solution.py:245
  28.1 0.1 collective-permute-start.2
  28.2 0.7 broadcast_in_dim.3.bias
  28.9 0.7 collective-permute-done.2.pids
  29.6 0.0 copy-done
  29.6 0.0 copy-start.3
  29.6 1.2 %copy-done.3 = bf16[128,3456]{1,0:T(8,128)(2,1)S(1)} copy-done((bf16[128,3456]{1,0:T(8,128)(2,1)S(1)}, bf16[128,3456]{1,0:T(8,128)(2,1)}, u32[]{:S(2)}) %copy-start.3) | copy-done | bytes 884760
  30.8 1.2 %copy-done.5 = bf16[128,3456]{1,0:T(8,128)(2,1)S(1)} copy-done((bf16[128,3456]{1,0:T(8,128)(2,1)S(1)}, bf16[128,3456]{1,0:T(8,128)(2,1)}, u32[]{:S(2)}) %copy-start.5) | copy-done | bytes 884760
  32.0 0.9 %copy-done.8 = bf16[256,256]{1,0:T(8,128)(2,1)S(1)} copy-done((bf16[256,256]{1,0:T(8,128)(2,1)S(1)}, bf16[256,256]{1,0:T(8,128)(2,1)}, u32[]{:S(2)}) %copy-start.8) | copy-done | bytes 131096
  32.9 0.9 %copy-done.10 = bf16[256,256]{1,0:T(8,128)(2,1)S(1)} copy-done((bf16[256,256]{1,0:T(8,128)(2,1)S(1)}, bf16[256,256]{1,0:T(8,128)(2,1)}, u32[]{:S(2)}) %copy-start.10) | copy-done | bytes 131096
  33.8 5.1 %tables.1 = (f32[26,32,128]{2,1,0:T(8,128)S(1)}, bf16[26,32,128]{2,1,0:T(8,128)(2,1)S(1)}, bf16[26,32,128]{2,1,0:T(8,128)(2,1)S(1)}, bf16[26,32,128]{2,1,0:T(8,128)(2,1)S(1)}) custom-call(s32[26]{0:T(128)S(1)} %copy-done.12, bf16[256,256]{1,0:T(8,128)(2,1)S(1)} %copy-done.8, bf16[256,256]{1,0:T(8,128)(2,1)S(1)} %copy-done.10, ...), custom_call_target="tpu_custom_call" | custom-call | flops 1358954496 | bytes 9437184 | tf_op jit(solution)/shard_map/tables/pallas_call | solution.py:35
  38.9 0.7 collective-permute-start.3
  39.5 2.0 %collective-permute-start.4 = (bf16[26,32,128]{2,1,0:T(8,128)(2,1)S(1)}, bf16[26,32,128]{2,1,0:T(8,128)(2,1)S(1)}, u32[]{:S(2)}, u32[]{:S(2)}) collective-permute-start(bf16[26,32,128]{2,1,0:T(8,128)(2,1)S(1)} %get-tuple-element.22), channel_id=1, source_target_pairs={{0,16},{8,24},{16,0},{24,8},{1,17},{9,25},{17,1},{25,9},{2,18},{10... | collective-permute-start | bytes 638984 | tf_op jit(solution)/shard_map/ppermute | solution.py:207
  41.6 1.3 %collective-permute-start.5 = (bf16[26,32,128]{2,1,0:T(8,128)(2,1)S(1)}, bf16[26,32,128]{2,1,0:T(8,128)(2,1)S(1)}, u32[]{:S(2)}, u32[]{:S(2)}) collective-permute-start(bf16[26,32,128]{2,1,0:T(8,128)(2,1)S(1)} %get-tuple-element.23), channel_id=1, source_target_pairs={{0,24},{8,0},{16,8},{24,16},{1,25},{9,1},{17,9},{25,17},{2,26},{10... | collective-permute-start | bytes 638984 | tf_op jit(solution)/shard_map/ppermute | solution.py:207
  42.9 9.2 %collective-permute-done.3.refs_1_ = bf16[26,32,128]{2,1,0:T(8,128)(2,1)S(1)} collective-permute-done((bf16[26,32,128]{2,1,0:T(8,128)(2,1)S(1)}, bf16[26,32,128]{2,1,0:T(8,128)(2,1)S(1)}, u32[]{:S(2)}, u32[]{:S(2)}) %collective-permute-start.3) | collective-permute-done | bytes 213024 | tf_op jit(solution)/shard_map/ppermute | solution.py:207
  52.0 0.0 collective-permute-done.4.refs_2_
  52.0 0.6 collective-permute-done.5.refs_3_
  52.6 0.1 table_second.1
  52.8 2.0 %collective-permute-start.6 = (bf16[26,8,128]{2,1,0:T(8,128)(2,1)S(1)}, bf16[26,8,128]{2,1,0:T(8,128)(2,1)S(1)}, u32[]{:S(2)}, u32[]{:S(2)}) collective-permute-start(bf16[26,8,128]{2,1,0:T(8,128)(2,1)S(1)} %get-tuple-element.25), channel_id=1, source_target_pairs={{0,64},{64,128},{128,192},{192,0},{1,65},{65,129},{129,193},{193,1... | collective-permute-start | bytes 159752 | tf_op jit(solution)/shard_map/ppermute | solution.py:207
  54.7 2.7 %collective-permute-start.7 = (bf16[26,8,128]{2,1,0:T(8,128)(2,1)S(1)}, bf16[26,8,128]{2,1,0:T(8,128)(2,1)S(1)}, u32[]{:S(2)}, u32[]{:S(2)}) collective-permute-start(bf16[26,8,128]{2,1,0:T(8,128)(2,1)S(1)} %get-tuple-element.26), channel_id=1, source_target_pairs={{0,128},{64,192},{128,0},{192,64},{1,129},{65,193},{129,1},{193,65... | collective-permute-start | bytes 159752 | tf_op jit(solution)/shard_map/ppermute | solution.py:207
  57.4 1.5 %collective-permute-start.8 = (bf16[26,8,128]{2,1,0:T(8,128)(2,1)S(1)}, bf16[26,8,128]{2,1,0:T(8,128)(2,1)S(1)}, u32[]{:S(2)}, u32[]{:S(2)}) collective-permute-start(bf16[26,8,128]{2,1,0:T(8,128)(2,1)S(1)} %get-tuple-element.27), channel_id=1, source_target_pairs={{0,192},{64,0},{128,64},{192,128},{1,193},{65,1},{129,65},{193,129... | collective-permute-start | bytes 159752 | tf_op jit(solution)/shard_map/ppermute | solution.py:207
  58.9 0.0 all-to-all-done.1.came
  58.9 2.1 %cross_sum.1.cross = bf16[32,54,128]{2,1,0:T(8,128)(2,1)S(1)} custom-call(bf16[4,32,6912]{2,1,0:T(8,128)(2,1)} %all-to-all-done.1.came), custom_call_target="tpu_custom_call" | custom-call | bytes 3145728 | tf_op jit(solution)/shard_map/cross_sum/pallas_call | solution.py:35
  61.0 0.0 collective-permute-done.6.refs_1_
  61.0 0.0 collective-permute-done.7.refs_2_
  61.0 0.5 collective-permute-done.8.refs_3_
  61.5 0.8 route.1
  62.3 24.7 %all_to_all.15.came = bf16[32,70,128]{2,1,0:T(8,128)(2,1)S(1)} all-to-all(bf16[32,70,128]{2,1,0:T(8,128)(2,1)S(1)} %route.1), channel_id=1, replica_groups=mesh['x'=4,'c'=2,'y'=4,'z'=8] {'y','z'}, dimensions={0} | all-to-all | bytes 1146880 | tf_op jit(solution)/shard_map/all_to_all | solution.py:304
  87.0 0.7 last.1
  (11 shorter events, 0.0 us)
Async XLA Ops:
  0.6 13.6 %copy-start.2 = (bf16[128,3456]{1,0:T(8,128)(2,1)S(1)}, bf16[128,3456]{1,0:T(8,128)(2,1)}, u32[]{:S(2)}) copy-start(bf16[128,3456]{1,0:T(8,128)(2,1)} %up.3) | copy-start | bytes 2654212
  0.6 13.6 %copy-start.6 = (bf16[128,3456]{1,0:T(8,128)(2,1)S(1)}, bf16[128,3456]{1,0:T(8,128)(2,1)}, u32[]{:S(2)}) copy-start(bf16[128,3456]{1,0:T(8,128)(2,1)} %x.1) | copy-start | bytes 2654212
  0.7 13.6 %collective-permute-start.1 = (bf16[128,3456]{1,0:T(8,128)(2,1)}, bf16[128,3456]{1,0:T(8,128)(2,1)S(1)}, u32[]{:S(2)}, u32[]{:S(2)}) collective-permute-start(bf16[128,3456]{1,0:T(8,128)(2,1)} %up.3), channel_id=1, source_target_pairs={{0,32},{32,0},{1,33},{33,1},{2,34},{34,2},{3,35},{35,3},{4,36},{36... | collective-permute-start | bytes 2654216 | tf_op jit(solution)/shard_map/ppermute | solution.py:216
  0.8 13.5 %collective-permute-start = (bf16[128,3456]{1,0:T(8,128)(2,1)}, bf16[128,3456]{1,0:T(8,128)(2,1)S(1)}, u32[]{:S(2)}, u32[]{:S(2)}) collective-permute-start(bf16[128,3456]{1,0:T(8,128)(2,1)} %x.1), channel_id=1, source_target_pairs={{0,32},{32,0},{1,33},{33,1},{2,34},{34,2},{3,35},{35,3},{4,36},{36... | collective-permute-start | bytes 2654216 | tf_op jit(solution)/shard_map/ppermute | solution.py:215
  1.2 0.9 %copy-start.13 = (s32[2,4,4096]{2,1,0:T(4,128)S(1)}, s32[2,4,4096]{2,1,0:T(4,128)}, u32[]{:S(2)}) copy-start(s32[2,4,4096]{2,1,0:T(4,128)} %ids.3) | copy-start | bytes 393220
  2.2 0.6 copy-start.11
  2.8 20.6 %all-to-all-start = ((s16[32,8,128]{2,1,0:T(8,128)(2,1)}), s16[32,8,128]{2,1,0:T(8,128)(2,1)}, u32[]{:S(2)}, u32[]{:S(2)}) async-start(s16[32,8,128]{2,1,0:T(8,128)(2,1)} %copy-done.11), calls=%async_computation | async-start | bytes 131072 | tf_op jit(solution)/shard_map/all_to_all | solution.py:219
  14.2 5.5 %copy-start.4 = (bf16[128,3456]{1,0:T(8,128)(2,1)}, bf16[128,3456]{1,0:T(8,128)(2,1)S(1)}, u32[]{:S(2)}) copy-start(bf16[128,3456]{1,0:T(8,128)(2,1)S(1)} %collective-permute-done.1.pup) | copy-start | bytes 2654212
  19.7 0.7 copy-start.7
  20.4 0.7 copy-start.9
  23.4 6.2 %copy-start = (bf16[256,3456]{1,0:T(8,128)(2,1)S(1)}, bf16[256,3456]{1,0:T(8,128)(2,1)}, u32[]{:S(2)}) copy-start(bf16[256,3456]{1,0:T(8,128)(2,1)} %v.1) | copy-start | bytes 5308420
  23.4 6.2 %copy-start.1 = (bf16[256,3456]{1,0:T(8,128)(2,1)S(1)}, bf16[256,3456]{1,0:T(8,128)(2,1)}, u32[]{:S(2)}) copy-start(bf16[256,3456]{1,0:T(8,128)(2,1)} %u.1) | copy-start | bytes 5308420
  23.4 6.2 %copy-start.12 = (s32[26]{0:T(128)S(1)}, s32[26]{0:T(128)}, u32[]{:S(2)}) copy-start(s32[26]{0:T(128)} %placement.3) | copy-start | bytes 316
  23.4 35.5 %all-to-all-start.1 = ((bf16[4,32,6912]{2,1,0:T(8,128)(2,1)}), bf16[4,32,6912]{2,1,0:T(8,128)(2,1)}, u32[]{:S(2)}, u32[]{:S(2)}) async-start(bf16[4,32,6912]{2,1,0:T(8,128)(2,1)} %get-tuple-element.16), calls=%async_computation.1 | async-start | bytes 3538944 | tf_op jit(solution)/shard_map/all_to_all | solution.py:245
  28.1 1.6 %collective-permute-start.2 = (s16[32,8,128]{2,1,0:T(8,128)(2,1)}, s16[32,8,128]{2,1,0:T(8,128)(2,1)S(1)}, u32[]{:S(2)}, u32[]{:S(2)}) collective-permute-start(s16[32,8,128]{2,1,0:T(8,128)(2,1)} %all-to-all-done.ids), channel_id=1, source_target_pairs={{0,32},{32,0},{1,33},{33,1},{2,34},{34,2},{3,35},{35,3},{4,36},{36... | collective-permute-start | bytes 196616 | tf_op jit(solution)/shard_map/ppermute | solution.py:246
  29.6 1.2 %copy-start.3 = (bf16[128,3456]{1,0:T(8,128)(2,1)S(1)}, bf16[128,3456]{1,0:T(8,128)(2,1)}, u32[]{:S(2)}) copy-start(bf16[128,3456]{1,0:T(8,128)(2,1)} %up.3) | copy-start | bytes 2654212
  30.8 1.2 %copy-start.5 = (bf16[128,3456]{1,0:T(8,128)(2,1)S(1)}, bf16[128,3456]{1,0:T(8,128)(2,1)}, u32[]{:S(2)}) copy-start(bf16[128,3456]{1,0:T(8,128)(2,1)} %copy-done.4) | copy-start | bytes 2654212
  32.0 0.9 %copy-start.8 = (bf16[256,256]{1,0:T(8,128)(2,1)S(1)}, bf16[256,256]{1,0:T(8,128)(2,1)}, u32[]{:S(2)}) copy-start(bf16[256,256]{1,0:T(8,128)(2,1)} %copy-done.7) | copy-start | bytes 393220
  32.9 0.9 %copy-start.10 = (bf16[256,256]{1,0:T(8,128)(2,1)S(1)}, bf16[256,256]{1,0:T(8,128)(2,1)}, u32[]{:S(2)}) copy-start(bf16[256,256]{1,0:T(8,128)(2,1)} %copy-done.9) | copy-start | bytes 393220
  38.9 13.2 %collective-permute-start.3 = (bf16[26,32,128]{2,1,0:T(8,128)(2,1)S(1)}, bf16[26,32,128]{2,1,0:T(8,128)(2,1)S(1)}, u32[]{:S(2)}, u32[]{:S(2)}) collective-permute-start(bf16[26,32,128]{2,1,0:T(8,128)(2,1)S(1)} %get-tuple-element.21), channel_id=1, source_target_pairs={{0,8},{8,16},{16,24},{24,0},{1,9},{9,17},{17,25},{25,1},{2,10},{10... | collective-permute-start | bytes 638984 | tf_op jit(solution)/shard_map/ppermute | solution.py:207
  39.5 12.5 %collective-permute-start.4 = (bf16[26,32,128]{2,1,0:T(8,128)(2,1)S(1)}, bf16[26,32,128]{2,1,0:T(8,128)(2,1)S(1)}, u32[]{:S(2)}, u32[]{:S(2)}) collective-permute-start(bf16[26,32,128]{2,1,0:T(8,128)(2,1)S(1)} %get-tuple-element.22), channel_id=1, source_target_pairs={{0,16},{8,24},{16,0},{24,8},{1,17},{9,25},{17,1},{25,9},{2,18},{10... | collective-permute-start | bytes 638984 | tf_op jit(solution)/shard_map/ppermute | solution.py:207
  41.6 11.1 %collective-permute-start.5 = (bf16[26,32,128]{2,1,0:T(8,128)(2,1)S(1)}, bf16[26,32,128]{2,1,0:T(8,128)(2,1)S(1)}, u32[]{:S(2)}, u32[]{:S(2)}) collective-permute-start(bf16[26,32,128]{2,1,0:T(8,128)(2,1)S(1)} %get-tuple-element.23), channel_id=1, source_target_pairs={{0,24},{8,0},{16,8},{24,16},{1,25},{9,1},{17,9},{25,17},{2,26},{10... | collective-permute-start | bytes 638984 | tf_op jit(solution)/shard_map/ppermute | solution.py:207
  52.8 8.2 %collective-permute-start.6 = (bf16[26,8,128]{2,1,0:T(8,128)(2,1)S(1)}, bf16[26,8,128]{2,1,0:T(8,128)(2,1)S(1)}, u32[]{:S(2)}, u32[]{:S(2)}) collective-permute-start(bf16[26,8,128]{2,1,0:T(8,128)(2,1)S(1)} %get-tuple-element.25), channel_id=1, source_target_pairs={{0,64},{64,128},{128,192},{192,0},{1,65},{65,129},{129,193},{193,1... | collective-permute-start | bytes 159752 | tf_op jit(solution)/shard_map/ppermute | solution.py:207
  54.7 6.3 %collective-permute-start.7 = (bf16[26,8,128]{2,1,0:T(8,128)(2,1)S(1)}, bf16[26,8,128]{2,1,0:T(8,128)(2,1)S(1)}, u32[]{:S(2)}, u32[]{:S(2)}) collective-permute-start(bf16[26,8,128]{2,1,0:T(8,128)(2,1)S(1)} %get-tuple-element.26), channel_id=1, source_target_pairs={{0,128},{64,192},{128,0},{192,64},{1,129},{65,193},{129,1},{193,65... | collective-permute-start | bytes 159752 | tf_op jit(solution)/shard_map/ppermute | solution.py:207
  57.4 4.1 %collective-permute-start.8 = (bf16[26,8,128]{2,1,0:T(8,128)(2,1)S(1)}, bf16[26,8,128]{2,1,0:T(8,128)(2,1)S(1)}, u32[]{:S(2)}, u32[]{:S(2)}) collective-permute-start(bf16[26,8,128]{2,1,0:T(8,128)(2,1)S(1)} %get-tuple-element.27), channel_id=1, source_target_pairs={{0,192},{64,0},{128,64},{192,128},{1,193},{65,1},{129,65},{193,129... | collective-permute-start | bytes 159752 | tf_op jit(solution)/shard_map/ppermute | solution.py:207

commit v7 on v6

--- a/solution.py
+++ b/solution.py
@@ -58,7 +58,7 @@
     return jnp.concatenate(picks, axis=0)
 
 
-def dense_kernel(x, px, up, pup, v_in, u_in, hid, hgr, out, both, prod, v, u, held, in_sems, sems):
+def dense_kernel(x, px, up, pup, v_in, u_in, bias, out, pooled, both, prod, v, u, held, held_p, in_sems, sems):
     n, width = x.shape
     core = lax.axis_index("c")
     loads = []
@@ -75,12 +75,12 @@
     prod[n:] = (px[...].astype(F32) * pup[...].astype(F32)).astype(BF)
     loads[0].wait()
     loads[1].wait()
-    hid[...] = nt(v[...], both[...]).astype(BF)
+    hid = nt(v[...], both[...]).astype(BF)
     loads[2].wait()
     loads[3].wait()
-    hgr[...] = nt(u[...], prod[...]).astype(BF)
-    hid_own = own_rows(hid[...].astype(F32), core).astype(BF)
-    hgr_own = own_rows(hgr[...].astype(F32), core).astype(BF)
+    hgr = nt(u[...], prod[...]).astype(BF)
+    hid_own = own_rows(hid.astype(F32), core).astype(BF)
+    hgr_own = own_rows(hgr.astype(F32), core).astype(BF)
     step = 1152
     copies = []
     for side, (left, right) in enumerate(((hid_own, prod), (hgr_own, both))):
@@ -95,6 +95,16 @@
                 )
             )
             copies[-1].start()
+    hid_s = hid.astype(F32).T.astype(BF)
+    hgr_s = hgr.astype(F32).T.astype(BF)
+    for pair in range(TABLES // 2):
+        cols = slice(EMB + pair * 256, EMB + pair * 256 + 256)
+        mixed = mm(hid_s, u[:, cols]) + bias[cols].reshape(1, 256)
+        back = mm(hgr_s, v[:, cols])
+        up_float = jnp.concatenate([up[:, cols], pup[:, cols]], axis=0).astype(F32)
+        held_p[:, pair * 256 : pair * 256 + 256] = (up_float * (1.0 + mixed) + back).astype(BF)
+    copies.append(pltpu.make_async_copy(held_p, pooled, sems.at[len(copies)]))
+    copies[-1].start()
     for copy in copies:
         copy.wait()
 
@@ -109,9 +119,9 @@
         visit(table, owner, slot)
 
 
-def table_kernel(placement, hid, hgr, up, u, v, pup, bias, ids, pids, *refs):
+def table_kernel(placement, pooled, ids, pids, *refs):
     outs, (state, counts, used) = refs[:4], refs[4:]
-    n = up.shape[0]
+    n = ids.shape[2]
     for p in range(NJ):
         state[p, :8] = ids[p].astype(I32)
         state[p, 8:] = pids[p].astype(I32)
@@ -130,19 +140,10 @@
             counts[table, :, half * n : (half + 1) * n] = count.astype(BF)
 
     slots_of(placement, used, count_rows)
-    hid_s = hid[...].astype(F32).T.astype(BF)
-    hgr_s = hgr[...].astype(F32).T.astype(BF)
-    for pair in range(TABLES // 2):
-        cols = slice(EMB + pair * 256, EMB + pair * 256 + 256)
-        mixed = mm(hid_s, u[:, cols]) + bias[:, cols]
-        back = mm(hgr_s, v[:, cols])
-        up_float = jnp.concatenate([up[:, cols], pup[:, cols]], axis=0).astype(F32)
-        pooled = (up_float * (1.0 + mixed) + back).astype(BF)
-        for which in range(2):
-            table = 2 * pair + which
-            total = mm(counts[table], pooled[:, which * EMB : (which + 1) * EMB])
-            for d in range(NY):
-                outs[d][table] = total[d * 32 : (d + 1) * 32].astype(outs[d].dtype)
+    for table in range(TABLES):
+        total = mm(counts[table], pooled[:, table * EMB : (table + 1) * EMB])
+        for d in range(NY):
+            outs[d][table] = total[d * 32 : (d + 1) * 32].astype(outs[d].dtype)
 
 
 def total_of(refs):
@@ -218,24 +219,26 @@
     (ids,) = call(ids_kernel, "ids", [((NJ, 8, EMB), I16)], owned_ids, specs=[VMEM], flops=40 << 30, size=60 << 20, vmem=4 << 20)
     ids = lax.all_to_all(ids, ("y", "z"), 0, 0, tiled=True)
 
-    hid, hgr, cross = call(
+    cross, pooled = call(
         dense_kernel,
         "dense",
-        [((RANK, 2 * samples), BF)] * 2 + [((NX, NJ, 2 * width), BF)],
+        [((NX, NJ, 2 * width), BF), ((2 * samples, TABLES * EMB), BF)],
         cross_input,
         px,
         upstream,
         pup,
         v_weight,
         u_weight,
-        specs=[VMEM] * 4 + [HBM] * 2,
-        out_specs=[VMEM] * 2 + [HBM],
+        bias,
+        specs=[VMEM] * 4 + [HBM] * 2 + [VMEM],
+        out_specs=[HBM] * 2,
         scratch=[pltpu.VMEM((2 * samples, width), BF)] * 2
         + [pltpu.VMEM((RANK, width), BF)] * 2
         + [
             pltpu.VMEM((NX, NJ, 2 * width), BF),
+            pltpu.VMEM((2 * samples, TABLES * EMB), BF),
             pltpu.SemaphoreType.DMA((4,)),
-            pltpu.SemaphoreType.DMA((6,)),
+            pltpu.SemaphoreType.DMA((7,)),
         ],
         vmem=50 << 20,
         flops=6 * 256 * 256 * width,
@@ -250,13 +253,7 @@
         "tables",
         [((TABLES, 32, EMB), F32)] + [((TABLES, 32, EMB), BF)] * 3,
         placement,
-        hid,
-        hgr,
-        upstream,
-        u_weight,
-        v_weight,
-        pup,
-        bias[None],
+        pooled,
         ids,
         pids,
         scratch=[

time: 88.2 us -> 82.4 us (0.934)
  local copies, waits for them, and re-layouts: 7.71 us -> 2.99 us
  Pallas kernels: 14.3 us -> 11.5 us
  waiting for transfers between devices: 13.4 us -> 15.9 us
    unnamed x28 -> x14, local copies, waits for them, and re-layouts: 6.98 us -> 2.99 us
    pallas_call x7, Pallas kernels: 14.3 us -> 11.5 us  [call(): pl.pallas_call(kernel, out_shape=tuple((jax.ShapeDtypeStruct(shape, dtype...]
    ppermute x6, waiting for transfers between devices: 10.3 us -> 11.8 us  [shift(): lax.ppermute(chunks[d], axis, [(i, (i + d) % n) for i in range(n)])]
  transfers between devices with their start and end apart: 11 -> 11, of which waited for: 5 -> 6; matrix products, arithmetic and copies ran while one was open for 1% -> 0% of each run, Pallas kernels for 15% -> 12%
where the time goes in v7:
time: 82.4 us; the launch traced here: 82 us
  starting transfers between devices  26.7 us (32%)
  blocking collectives  24.2 us (29%)
  waiting for transfers between devices  15.9 us (19%)
  Pallas kernels  11.5 us (14%)
  local copies, waits for them, and re-layouts  2.99 us (4%)
    all_to_all x1, blocking collectives, on_device(): routed = lax.all_to_all(routed, ('y', 'z'), 0, 0, tiled=True)  24.2 us
    ppermute x6, waiting for transfers between devices, shift(): lax.ppermute(chunks[d], axis, [(i, (i + d) % n) for i in range(n)])  11.8 us
    pallas_call x7, Pallas kernels, call(): pl.pallas_call(kernel, out_shape=tuple((jax.ShapeDtypeStruct(shape, dtype...  11.5 us
    all_to_all x1, starting transfers between devices, on_device(): ids = lax.all_to_all(ids, ('y', 'z'), 0, 0, tiled=True)  11.4 us
    ppermute x6, starting transfers between devices, shift(): lax.ppermute(chunks[d], axis, [(i, (i + d) % n) for i in range(n)])  10.2 us
    all_to_all x1, starting transfers between devices, on_device(): cross = lax.all_to_all(cross, 'x', 0, 0, tiled=True)  4.42 us
    unnamed x14, local copies, waits for them, and re-layouts  2.99 us
    all_to_all x1, waiting for transfers between devices, on_device(): ids = lax.all_to_all(ids, ('y', 'z'), 0, 0, tiled=True)  2.68 us
  transfers between devices with their start and end apart: 11, of which 6 were waited for; matrix products, arithmetic and copies ran while one was open for 0% of the time, Pallas kernels for 12%

profile of v7, /device:TPU:32, one launch (start us, length us, event | category | flops | bytes accessed | tf_op | source)
XLA Modules:
  0.0 82.0 jit_solution(17339665505856283462)
XLA Ops:
  0.6 0.0 copy-start
  0.6 0.0 copy-start.1
  0.7 0.0 copy-start.3
  0.7 0.1 collective-permute-start
  0.8 0.5 collective-permute-start.1
  1.3 0.0 copy-start.6
  1.3 0.9 %copy-done.6 = s32[2,4,4096]{2,1,0:T(4,128)S(1)} copy-done((s32[2,4,4096]{2,1,0:T(4,128)S(1)}, s32[2,4,4096]{2,1,0:T(4,128)}, u32[]{:S(2)}) %copy-start.6) | copy-done | bytes 131096
  2.2 0.0 copy-start.2
  2.2 0.6 copy-done.2
  2.8 11.4 %all-to-all-start = ((s16[32,8,128]{2,1,0:T(8,128)(2,1)}), s16[32,8,128]{2,1,0:T(8,128)(2,1)}, u32[]{:S(2)}, u32[]{:S(2)}) async-start(s16[32,8,128]{2,1,0:T(8,128)(2,1)} %copy-done.2), calls=%async_computation | async-start | bytes 131072 | tf_op jit(solution)/shard_map/all_to_all | solution.py:220
  14.2 0.0 collective-permute-done.px
  14.2 0.0 collective-permute-done.1.pup
  14.3 0.0 copy-done
  14.3 0.0 copy-done.1
  14.3 0.0 copy-done.3
  14.3 6.4 %dense.1 = (bf16[4,32,6912]{2,1,0:T(8,128)(2,1)}, bf16[256,3328]{1,0:T(8,128)(2,1)}) custom-call(bf16[128,3456]{1,0:T(8,128)(2,1)S(1)} %copy-done, bf16[128,3456]{1,0:T(8,128)(2,1)S(1)} %collective-permute-done.px, bf16[128,3456]{1,0:T(8,128)(2,1)S(1)} %copy-done.1, bf16[128,3456]{1,0:T(8,128)(2,1)S(1)} %collective-permute-done.1.pup, ...), custom_call_target="tpu_custom_call" | custom-call | flops 1358954496 | bytes 6291456 | tf_op jit(solution)/shard_map/dense/pallas_call | solution.py:35
  20.7 2.7 %all-to-all-done.ids = s16[32,8,128]{2,1,0:T(8,128)(2,1)} async-done(((s16[32,8,128]{2,1,0:T(8,128)(2,1)}), s16[32,8,128]{2,1,0:T(8,128)(2,1)}, u32[]{:S(2)}, u32[]{:S(2)}) %all-to-all-start) | async-done | bytes 65568 | tf_op jit(solution)/shard_map/all_to_all | solution.py:220
  23.4 0.0 copy-start.4
  23.4 4.4 %all-to-all-start.1 = ((bf16[4,32,6912]{2,1,0:T(8,128)(2,1)}), bf16[4,32,6912]{2,1,0:T(8,128)(2,1)S(1)}, u32[]{:S(2)}, u32[]{:S(2)}) async-start(bf16[4,32,6912]{2,1,0:T(8,128)(2,1)} %get-tuple-element.15), calls=%async_computation.1 | async-start | bytes 3538944 | tf_op jit(solution)/shard_map/all_to_all | solution.py:248
  27.8 0.0 collective-permute-start.2
  27.8 1.5 %collective-permute-done.2.pids = s16[32,8,128]{2,1,0:T(8,128)(2,1)S(1)} collective-permute-done((s16[32,8,128]{2,1,0:T(8,128)(2,1)}, s16[32,8,128]{2,1,0:T(8,128)(2,1)S(1)}, u32[]{:S(2)}, u32[]{:S(2)}) %collective-permute-start.2) | collective-permute-done | bytes 65568 | tf_op jit(solution)/shard_map/ppermute | solution.py:249
  29.3 0.0 copy-done.4
  29.3 0.0 copy-start.5
  29.3 1.5 %copy-done.5 = bf16[256,3328]{1,0:T(8,128)(2,1)S(1)} copy-done((bf16[256,3328]{1,0:T(8,128)(2,1)S(1)}, bf16[256,3328]{1,0:T(8,128)(2,1)}, u32[]{:S(2)}) %copy-start.5) | copy-done | bytes 1703960
  30.8 2.8 %tables.1 = (f32[26,32,128]{2,1,0:T(8,128)S(1)}, bf16[26,32,128]{2,1,0:T(8,128)(2,1)S(1)}, bf16[26,32,128]{2,1,0:T(8,128)(2,1)S(1)}, bf16[26,32,128]{2,1,0:T(8,128)(2,1)S(1)}) custom-call(s32[26]{0:T(128)S(1)} %copy-done.4, bf16[256,3328]{1,0:T(8,128)(2,1)S(1)} %copy-done.5, s16[32,8,128]{2,1,0:T(8,128)(2,1)} %all-to-all-done.ids, ...), custom_call_target="tpu_custom_call" | custom-call | flops 1358954496 | bytes 9437184 | tf_op jit(solution)/shard_map/tables/pallas_call | solution.py:35
  33.6 0.7 collective-permute-start.3
  34.2 2.0 %collective-permute-start.4 = (bf16[26,32,128]{2,1,0:T(8,128)(2,1)S(1)}, bf16[26,32,128]{2,1,0:T(8,128)(2,1)S(1)}, u32[]{:S(2)}, u32[]{:S(2)}) collective-permute-start(bf16[26,32,128]{2,1,0:T(8,128)(2,1)S(1)} %get-tuple-element.20), channel_id=1, source_target_pairs={{0,16},{8,24},{16,0},{24,8},{1,17},{9,25},{17,1},{25,9},{2,18},{10... | collective-permute-start | bytes 638984 | tf_op jit(solution)/shard_map/ppermute | solution.py:208
  36.3 1.3 %collective-permute-start.5 = (bf16[26,32,128]{2,1,0:T(8,128)(2,1)S(1)}, bf16[26,32,128]{2,1,0:T(8,128)(2,1)S(1)}, u32[]{:S(2)}, u32[]{:S(2)}) collective-permute-start(bf16[26,32,128]{2,1,0:T(8,128)(2,1)S(1)} %get-tuple-element.21), channel_id=1, source_target_pairs={{0,24},{8,0},{16,8},{24,16},{1,25},{9,1},{17,9},{25,17},{2,26},{10... | collective-permute-start | bytes 638984 | tf_op jit(solution)/shard_map/ppermute | solution.py:208
  37.6 9.2 %collective-permute-done.3.refs_1_ = bf16[26,32,128]{2,1,0:T(8,128)(2,1)S(1)} collective-permute-done((bf16[26,32,128]{2,1,0:T(8,128)(2,1)S(1)}, bf16[26,32,128]{2,1,0:T(8,128)(2,1)S(1)}, u32[]{:S(2)}, u32[]{:S(2)}) %collective-permute-start.3) | collective-permute-done | bytes 213024 | tf_op jit(solution)/shard_map/ppermute | solution.py:208
  46.7 0.0 collective-permute-done.4.refs_2_
  46.7 0.6 collective-permute-done.5.refs_3_
  47.4 0.1 table_second.1
  47.5 2.1 %collective-permute-start.6 = (bf16[26,8,128]{2,1,0:T(8,128)(2,1)S(1)}, bf16[26,8,128]{2,1,0:T(8,128)(2,1)S(1)}, u32[]{:S(2)}, u32[]{:S(2)}) collective-permute-start(bf16[26,8,128]{2,1,0:T(8,128)(2,1)S(1)} %get-tuple-element.23), channel_id=1, source_target_pairs={{0,64},{64,128},{128,192},{192,0},{1,65},{65,129},{129,193},{193,1... | collective-permute-start | bytes 159752 | tf_op jit(solution)/shard_map/ppermute | solution.py:208
  49.6 2.7 %collective-permute-start.7 = (bf16[26,8,128]{2,1,0:T(8,128)(2,1)S(1)}, bf16[26,8,128]{2,1,0:T(8,128)(2,1)S(1)}, u32[]{:S(2)}, u32[]{:S(2)}) collective-permute-start(bf16[26,8,128]{2,1,0:T(8,128)(2,1)S(1)} %get-tuple-element.24), channel_id=1, source_target_pairs={{0,128},{64,192},{128,0},{192,64},{1,129},{65,193},{129,1},{193,65... | collective-permute-start | bytes 159752 | tf_op jit(solution)/shard_map/ppermute | solution.py:208
  52.2 1.5 %collective-permute-start.8 = (bf16[26,8,128]{2,1,0:T(8,128)(2,1)S(1)}, bf16[26,8,128]{2,1,0:T(8,128)(2,1)S(1)}, u32[]{:S(2)}, u32[]{:S(2)}) collective-permute-start(bf16[26,8,128]{2,1,0:T(8,128)(2,1)S(1)} %get-tuple-element.25), channel_id=1, source_target_pairs={{0,192},{64,0},{128,64},{192,128},{1,193},{65,1},{129,65},{193,129... | collective-permute-start | bytes 159752 | tf_op jit(solution)/shard_map/ppermute | solution.py:208
  53.7 0.0 all-to-all-done.1.came
  53.7 0.6 cross_sum.1.cross
  54.4 0.0 collective-permute-done.6.refs_1_
  54.4 0.8 %collective-permute-done.7.refs_2_ = bf16[26,8,128]{2,1,0:T(8,128)(2,1)S(1)} collective-permute-done((bf16[26,8,128]{2,1,0:T(8,128)(2,1)S(1)}, bf16[26,8,128]{2,1,0:T(8,128)(2,1)S(1)}, u32[]{:S(2)}, u32[]{:S(2)}) %collective-permute-start.7) | collective-permute-done | bytes 53280 | tf_op jit(solution)/shard_map/ppermute | solution.py:208
  55.2 1.2 %collective-permute-done.8.refs_3_ = bf16[26,8,128]{2,1,0:T(8,128)(2,1)S(1)} collective-permute-done((bf16[26,8,128]{2,1,0:T(8,128)(2,1)S(1)}, bf16[26,8,128]{2,1,0:T(8,128)(2,1)S(1)}, u32[]{:S(2)}, u32[]{:S(2)}) %collective-permute-start.8) | collective-permute-done | bytes 53280 | tf_op jit(solution)/shard_map/ppermute | solution.py:208
  56.4 0.8 route.1
  57.1 24.2 %all_to_all.15.came = bf16[32,70,128]{2,1,0:T(8,128)(2,1)S(1)} all-to-all(bf16[32,70,128]{2,1,0:T(8,128)(2,1)S(1)} %route.1), channel_id=1, replica_groups=mesh['x'=4,'c'=2,'y'=4,'z'=8] {'y','z'}, dimensions={0} | all-to-all | bytes 1146880 | tf_op jit(solution)/shard_map/all_to_all | solution.py:301
  81.3 0.7 last.1
  (1 shorter events, 0.0 us)
Async XLA Ops:
  0.6 13.6 %copy-start = (bf16[128,3456]{1,0:T(8,128)(2,1)S(1)}, bf16[128,3456]{1,0:T(8,128)(2,1)}, u32[]{:S(2)}) copy-start(bf16[128,3456]{1,0:T(8,128)(2,1)} %x.1) | copy-start | bytes 2654212
  0.6 13.6 %copy-start.1 = (bf16[128,3456]{1,0:T(8,128)(2,1)S(1)}, bf16[128,3456]{1,0:T(8,128)(2,1)}, u32[]{:S(2)}) copy-start(bf16[128,3456]{1,0:T(8,128)(2,1)} %up.1) | copy-start | bytes 2654212
  0.7 13.6 %copy-start.3 = (f32[3456]{0:T(1024)S(1)}, f32[3456]{0:T(1024)}, u32[]{:S(2)}) copy-start(f32[3456]{0:T(1024)} %bias.1) | copy-start | bytes 41476
  0.7 13.6 %collective-permute-start = (bf16[128,3456]{1,0:T(8,128)(2,1)}, bf16[128,3456]{1,0:T(8,128)(2,1)S(1)}, u32[]{:S(2)}, u32[]{:S(2)}) collective-permute-start(bf16[128,3456]{1,0:T(8,128)(2,1)} %x.1), channel_id=1, source_target_pairs={{0,32},{32,0},{1,33},{33,1},{2,34},{34,2},{3,35},{35,3},{4,36},{36... | collective-permute-start | bytes 2654216 | tf_op jit(solution)/shard_map/ppermute | solution.py:216
  0.8 13.5 %collective-permute-start.1 = (bf16[128,3456]{1,0:T(8,128)(2,1)}, bf16[128,3456]{1,0:T(8,128)(2,1)S(1)}, u32[]{:S(2)}, u32[]{:S(2)}) collective-permute-start(bf16[128,3456]{1,0:T(8,128)(2,1)} %up.1), channel_id=1, source_target_pairs={{0,32},{32,0},{1,33},{33,1},{2,34},{34,2},{3,35},{35,3},{4,36},{36... | collective-permute-start | bytes 2654216 | tf_op jit(solution)/shard_map/ppermute | solution.py:217
  1.3 0.9 %copy-start.6 = (s32[2,4,4096]{2,1,0:T(4,128)S(1)}, s32[2,4,4096]{2,1,0:T(4,128)}, u32[]{:S(2)}) copy-start(s32[2,4,4096]{2,1,0:T(4,128)} %ids.3) | copy-start | bytes 393220
  2.2 0.6 copy-start.2
  2.8 20.6 %all-to-all-start = ((s16[32,8,128]{2,1,0:T(8,128)(2,1)}), s16[32,8,128]{2,1,0:T(8,128)(2,1)}, u32[]{:S(2)}, u32[]{:S(2)}) async-start(s16[32,8,128]{2,1,0:T(8,128)(2,1)} %copy-done.2), calls=%async_computation | async-start | bytes 131072 | tf_op jit(solution)/shard_map/all_to_all | solution.py:220
  23.4 5.9 %copy-start.4 = (s32[26]{0:T(128)S(1)}, s32[26]{0:T(128)}, u32[]{:S(2)}) copy-start(s32[26]{0:T(128)} %placement.3) | copy-start | bytes 316
  23.4 30.3 %all-to-all-start.1 = ((bf16[4,32,6912]{2,1,0:T(8,128)(2,1)}), bf16[4,32,6912]{2,1,0:T(8,128)(2,1)S(1)}, u32[]{:S(2)}, u32[]{:S(2)}) async-start(bf16[4,32,6912]{2,1,0:T(8,128)(2,1)} %get-tuple-element.15), calls=%async_computation.1 | async-start | bytes 3538944 | tf_op jit(solution)/shard_map/all_to_all | solution.py:248
  27.8 1.5 %collective-permute-start.2 = (s16[32,8,128]{2,1,0:T(8,128)(2,1)}, s16[32,8,128]{2,1,0:T(8,128)(2,1)S(1)}, u32[]{:S(2)}, u32[]{:S(2)}) collective-permute-start(s16[32,8,128]{2,1,0:T(8,128)(2,1)} %all-to-all-done.ids), channel_id=1, source_target_pairs={{0,32},{32,0},{1,33},{33,1},{2,34},{34,2},{3,35},{35,3},{4,36},{36... | collective-permute-start | bytes 196616 | tf_op jit(solution)/shard_map/ppermute | solution.py:249
  29.3 1.5 %copy-start.5 = (bf16[256,3328]{1,0:T(8,128)(2,1)S(1)}, bf16[256,3328]{1,0:T(8,128)(2,1)}, u32[]{:S(2)}) copy-start(bf16[256,3328]{1,0:T(8,128)(2,1)} %get-tuple-element.16.pooled) | copy-start | bytes 5111812
  33.6 13.2 %collective-permute-start.3 = (bf16[26,32,128]{2,1,0:T(8,128)(2,1)S(1)}, bf16[26,32,128]{2,1,0:T(8,128)(2,1)S(1)}, u32[]{:S(2)}, u32[]{:S(2)}) collective-permute-start(bf16[26,32,128]{2,1,0:T(8,128)(2,1)S(1)} %get-tuple-element.19), channel_id=1, source_target_pairs={{0,8},{8,16},{16,24},{24,0},{1,9},{9,17},{17,25},{25,1},{2,10},{10... | collective-permute-start | bytes 638984 | tf_op jit(solution)/shard_map/ppermute | solution.py:208
  34.2 12.5 %collective-permute-start.4 = (bf16[26,32,128]{2,1,0:T(8,128)(2,1)S(1)}, bf16[26,32,128]{2,1,0:T(8,128)(2,1)S(1)}, u32[]{:S(2)}, u32[]{:S(2)}) collective-permute-start(bf16[26,32,128]{2,1,0:T(8,128)(2,1)S(1)} %get-tuple-element.20), channel_id=1, source_target_pairs={{0,16},{8,24},{16,0},{24,8},{1,17},{9,25},{17,1},{25,9},{2,18},{10... | collective-permute-start | bytes 638984 | tf_op jit(solution)/shard_map/ppermute | solution.py:208
  36.3 11.1 %collective-permute-start.5 = (bf16[26,32,128]{2,1,0:T(8,128)(2,1)S(1)}, bf16[26,32,128]{2,1,0:T(8,128)(2,1)S(1)}, u32[]{:S(2)}, u32[]{:S(2)}) collective-permute-start(bf16[26,32,128]{2,1,0:T(8,128)(2,1)S(1)} %get-tuple-element.21), channel_id=1, source_target_pairs={{0,24},{8,0},{16,8},{24,16},{1,25},{9,1},{17,9},{25,17},{2,26},{10... | collective-permute-start | bytes 638984 | tf_op jit(solution)/shard_map/ppermute | solution.py:208
  47.5 6.9 %collective-permute-start.6 = (bf16[26,8,128]{2,1,0:T(8,128)(2,1)S(1)}, bf16[26,8,128]{2,1,0:T(8,128)(2,1)S(1)}, u32[]{:S(2)}, u32[]{:S(2)}) collective-permute-start(bf16[26,8,128]{2,1,0:T(8,128)(2,1)S(1)} %get-tuple-element.23), channel_id=1, source_target_pairs={{0,64},{64,128},{128,192},{192,0},{1,65},{65,129},{129,193},{193,1... | collective-permute-start | bytes 159752 | tf_op jit(solution)/shard_map/ppermute | solution.py:208
  49.6 5.6 %collective-permute-start.7 = (bf16[26,8,128]{2,1,0:T(8,128)(2,1)S(1)}, bf16[26,8,128]{2,1,0:T(8,128)(2,1)S(1)}, u32[]{:S(2)}, u32[]{:S(2)}) collective-permute-start(bf16[26,8,128]{2,1,0:T(8,128)(2,1)S(1)} %get-tuple-element.24), channel_id=1, source_target_pairs={{0,128},{64,192},{128,0},{192,64},{1,129},{65,193},{129,1},{193,65... | collective-permute-start | bytes 159752 | tf_op jit(solution)/shard_map/ppermute | solution.py:208
  52.2 4.1 %collective-permute-start.8 = (bf16[26,8,128]{2,1,0:T(8,128)(2,1)S(1)}, bf16[26,8,128]{2,1,0:T(8,128)(2,1)S(1)}, u32[]{:S(2)}, u32[]{:S(2)}) collective-permute-start(bf16[26,8,128]{2,1,0:T(8,128)(2,1)S(1)} %get-tuple-element.25), channel_id=1, source_target_pairs={{0,192},{64,0},{128,64},{192,128},{1,193},{65,1},{129,65},{193,129... | collective-permute-start | bytes 159752 | tf_op jit(solution)/shard_map/ppermute | solution.py:208

commit v8 on v7

--- a/solution.py
+++ b/solution.py
@@ -119,29 +119,30 @@
         visit(table, owner, slot)
 
 
-def table_kernel(placement, pooled, ids, pids, *refs):
-    outs, (state, counts, used) = refs[:4], refs[4:]
+def count_kernel(placement, ids, counts, state, used):
     n = ids.shape[2]
-    for p in range(NJ):
-        state[p, :8] = ids[p].astype(I32)
-        state[p, 8:] = pids[p].astype(I32)
+    state[...] = ids[...].astype(I32)
     at = lax.broadcasted_iota(I32, (RANK // 2, n), 0)
     row = lax.rem(lax.axis_index("x") + (at // 8) % 4, NX) * 64 + at % 8
     row = row + lax.rem(lax.axis_index("y") + at // 32, NY) * 8 + lax.axis_index("c") * 32
 
     def count_rows(table, owner, slot):
-        looked = state[owner]
-        for half in range(2):
-            eight = looked[half * 8 : half * 8 + 8]
-            four = jnp.where(slot == 0, eight[:4], eight[4:])
-            count = jnp.where(four[0:1] == row, 1.0, 0.0)
-            for k in range(1, 4):
-                count = count + jnp.where(four[k : k + 1] == row, 1.0, 0.0)
-            counts[table, :, half * n : (half + 1) * n] = count.astype(BF)
+        eight = state[owner]
+        four = jnp.where(slot == 0, eight[:4], eight[4:])
+        count = jnp.where(four[0:1] == row, 1.0, 0.0)
+        for k in range(1, 4):
+            count = count + jnp.where(four[k : k + 1] == row, 1.0, 0.0)
+        counts[table] = count.astype(BF)
 
     slots_of(placement, used, count_rows)
+
+
+def table_kernel(placement, mine, pooled, pids, *refs):
+    outs, (theirs, state, used) = refs[:4], refs[4:]
+    count_kernel(placement, pids, theirs, state, used)
     for table in range(TABLES):
-        total = mm(counts[table], pooled[:, table * EMB : (table + 1) * EMB])
+        both = jnp.concatenate([mine[table], theirs[table]], axis=1)
+        total = mm(both, pooled[:, table * EMB : (table + 1) * EMB])
         for d in range(NY):
             outs[d][table] = total[d * 32 : (d + 1) * 32].astype(outs[d].dtype)
 
@@ -248,20 +249,27 @@
     cross = lax.all_to_all(cross, "x", 0, 0, tiled=True)
     pids = lax.ppermute(ids, "c", swap)
 
+    counted = ((TABLES, RANK // 2, samples), BF)
+    work = [pltpu.VMEM((NJ, 8, EMB), I32), pltpu.SMEM((NJ,), I32)]
+    (counts,) = call(
+        count_kernel,
+        "counts",
+        [counted],
+        placement,
+        ids,
+        scratch=work,
+        flops=1 << 30,
+        size=1 << 20,
+    )
     tables = call(
         table_kernel,
         "tables",
         [((TABLES, 32, EMB), F32)] + [((TABLES, 32, EMB), BF)] * 3,
         placement,
+        counts,
         pooled,
-        ids,
         pids,
-        scratch=[
-            pltpu.VMEM((NJ, 16, EMB), I32),
-            pltpu.VMEM((TABLES, RANK // 2, 2 * samples), BF),
-            pltpu.SMEM((NJ,), I32),
-        ],
-        vmem=40 << 20,
+        scratch=[pltpu.VMEM(*counted)] + work,
         flops=6 * 256 * 256 * width,
         size=9 << 20,
     )

time: 82.4 us -> 80.3 us (0.975)
  local copies, waits for them, and re-layouts: 2.99 us -> 1.54 us
  waiting for transfers between devices: 15.9 us -> 14.7 us
    ppermute x1, waiting for transfers between devices: 1.46 us -> 0.01 us  [on_device(): pids = lax.ppermute(ids, 'c', swap)]
    unnamed x14, local copies, waits for them, and re-layouts: 2.99 us -> 1.54 us
    pallas_call x7 -> x8, Pallas kernels: 11.5 us -> 12.1 us  [call(): pl.pallas_call(kernel, out_shape=tuple((jax.ShapeDtypeStruct(shape, dtype...]
  transfers between devices with their start and end apart: 11 -> 11, of which waited for: 6 -> 5; matrix products, arithmetic and copies ran while one was open for 0% -> 0% of each run, Pallas kernels for 12% -> 13%
where the time goes in v8:
time: 80.3 us; the launch traced here: 79.9 us
  starting transfers between devices  26.7 us (33%)
  blocking collectives  24.2 us (30%)
  waiting for transfers between devices  14.7 us (18%)
  Pallas kernels  12.1 us (15%)
  local copies, waits for them, and re-layouts  1.54 us (2%)
    all_to_all x1, blocking collectives, on_device(): routed = lax.all_to_all(routed, ('y', 'z'), 0, 0, tiled=True)  24.2 us
    pallas_call x8, Pallas kernels, call(): pl.pallas_call(kernel, out_shape=tuple((jax.ShapeDtypeStruct(shape, dtype...  12.1 us
    ppermute x6, waiting for transfers between devices, shift(): lax.ppermute(chunks[d], axis, [(i, (i + d) % n) for i in range(n)])  12 us
    all_to_all x1, starting transfers between devices, on_device(): ids = lax.all_to_all(ids, ('y', 'z'), 0, 0, tiled=True)  11.4 us
    ppermute x6, starting transfers between devices, shift(): lax.ppermute(chunks[d], axis, [(i, (i + d) % n) for i in range(n)])  10.2 us
    all_to_all x1, starting transfers between devices, on_device(): cross = lax.all_to_all(cross, 'x', 0, 0, tiled=True)  4.42 us
    all_to_all x1, waiting for transfers between devices, on_device(): ids = lax.all_to_all(ids, ('y', 'z'), 0, 0, tiled=True)  2.68 us
  transfers between devices with their start and end apart: 11, of which 5 were waited for; matrix products, arithmetic and copies ran while one was open for 0% of the time, Pallas kernels for 13%

profile of v8, /device:TPU:32, one launch (start us, length us, event | category | flops | bytes accessed | tf_op | source)
XLA Modules:
  0.0 79.9 jit_solution(16471421523292260118)
XLA Ops:
  0.6 0.0 copy-start
  0.6 0.0 copy-start.1
  0.7 0.0 copy-start.3
  0.7 0.1 collective-permute-start
  0.8 0.5 collective-permute-start.1
  1.3 0.0 copy-start.6
  1.3 0.9 %copy-done.6 = s32[2,4,4096]{2,1,0:T(4,128)S(1)} copy-done((s32[2,4,4096]{2,1,0:T(4,128)S(1)}, s32[2,4,4096]{2,1,0:T(4,128)}, u32[]{:S(2)}) %copy-start.6) | copy-done | bytes 131096
  2.2 0.0 copy-start.2
  2.2 0.6 copy-done.2
  2.8 11.4 %all-to-all-start = ((s16[32,8,128]{2,1,0:T(8,128)(2,1)}), s16[32,8,128]{2,1,0:T(8,128)(2,1)}, u32[]{:S(2)}, u32[]{:S(2)}) async-start(s16[32,8,128]{2,1,0:T(8,128)(2,1)} %copy-done.2), calls=%async_computation | async-start | bytes 131072 | tf_op jit(solution)/shard_map/all_to_all | solution.py:221
  14.2 0.0 collective-permute-done.px
  14.2 0.0 collective-permute-done.1.pup
  14.3 0.0 copy-done
  14.3 0.0 copy-done.1
  14.3 0.0 copy-done.3
  14.3 6.4 %dense.1 = (bf16[4,32,6912]{2,1,0:T(8,128)(2,1)}, bf16[256,3328]{1,0:T(8,128)(2,1)}) custom-call(bf16[128,3456]{1,0:T(8,128)(2,1)S(1)} %copy-done, bf16[128,3456]{1,0:T(8,128)(2,1)S(1)} %collective-permute-done.px, bf16[128,3456]{1,0:T(8,128)(2,1)S(1)} %copy-done.1, bf16[128,3456]{1,0:T(8,128)(2,1)S(1)} %collective-permute-done.1.pup, ...), custom_call_target="tpu_custom_call" | custom-call | flops 1358954496 | bytes 6291456 | tf_op jit(solution)/shard_map/dense/pallas_call | solution.py:35
  20.7 2.7 %all-to-all-done.ids = s16[32,8,128]{2,1,0:T(8,128)(2,1)} async-done(((s16[32,8,128]{2,1,0:T(8,128)(2,1)}), s16[32,8,128]{2,1,0:T(8,128)(2,1)}, u32[]{:S(2)}, u32[]{:S(2)}) %all-to-all-start) | async-done | bytes 65568 | tf_op jit(solution)/shard_map/all_to_all | solution.py:221
  23.4 0.0 copy-start.4
  23.4 4.4 %all-to-all-start.1 = ((bf16[4,32,6912]{2,1,0:T(8,128)(2,1)}), bf16[4,32,6912]{2,1,0:T(8,128)(2,1)S(1)}, u32[]{:S(2)}, u32[]{:S(2)}) async-start(bf16[4,32,6912]{2,1,0:T(8,128)(2,1)} %get-tuple-element.15), calls=%async_computation.1 | async-start | bytes 3538944 | tf_op jit(solution)/shard_map/all_to_all | solution.py:249
  27.8 0.0 copy-start.5
  27.8 0.0 collective-permute-start.2
  27.8 0.0 copy-done.4
  27.8 1.7 %counts.1.mine = bf16[26,128,128]{2,1,0:T(8,128)(2,1)S(1)} custom-call(s32[26]{0:T(128)S(1)} %copy-done.4, s16[32,8,128]{2,1,0:T(8,128)(2,1)} %all-to-all-done.ids), custom_call_target="tpu_custom_call" | custom-call | flops 1073741824 | bytes 1048576 | tf_op jit(solution)/shard_map/counts/pallas_call | solution.py:35
  29.6 0.0 collective-permute-done.2.pids
  29.6 0.0 copy-done.5
  29.6 1.7 %tables.1 = (f32[26,32,128]{2,1,0:T(8,128)S(1)}, bf16[26,32,128]{2,1,0:T(8,128)(2,1)S(1)}, bf16[26,32,128]{2,1,0:T(8,128)(2,1)S(1)}, bf16[26,32,128]{2,1,0:T(8,128)(2,1)S(1)}) custom-call(s32[26]{0:T(128)S(1)} %copy-done.4, bf16[26,128,128]{2,1,0:T(8,128)(2,1)S(1)} %counts.1.mine, bf16[256,3328]{1,0:T(8,128)(2,1)S(1)} %copy-done.5, ...), custom_call_target="tpu_custom_call" | custom-call | flops 1358954496 | bytes 9437184 | tf_op jit(solution)/shard_map/tables/pallas_call | solution.py:35
  31.2 0.7 collective-permute-start.3
  32.0 2.0 %collective-permute-start.4 = (bf16[26,32,128]{2,1,0:T(8,128)(2,1)S(1)}, bf16[26,32,128]{2,1,0:T(8,128)(2,1)S(1)}, u32[]{:S(2)}, u32[]{:S(2)}) collective-permute-start(bf16[26,32,128]{2,1,0:T(8,128)(2,1)S(1)} %get-tuple-element.20), channel_id=1, source_target_pairs={{0,16},{8,24},{16,0},{24,8},{1,17},{9,25},{17,1},{25,9},{2,18},{10... | collective-permute-start | bytes 638984 | tf_op jit(solution)/shard_map/ppermute | solution.py:209
  34.0 1.3 %collective-permute-start.5 = (bf16[26,32,128]{2,1,0:T(8,128)(2,1)S(1)}, bf16[26,32,128]{2,1,0:T(8,128)(2,1)S(1)}, u32[]{:S(2)}, u32[]{:S(2)}) collective-permute-start(bf16[26,32,128]{2,1,0:T(8,128)(2,1)S(1)} %get-tuple-element.21), channel_id=1, source_target_pairs={{0,24},{8,0},{16,8},{24,16},{1,25},{9,1},{17,9},{25,17},{2,26},{10... | collective-permute-start | bytes 638984 | tf_op jit(solution)/shard_map/ppermute | solution.py:209
  35.3 9.4 %collective-permute-done.3.refs_1_ = bf16[26,32,128]{2,1,0:T(8,128)(2,1)S(1)} collective-permute-done((bf16[26,32,128]{2,1,0:T(8,128)(2,1)S(1)}, bf16[26,32,128]{2,1,0:T(8,128)(2,1)S(1)}, u32[]{:S(2)}, u32[]{:S(2)}) %collective-permute-start.3) | collective-permute-done | bytes 213024 | tf_op jit(solution)/shard_map/ppermute | solution.py:209
  44.6 0.0 collective-permute-done.4.refs_2_
  44.6 0.6 collective-permute-done.5.refs_3_
  45.3 0.1 table_second.1
  45.4 2.1 %collective-permute-start.6 = (bf16[26,8,128]{2,1,0:T(8,128)(2,1)S(1)}, bf16[26,8,128]{2,1,0:T(8,128)(2,1)S(1)}, u32[]{:S(2)}, u32[]{:S(2)}) collective-permute-start(bf16[26,8,128]{2,1,0:T(8,128)(2,1)S(1)} %get-tuple-element.23), channel_id=1, source_target_pairs={{0,64},{64,128},{128,192},{192,0},{1,65},{65,129},{129,193},{193,1... | collective-permute-start | bytes 159752 | tf_op jit(solution)/shard_map/ppermute | solution.py:209
  47.5 2.7 %collective-permute-start.7 = (bf16[26,8,128]{2,1,0:T(8,128)(2,1)S(1)}, bf16[26,8,128]{2,1,0:T(8,128)(2,1)S(1)}, u32[]{:S(2)}, u32[]{:S(2)}) collective-permute-start(bf16[26,8,128]{2,1,0:T(8,128)(2,1)S(1)} %get-tuple-element.24), channel_id=1, source_target_pairs={{0,128},{64,192},{128,0},{192,64},{1,129},{65,193},{129,1},{193,65... | collective-permute-start | bytes 159752 | tf_op jit(solution)/shard_map/ppermute | solution.py:209
  50.1 1.5 %collective-permute-start.8 = (bf16[26,8,128]{2,1,0:T(8,128)(2,1)S(1)}, bf16[26,8,128]{2,1,0:T(8,128)(2,1)S(1)}, u32[]{:S(2)}, u32[]{:S(2)}) collective-permute-start(bf16[26,8,128]{2,1,0:T(8,128)(2,1)S(1)} %get-tuple-element.25), channel_id=1, source_target_pairs={{0,192},{64,0},{128,64},{192,128},{1,193},{65,1},{129,65},{193,129... | collective-permute-start | bytes 159752 | tf_op jit(solution)/shard_map/ppermute | solution.py:209
  51.6 0.0 all-to-all-done.1.came
  51.6 0.6 cross_sum.1.cross
  52.3 0.0 collective-permute-done.6.refs_1_
  52.3 0.8 %collective-permute-done.7.refs_2_ = bf16[26,8,128]{2,1,0:T(8,128)(2,1)S(1)} collective-permute-done((bf16[26,8,128]{2,1,0:T(8,128)(2,1)S(1)}, bf16[26,8,128]{2,1,0:T(8,128)(2,1)S(1)}, u32[]{:S(2)}, u32[]{:S(2)}) %collective-permute-start.7) | collective-permute-done | bytes 53280 | tf_op jit(solution)/shard_map/ppermute | solution.py:209
  53.1 1.2 %collective-permute-done.8.refs_3_ = bf16[26,8,128]{2,1,0:T(8,128)(2,1)S(1)} collective-permute-done((bf16[26,8,128]{2,1,0:T(8,128)(2,1)S(1)}, bf16[26,8,128]{2,1,0:T(8,128)(2,1)S(1)}, u32[]{:S(2)}, u32[]{:S(2)}) %collective-permute-start.8) | collective-permute-done | bytes 53280 | tf_op jit(solution)/shard_map/ppermute | solution.py:209
  54.3 0.8 route.1
  55.1 24.2 %all_to_all.15.came = bf16[32,70,128]{2,1,0:T(8,128)(2,1)S(1)} all-to-all(bf16[32,70,128]{2,1,0:T(8,128)(2,1)S(1)} %route.1), channel_id=1, replica_groups=mesh['x'=4,'c'=2,'y'=4,'z'=8] {'y','z'}, dimensions={0} | all-to-all | bytes 1146880 | tf_op jit(solution)/shard_map/all_to_all | solution.py:309
  79.2 0.7 last.1
  (1 shorter events, 0.0 us)
Async XLA Ops:
  0.6 13.6 %copy-start = (bf16[128,3456]{1,0:T(8,128)(2,1)S(1)}, bf16[128,3456]{1,0:T(8,128)(2,1)}, u32[]{:S(2)}) copy-start(bf16[128,3456]{1,0:T(8,128)(2,1)} %x.1) | copy-start | bytes 2654212
  0.6 13.6 %copy-start.1 = (bf16[128,3456]{1,0:T(8,128)(2,1)S(1)}, bf16[128,3456]{1,0:T(8,128)(2,1)}, u32[]{:S(2)}) copy-start(bf16[128,3456]{1,0:T(8,128)(2,1)} %up.1) | copy-start | bytes 2654212
  0.7 13.6 %copy-start.3 = (f32[3456]{0:T(1024)S(1)}, f32[3456]{0:T(1024)}, u32[]{:S(2)}) copy-start(f32[3456]{0:T(1024)} %bias.1) | copy-start | bytes 41476
  0.7 13.6 %collective-permute-start = (bf16[128,3456]{1,0:T(8,128)(2,1)}, bf16[128,3456]{1,0:T(8,128)(2,1)S(1)}, u32[]{:S(2)}, u32[]{:S(2)}) collective-permute-start(bf16[128,3456]{1,0:T(8,128)(2,1)} %x.1), channel_id=1, source_target_pairs={{0,32},{32,0},{1,33},{33,1},{2,34},{34,2},{3,35},{35,3},{4,36},{36... | collective-permute-start | bytes 2654216 | tf_op jit(solution)/shard_map/ppermute | solution.py:217
  0.8 13.5 %collective-permute-start.1 = (bf16[128,3456]{1,0:T(8,128)(2,1)}, bf16[128,3456]{1,0:T(8,128)(2,1)S(1)}, u32[]{:S(2)}, u32[]{:S(2)}) collective-permute-start(bf16[128,3456]{1,0:T(8,128)(2,1)} %up.1), channel_id=1, source_target_pairs={{0,32},{32,0},{1,33},{33,1},{2,34},{34,2},{3,35},{35,3},{4,36},{36... | collective-permute-start | bytes 2654216 | tf_op jit(solution)/shard_map/ppermute | solution.py:218
  1.3 0.9 %copy-start.6 = (s32[2,4,4096]{2,1,0:T(4,128)S(1)}, s32[2,4,4096]{2,1,0:T(4,128)}, u32[]{:S(2)}) copy-start(s32[2,4,4096]{2,1,0:T(4,128)} %ids.3) | copy-start | bytes 393220
  2.2 0.6 copy-start.2
  2.8 20.6 %all-to-all-start = ((s16[32,8,128]{2,1,0:T(8,128)(2,1)}), s16[32,8,128]{2,1,0:T(8,128)(2,1)}, u32[]{:S(2)}, u32[]{:S(2)}) async-start(s16[32,8,128]{2,1,0:T(8,128)(2,1)} %copy-done.2), calls=%async_computation | async-start | bytes 131072 | tf_op jit(solution)/shard_map/all_to_all | solution.py:221
  23.4 4.4 %copy-start.4 = (s32[26]{0:T(128)S(1)}, s32[26]{0:T(128)}, u32[]{:S(2)}) copy-start(s32[26]{0:T(128)} %placement.5) | copy-start | bytes 316
  23.4 28.2 %all-to-all-start.1 = ((bf16[4,32,6912]{2,1,0:T(8,128)(2,1)}), bf16[4,32,6912]{2,1,0:T(8,128)(2,1)S(1)}, u32[]{:S(2)}, u32[]{:S(2)}) async-start(bf16[4,32,6912]{2,1,0:T(8,128)(2,1)} %get-tuple-element.15), calls=%async_computation.1 | async-start | bytes 3538944 | tf_op jit(solution)/shard_map/all_to_all | solution.py:249
  27.8 1.7 %copy-start.5 = (bf16[256,3328]{1,0:T(8,128)(2,1)S(1)}, bf16[256,3328]{1,0:T(8,128)(2,1)}, u32[]{:S(2)}) copy-start(bf16[256,3328]{1,0:T(8,128)(2,1)} %get-tuple-element.17.pooled) | copy-start | bytes 5111812
  27.8 1.7 %collective-permute-start.2 = (s16[32,8,128]{2,1,0:T(8,128)(2,1)}, s16[32,8,128]{2,1,0:T(8,128)(2,1)S(1)}, u32[]{:S(2)}, u32[]{:S(2)}) collective-permute-start(s16[32,8,128]{2,1,0:T(8,128)(2,1)} %all-to-all-done.ids), channel_id=1, source_target_pairs={{0,32},{32,0},{1,33},{33,1},{2,34},{34,2},{3,35},{35,3},{4,36},{36... | collective-permute-start | bytes 196616 | tf_op jit(solution)/shard_map/ppermute | solution.py:250
  31.2 13.4 %collective-permute-start.3 = (bf16[26,32,128]{2,1,0:T(8,128)(2,1)S(1)}, bf16[26,32,128]{2,1,0:T(8,128)(2,1)S(1)}, u32[]{:S(2)}, u32[]{:S(2)}) collective-permute-start(bf16[26,32,128]{2,1,0:T(8,128)(2,1)S(1)} %get-tuple-element.19), channel_id=1, source_target_pairs={{0,8},{8,16},{16,24},{24,0},{1,9},{9,17},{17,25},{25,1},{2,10},{10... | collective-permute-start | bytes 638984 | tf_op jit(solution)/shard_map/ppermute | solution.py:209
  32.0 12.7 %collective-permute-start.4 = (bf16[26,32,128]{2,1,0:T(8,128)(2,1)S(1)}, bf16[26,32,128]{2,1,0:T(8,128)(2,1)S(1)}, u32[]{:S(2)}, u32[]{:S(2)}) collective-permute-start(bf16[26,32,128]{2,1,0:T(8,128)(2,1)S(1)} %get-tuple-element.20), channel_id=1, source_target_pairs={{0,16},{8,24},{16,0},{24,8},{1,17},{9,25},{17,1},{25,9},{2,18},{10... | collective-permute-start | bytes 638984 | tf_op jit(solution)/shard_map/ppermute | solution.py:209
  34.0 11.3 %collective-permute-start.5 = (bf16[26,32,128]{2,1,0:T(8,128)(2,1)S(1)}, bf16[26,32,128]{2,1,0:T(8,128)(2,1)S(1)}, u32[]{:S(2)}, u32[]{:S(2)}) collective-permute-start(bf16[26,32,128]{2,1,0:T(8,128)(2,1)S(1)} %get-tuple-element.21), channel_id=1, source_target_pairs={{0,24},{8,0},{16,8},{24,16},{1,25},{9,1},{17,9},{25,17},{2,26},{10... | collective-permute-start | bytes 638984 | tf_op jit(solution)/shard_map/ppermute | solution.py:209
  45.4 6.9 %collective-permute-start.6 = (bf16[26,8,128]{2,1,0:T(8,128)(2,1)S(1)}, bf16[26,8,128]{2,1,0:T(8,128)(2,1)S(1)}, u32[]{:S(2)}, u32[]{:S(2)}) collective-permute-start(bf16[26,8,128]{2,1,0:T(8,128)(2,1)S(1)} %get-tuple-element.23), channel_id=1, source_target_pairs={{0,64},{64,128},{128,192},{192,0},{1,65},{65,129},{129,193},{193,1... | collective-permute-start | bytes 159752 | tf_op jit(solution)/shard_map/ppermute | solution.py:209
  47.5 5.6 %collective-permute-start.7 = (bf16[26,8,128]{2,1,0:T(8,128)(2,1)S(1)}, bf16[26,8,128]{2,1,0:T(8,128)(2,1)S(1)}, u32[]{:S(2)}, u32[]{:S(2)}) collective-permute-start(bf16[26,8,128]{2,1,0:T(8,128)(2,1)S(1)} %get-tuple-element.24), channel_id=1, source_target_pairs={{0,128},{64,192},{128,0},{192,64},{1,129},{65,193},{129,1},{193,65... | collective-permute-start | bytes 159752 | tf_op jit(solution)/shard_map/ppermute | solution.py:209
  50.1 4.1 %collective-permute-start.8 = (bf16[26,8,128]{2,1,0:T(8,128)(2,1)S(1)}, bf16[26,8,128]{2,1,0:T(8,128)(2,1)S(1)}, u32[]{:S(2)}, u32[]{:S(2)}) collective-permute-start(bf16[26,8,128]{2,1,0:T(8,128)(2,1)S(1)} %get-tuple-element.25), channel_id=1, source_target_pairs={{0,192},{64,0},{128,64},{192,128},{1,193},{65,1},{129,65},{193,129... | collective-permute-start | bytes 159752 | tf_op jit(solution)/shard_map/ppermute | solution.py:209

commit v9 on v8

--- a/solution.py
+++ b/solution.py
@@ -61,50 +61,58 @@
 def dense_kernel(x, px, up, pup, v_in, u_in, bias, out, pooled, both, prod, v, u, held, held_p, in_sems, sems):
     n, width = x.shape
     core = lax.axis_index("c")
-    loads = []
-    for source, target in ((v_in, v), (u_in, u)):
-        for k in range(2):
-            rows = slice(k * 128, (k + 1) * 128)
-            loads.append(
-                pltpu.make_async_copy(source.at[rows], target.at[rows], in_sems.at[len(loads)])
-            )
-            loads[-1].start()
+    step = 1152
+    copies = []
+
+    def load(source, target, first):
+        parts = [slice(k * 128, (k + 1) * 128) for k in range(2)]
+        loads = [
+            pltpu.make_async_copy(source.at[rows], target.at[rows], in_sems.at[first + k])
+            for k, rows in enumerate(parts)
+        ]
+        for part in loads:
+            part.start()
+        return loads
+
+    def send(source, target):
+        copies.append(pltpu.make_async_copy(source, target, sems.at[len(copies)]))
+        copies[-1].start()
+
+    def half(left, right, base):
+        for k in range(width // step):
+            total = mm(left, right[:, k * step : (k + 1) * step])
+            cols = slice(base + k * step, base + (k + 1) * step)
+            for i in range(NX):
+                held[i, :, cols] = total[i * NJ : (i + 1) * NJ].astype(BF)
+            send(held.at[:, :, cols], out.at[:, :, cols])
+
+    loads = load(v_in, v, 0)
     both[:n] = x[...]
     both[n:] = px[...]
     prod[:n] = (x[...].astype(F32) * up[...].astype(F32)).astype(BF)
     prod[n:] = (px[...].astype(F32) * pup[...].astype(F32)).astype(BF)
-    loads[0].wait()
-    loads[1].wait()
+    for part in loads:
+        part.wait()
+    loads = load(u_in, u, 2)
     hid = nt(v[...], both[...]).astype(BF)
-    loads[2].wait()
-    loads[3].wait()
+    half(own_rows(hid.astype(F32), core).astype(BF), prod, 0)
+    for part in loads:
+        part.wait()
     hgr = nt(u[...], prod[...]).astype(BF)
-    hid_own = own_rows(hid.astype(F32), core).astype(BF)
-    hgr_own = own_rows(hgr.astype(F32), core).astype(BF)
-    step = 1152
-    copies = []
-    for side, (left, right) in enumerate(((hid_own, prod), (hgr_own, both))):
-        for k in range(width // step):
-            total = mm(left, right[:, k * step : (k + 1) * step])
-            cols = slice(side * width + k * step, side * width + (k + 1) * step)
-            for i in range(NX):
-                held[i, :, cols] = total[i * NJ : (i + 1) * NJ].astype(BF)
-            copies.append(
-                pltpu.make_async_copy(
-                    held.at[:, :, cols], out.at[:, :, cols], sems.at[len(copies)]
-                )
-            )
-            copies[-1].start()
+    half(own_rows(hgr.astype(F32), core).astype(BF), both, width)
     hid_s = hid.astype(F32).T.astype(BF)
     hgr_s = hgr.astype(F32).T.astype(BF)
+    sent = 0
     for pair in range(TABLES // 2):
         cols = slice(EMB + pair * 256, EMB + pair * 256 + 256)
         mixed = mm(hid_s, u[:, cols]) + bias[cols].reshape(1, 256)
         back = mm(hgr_s, v[:, cols])
         up_float = jnp.concatenate([up[:, cols], pup[:, cols]], axis=0).astype(F32)
         held_p[:, pair * 256 : pair * 256 + 256] = (up_float * (1.0 + mixed) + back).astype(BF)
-    copies.append(pltpu.make_async_copy(held_p, pooled, sems.at[len(copies)]))
-    copies[-1].start()
+        if pair in (3, 7, 10, 12):
+            cols = slice(sent, pair * 256 + 256)
+            send(held_p.at[:, cols], pooled.at[:, cols])
+            sent = pair * 256 + 256
     for copy in copies:
         copy.wait()
 
@@ -239,7 +247,7 @@
             pltpu.VMEM((NX, NJ, 2 * width), BF),
             pltpu.VMEM((2 * samples, TABLES * EMB), BF),
             pltpu.SemaphoreType.DMA((4,)),
-            pltpu.SemaphoreType.DMA((7,)),
+            pltpu.SemaphoreType.DMA((10,)),
         ],
         vmem=50 << 20,
         flops=6 * 256 * 256 * width,

time: 80.3 us -> 80.5 us (level)
  no operation moved by 1% of the time
where the time goes in v9:
time: 80.5 us; the launch traced here: 80.1 us
  starting transfers between devices  26.7 us (33%)
  blocking collectives  24.4 us (30%)
  waiting for transfers between devices  14.5 us (18%)
  Pallas kernels  12.3 us (15%)
  local copies, waits for them, and re-layouts  1.54 us (2%)
    all_to_all x1, blocking collectives, on_device(): routed = lax.all_to_all(routed, ('y', 'z'), 0, 0, tiled=True)  24.4 us
    pallas_call x8, Pallas kernels, call(): pl.pallas_call(kernel, out_shape=tuple((jax.ShapeDtypeStruct(shape, dtype...  12.3 us
    ppermute x6, waiting for transfers between devices, shift(): lax.ppermute(chunks[d], axis, [(i, (i + d) % n) for i in range(n)])  12 us
    all_to_all x1, starting transfers between devices, on_device(): ids = lax.all_to_all(ids, ('y', 'z'), 0, 0, tiled=True)  11.4 us
    ppermute x6, starting transfers between devices, shift(): lax.ppermute(chunks[d], axis, [(i, (i + d) % n) for i in range(n)])  10.2 us
    all_to_all x1, starting transfers between devices, on_device(): cross = lax.all_to_all(cross, 'x', 0, 0, tiled=True)  4.42 us
    all_to_all x1, waiting for transfers between devices, on_device(): ids = lax.all_to_all(ids, ('y', 'z'), 0, 0, tiled=True)  2.48 us
  transfers between devices with their start and end apart: 11, of which 5 were waited for; matrix products, arithmetic and copies ran while one was open for 0% of the time, Pallas kernels for 13%

profile of v9, /device:TPU:32, one launch (start us, length us, event | category | flops | bytes accessed | tf_op | source)
XLA Modules:
  0.0 80.1 jit_solution(15222781919907866411)
XLA Ops:
  0.6 0.0 copy-start
  0.6 0.0 copy-start.1
  0.7 0.0 copy-start.3
  0.7 0.1 collective-permute-start
  0.8 0.5 collective-permute-start.1
  1.3 0.0 copy-start.6
  1.3 0.9 %copy-done.6 = s32[2,4,4096]{2,1,0:T(4,128)S(1)} copy-done((s32[2,4,4096]{2,1,0:T(4,128)S(1)}, s32[2,4,4096]{2,1,0:T(4,128)}, u32[]{:S(2)}) %copy-start.6) | copy-done | bytes 131096
  2.2 0.0 copy-start.2
  2.2 0.6 copy-done.2
  2.8 11.4 %all-to-all-start = ((s16[32,8,128]{2,1,0:T(8,128)(2,1)}), s16[32,8,128]{2,1,0:T(8,128)(2,1)}, u32[]{:S(2)}, u32[]{:S(2)}) async-start(s16[32,8,128]{2,1,0:T(8,128)(2,1)} %copy-done.2), calls=%async_computation | async-start | bytes 131072 | tf_op jit(solution)/shard_map/all_to_all | solution.py:229
  14.2 0.0 collective-permute-done.px
  14.2 0.0 collective-permute-done.1.pup
  14.3 0.0 copy-done
  14.3 0.0 copy-done.1
  14.3 0.0 copy-done.3
  14.3 6.6 %dense.1 = (bf16[4,32,6912]{2,1,0:T(8,128)(2,1)}, bf16[256,3328]{1,0:T(8,128)(2,1)}) custom-call(bf16[128,3456]{1,0:T(8,128)(2,1)S(1)} %copy-done, bf16[128,3456]{1,0:T(8,128)(2,1)S(1)} %collective-permute-done.px, bf16[128,3456]{1,0:T(8,128)(2,1)S(1)} %copy-done.1, bf16[128,3456]{1,0:T(8,128)(2,1)S(1)} %collective-permute-done.1.pup, ...), custom_call_target="tpu_custom_call" | custom-call | flops 1358954496 | bytes 6291456 | tf_op jit(solution)/shard_map/dense/pallas_call | solution.py:35
  20.9 2.5 %all-to-all-done.ids = s16[32,8,128]{2,1,0:T(8,128)(2,1)} async-done(((s16[32,8,128]{2,1,0:T(8,128)(2,1)}), s16[32,8,128]{2,1,0:T(8,128)(2,1)}, u32[]{:S(2)}, u32[]{:S(2)}) %all-to-all-start) | async-done | bytes 65568 | tf_op jit(solution)/shard_map/all_to_all | solution.py:229
  23.4 0.0 copy-start.4
  23.4 4.4 %all-to-all-start.1 = ((bf16[4,32,6912]{2,1,0:T(8,128)(2,1)}), bf16[4,32,6912]{2,1,0:T(8,128)(2,1)S(1)}, u32[]{:S(2)}, u32[]{:S(2)}) async-start(bf16[4,32,6912]{2,1,0:T(8,128)(2,1)} %get-tuple-element.15), calls=%async_computation.1 | async-start | bytes 3538944 | tf_op jit(solution)/shard_map/all_to_all | solution.py:257
  27.8 0.0 copy-start.5
  27.8 0.0 collective-permute-start.2
  27.8 0.0 copy-done.4
  27.8 1.7 %counts.1.mine = bf16[26,128,128]{2,1,0:T(8,128)(2,1)S(1)} custom-call(s32[26]{0:T(128)S(1)} %copy-done.4, s16[32,8,128]{2,1,0:T(8,128)(2,1)} %all-to-all-done.ids), custom_call_target="tpu_custom_call" | custom-call | flops 1073741824 | bytes 1048576 | tf_op jit(solution)/shard_map/counts/pallas_call | solution.py:35
  29.6 0.0 collective-permute-done.2.pids
  29.6 0.0 copy-done.5
  29.6 1.7 %tables.1 = (f32[26,32,128]{2,1,0:T(8,128)S(1)}, bf16[26,32,128]{2,1,0:T(8,128)(2,1)S(1)}, bf16[26,32,128]{2,1,0:T(8,128)(2,1)S(1)}, bf16[26,32,128]{2,1,0:T(8,128)(2,1)S(1)}) custom-call(s32[26]{0:T(128)S(1)} %copy-done.4, bf16[26,128,128]{2,1,0:T(8,128)(2,1)S(1)} %counts.1.mine, bf16[256,3328]{1,0:T(8,128)(2,1)S(1)} %copy-done.5, ...), custom_call_target="tpu_custom_call" | custom-call | flops 1358954496 | bytes 9437184 | tf_op jit(solution)/shard_map/tables/pallas_call | solution.py:35
  31.3 0.7 collective-permute-start.3
  32.0 2.0 %collective-permute-start.4 = (bf16[26,32,128]{2,1,0:T(8,128)(2,1)S(1)}, bf16[26,32,128]{2,1,0:T(8,128)(2,1)S(1)}, u32[]{:S(2)}, u32[]{:S(2)}) collective-permute-start(bf16[26,32,128]{2,1,0:T(8,128)(2,1)S(1)} %get-tuple-element.20), channel_id=1, source_target_pairs={{0,16},{8,24},{16,0},{24,8},{1,17},{9,25},{17,1},{25,9},{2,18},{10... | collective-permute-start | bytes 638984 | tf_op jit(solution)/shard_map/ppermute | solution.py:217
  34.0 1.3 %collective-permute-start.5 = (bf16[26,32,128]{2,1,0:T(8,128)(2,1)S(1)}, bf16[26,32,128]{2,1,0:T(8,128)(2,1)S(1)}, u32[]{:S(2)}, u32[]{:S(2)}) collective-permute-start(bf16[26,32,128]{2,1,0:T(8,128)(2,1)S(1)} %get-tuple-element.21), channel_id=1, source_target_pairs={{0,24},{8,0},{16,8},{24,16},{1,25},{9,1},{17,9},{25,17},{2,26},{10... | collective-permute-start | bytes 638984 | tf_op jit(solution)/shard_map/ppermute | solution.py:217
  35.3 9.4 %collective-permute-done.3.refs_1_ = bf16[26,32,128]{2,1,0:T(8,128)(2,1)S(1)} collective-permute-done((bf16[26,32,128]{2,1,0:T(8,128)(2,1)S(1)}, bf16[26,32,128]{2,1,0:T(8,128)(2,1)S(1)}, u32[]{:S(2)}, u32[]{:S(2)}) %collective-permute-start.3) | collective-permute-done | bytes 213024 | tf_op jit(solution)/shard_map/ppermute | solution.py:217
  44.6 0.0 collective-permute-done.4.refs_2_
  44.6 0.6 collective-permute-done.5.refs_3_
  45.3 0.1 table_second.1
  45.4 2.1 %collective-permute-start.6 = (bf16[26,8,128]{2,1,0:T(8,128)(2,1)S(1)}, bf16[26,8,128]{2,1,0:T(8,128)(2,1)S(1)}, u32[]{:S(2)}, u32[]{:S(2)}) collective-permute-start(bf16[26,8,128]{2,1,0:T(8,128)(2,1)S(1)} %get-tuple-element.23), channel_id=1, source_target_pairs={{0,64},{64,128},{128,192},{192,0},{1,65},{65,129},{129,193},{193,1... | collective-permute-start | bytes 159752 | tf_op jit(solution)/shard_map/ppermute | solution.py:217
  47.5 2.7 %collective-permute-start.7 = (bf16[26,8,128]{2,1,0:T(8,128)(2,1)S(1)}, bf16[26,8,128]{2,1,0:T(8,128)(2,1)S(1)}, u32[]{:S(2)}, u32[]{:S(2)}) collective-permute-start(bf16[26,8,128]{2,1,0:T(8,128)(2,1)S(1)} %get-tuple-element.24), channel_id=1, source_target_pairs={{0,128},{64,192},{128,0},{192,64},{1,129},{65,193},{129,1},{193,65... | collective-permute-start | bytes 159752 | tf_op jit(solution)/shard_map/ppermute | solution.py:217
  50.1 1.5 %collective-permute-start.8 = (bf16[26,8,128]{2,1,0:T(8,128)(2,1)S(1)}, bf16[26,8,128]{2,1,0:T(8,128)(2,1)S(1)}, u32[]{:S(2)}, u32[]{:S(2)}) collective-permute-start(bf16[26,8,128]{2,1,0:T(8,128)(2,1)S(1)} %get-tuple-element.25), channel_id=1, source_target_pairs={{0,192},{64,0},{128,64},{192,128},{1,193},{65,1},{129,65},{193,129... | collective-permute-start | bytes 159752 | tf_op jit(solution)/shard_map/ppermute | solution.py:217
  51.6 0.0 all-to-all-done.1.came
  51.6 0.6 cross_sum.1.cross
  52.3 0.0 collective-permute-done.6.refs_1_
  52.3 0.8 %collective-permute-done.7.refs_2_ = bf16[26,8,128]{2,1,0:T(8,128)(2,1)S(1)} collective-permute-done((bf16[26,8,128]{2,1,0:T(8,128)(2,1)S(1)}, bf16[26,8,128]{2,1,0:T(8,128)(2,1)S(1)}, u32[]{:S(2)}, u32[]{:S(2)}) %collective-permute-start.7) | collective-permute-done | bytes 53280 | tf_op jit(solution)/shard_map/ppermute | solution.py:217
  53.1 1.2 %collective-permute-done.8.refs_3_ = bf16[26,8,128]{2,1,0:T(8,128)(2,1)S(1)} collective-permute-done((bf16[26,8,128]{2,1,0:T(8,128)(2,1)S(1)}, bf16[26,8,128]{2,1,0:T(8,128)(2,1)S(1)}, u32[]{:S(2)}, u32[]{:S(2)}) %collective-permute-start.8) | collective-permute-done | bytes 53280 | tf_op jit(solution)/shard_map/ppermute | solution.py:217
  54.3 0.8 route.1
  55.1 24.4 %all_to_all.15.came = bf16[32,70,128]{2,1,0:T(8,128)(2,1)S(1)} all-to-all(bf16[32,70,128]{2,1,0:T(8,128)(2,1)S(1)} %route.1), channel_id=1, replica_groups=mesh['x'=4,'c'=2,'y'=4,'z'=8] {'y','z'}, dimensions={0} | all-to-all | bytes 1146880 | tf_op jit(solution)/shard_map/all_to_all | solution.py:317
  79.4 0.7 last.1
  (1 shorter events, 0.0 us)
Async XLA Ops:
  0.6 13.6 %copy-start = (bf16[128,3456]{1,0:T(8,128)(2,1)S(1)}, bf16[128,3456]{1,0:T(8,128)(2,1)}, u32[]{:S(2)}) copy-start(bf16[128,3456]{1,0:T(8,128)(2,1)} %x.1) | copy-start | bytes 2654212
  0.6 13.6 %copy-start.1 = (bf16[128,3456]{1,0:T(8,128)(2,1)S(1)}, bf16[128,3456]{1,0:T(8,128)(2,1)}, u32[]{:S(2)}) copy-start(bf16[128,3456]{1,0:T(8,128)(2,1)} %up.1) | copy-start | bytes 2654212
  0.7 13.6 %copy-start.3 = (f32[3456]{0:T(1024)S(1)}, f32[3456]{0:T(1024)}, u32[]{:S(2)}) copy-start(f32[3456]{0:T(1024)} %bias.1) | copy-start | bytes 41476
  0.7 13.6 %collective-permute-start = (bf16[128,3456]{1,0:T(8,128)(2,1)}, bf16[128,3456]{1,0:T(8,128)(2,1)S(1)}, u32[]{:S(2)}, u32[]{:S(2)}) collective-permute-start(bf16[128,3456]{1,0:T(8,128)(2,1)} %x.1), channel_id=1, source_target_pairs={{0,32},{32,0},{1,33},{33,1},{2,34},{34,2},{3,35},{35,3},{4,36},{36... | collective-permute-start | bytes 2654216 | tf_op jit(solution)/shard_map/ppermute | solution.py:225
  0.8 13.5 %collective-permute-start.1 = (bf16[128,3456]{1,0:T(8,128)(2,1)}, bf16[128,3456]{1,0:T(8,128)(2,1)S(1)}, u32[]{:S(2)}, u32[]{:S(2)}) collective-permute-start(bf16[128,3456]{1,0:T(8,128)(2,1)} %up.1), channel_id=1, source_target_pairs={{0,32},{32,0},{1,33},{33,1},{2,34},{34,2},{3,35},{35,3},{4,36},{36... | collective-permute-start | bytes 2654216 | tf_op jit(solution)/shard_map/ppermute | solution.py:226
  1.3 0.9 %copy-start.6 = (s32[2,4,4096]{2,1,0:T(4,128)S(1)}, s32[2,4,4096]{2,1,0:T(4,128)}, u32[]{:S(2)}) copy-start(s32[2,4,4096]{2,1,0:T(4,128)} %ids.3) | copy-start | bytes 393220
  2.2 0.6 copy-start.2
  2.8 20.6 %all-to-all-start = ((s16[32,8,128]{2,1,0:T(8,128)(2,1)}), s16[32,8,128]{2,1,0:T(8,128)(2,1)}, u32[]{:S(2)}, u32[]{:S(2)}) async-start(s16[32,8,128]{2,1,0:T(8,128)(2,1)} %copy-done.2), calls=%async_computation | async-start | bytes 131072 | tf_op jit(solution)/shard_map/all_to_all | solution.py:229
  23.4 4.4 %copy-start.4 = (s32[26]{0:T(128)S(1)}, s32[26]{0:T(128)}, u32[]{:S(2)}) copy-start(s32[26]{0:T(128)} %placement.5) | copy-start | bytes 316
  23.4 28.2 %all-to-all-start.1 = ((bf16[4,32,6912]{2,1,0:T(8,128)(2,1)}), bf16[4,32,6912]{2,1,0:T(8,128)(2,1)S(1)}, u32[]{:S(2)}, u32[]{:S(2)}) async-start(bf16[4,32,6912]{2,1,0:T(8,128)(2,1)} %get-tuple-element.15), calls=%async_computation.1 | async-start | bytes 3538944 | tf_op jit(solution)/shard_map/all_to_all | solution.py:257
  27.8 1.7 %copy-start.5 = (bf16[256,3328]{1,0:T(8,128)(2,1)S(1)}, bf16[256,3328]{1,0:T(8,128)(2,1)}, u32[]{:S(2)}) copy-start(bf16[256,3328]{1,0:T(8,128)(2,1)} %get-tuple-element.17.pooled) | copy-start | bytes 5111812
  27.8 1.7 %collective-permute-start.2 = (s16[32,8,128]{2,1,0:T(8,128)(2,1)}, s16[32,8,128]{2,1,0:T(8,128)(2,1)S(1)}, u32[]{:S(2)}, u32[]{:S(2)}) collective-permute-start(s16[32,8,128]{2,1,0:T(8,128)(2,1)} %all-to-all-done.ids), channel_id=1, source_target_pairs={{0,32},{32,0},{1,33},{33,1},{2,34},{34,2},{3,35},{35,3},{4,36},{36... | collective-permute-start | bytes 196616 | tf_op jit(solution)/shard_map/ppermute | solution.py:258
  31.3 13.4 %collective-permute-start.3 = (bf16[26,32,128]{2,1,0:T(8,128)(2,1)S(1)}, bf16[26,32,128]{2,1,0:T(8,128)(2,1)S(1)}, u32[]{:S(2)}, u32[]{:S(2)}) collective-permute-start(bf16[26,32,128]{2,1,0:T(8,128)(2,1)S(1)} %get-tuple-element.19), channel_id=1, source_target_pairs={{0,8},{8,16},{16,24},{24,0},{1,9},{9,17},{17,25},{25,1},{2,10},{10... | collective-permute-start | bytes 638984 | tf_op jit(solution)/shard_map/ppermute | solution.py:217
  32.0 12.7 %collective-permute-start.4 = (bf16[26,32,128]{2,1,0:T(8,128)(2,1)S(1)}, bf16[26,32,128]{2,1,0:T(8,128)(2,1)S(1)}, u32[]{:S(2)}, u32[]{:S(2)}) collective-permute-start(bf16[26,32,128]{2,1,0:T(8,128)(2,1)S(1)} %get-tuple-element.20), channel_id=1, source_target_pairs={{0,16},{8,24},{16,0},{24,8},{1,17},{9,25},{17,1},{25,9},{2,18},{10... | collective-permute-start | bytes 638984 | tf_op jit(solution)/shard_map/ppermute | solution.py:217
  34.0 11.3 %collective-permute-start.5 = (bf16[26,32,128]{2,1,0:T(8,128)(2,1)S(1)}, bf16[26,32,128]{2,1,0:T(8,128)(2,1)S(1)}, u32[]{:S(2)}, u32[]{:S(2)}) collective-permute-start(bf16[26,32,128]{2,1,0:T(8,128)(2,1)S(1)} %get-tuple-element.21), channel_id=1, source_target_pairs={{0,24},{8,0},{16,8},{24,16},{1,25},{9,1},{17,9},{25,17},{2,26},{10... | collective-permute-start | bytes 638984 | tf_op jit(solution)/shard_map/ppermute | solution.py:217
  45.4 6.9 %collective-permute-start.6 = (bf16[26,8,128]{2,1,0:T(8,128)(2,1)S(1)}, bf16[26,8,128]{2,1,0:T(8,128)(2,1)S(1)}, u32[]{:S(2)}, u32[]{:S(2)}) collective-permute-start(bf16[26,8,128]{2,1,0:T(8,128)(2,1)S(1)} %get-tuple-element.23), channel_id=1, source_target_pairs={{0,64},{64,128},{128,192},{192,0},{1,65},{65,129},{129,193},{193,1... | collective-permute-start | bytes 159752 | tf_op jit(solution)/shard_map/ppermute | solution.py:217
  47.5 5.6 %collective-permute-start.7 = (bf16[26,8,128]{2,1,0:T(8,128)(2,1)S(1)}, bf16[26,8,128]{2,1,0:T(8,128)(2,1)S(1)}, u32[]{:S(2)}, u32[]{:S(2)}) collective-permute-start(bf16[26,8,128]{2,1,0:T(8,128)(2,1)S(1)} %get-tuple-element.24), channel_id=1, source_target_pairs={{0,128},{64,192},{128,0},{192,64},{1,129},{65,193},{129,1},{193,65... | collective-permute-start | bytes 159752 | tf_op jit(solution)/shard_map/ppermute | solution.py:217
  50.1 4.1 %collective-permute-start.8 = (bf16[26,8,128]{2,1,0:T(8,128)(2,1)S(1)}, bf16[26,8,128]{2,1,0:T(8,128)(2,1)S(1)}, u32[]{:S(2)}, u32[]{:S(2)}) collective-permute-start(bf16[26,8,128]{2,1,0:T(8,128)(2,1)S(1)} %get-tuple-element.25), channel_id=1, source_target_pairs={{0,192},{64,0},{128,64},{192,128},{1,193},{65,1},{129,65},{193,129... | collective-permute-start | bytes 159752 | tf_op jit(solution)/shard_map/ppermute | solution.py:217

commit v10 on v9

--- a/solution.py
+++ b/solution.py
@@ -58,7 +58,7 @@
     return jnp.concatenate(picks, axis=0)
 
 
-def dense_kernel(x, px, up, pup, v_in, u_in, bias, out, pooled, both, prod, v, u, held, held_p, in_sems, sems):
+def dense_kernel(v, x, px, up, pup_in, u_in, bias, out, pooled, both, prod, pup, u, held, held_p, in_sems, sems):
     n, width = x.shape
     core = lax.axis_index("c")
     step = 1152
@@ -86,17 +86,22 @@
                 held[i, :, cols] = total[i * NJ : (i + 1) * NJ].astype(BF)
             send(held.at[:, :, cols], out.at[:, :, cols])
 
-    loads = load(v_in, v, 0)
+    loads = [
+        pltpu.make_async_copy(px, both.at[n:], in_sems.at[2]),
+        pltpu.make_async_copy(pup_in, pup, in_sems.at[3]),
+    ]
+    for part in loads:
+        part.start()
+    later = load(u_in, u, 0)
     both[:n] = x[...]
-    both[n:] = px[...]
     prod[:n] = (x[...].astype(F32) * up[...].astype(F32)).astype(BF)
-    prod[n:] = (px[...].astype(F32) * pup[...].astype(F32)).astype(BF)
-    for part in loads:
-        part.wait()
-    loads = load(u_in, u, 2)
-    hid = nt(v[...], both[...]).astype(BF)
+    hid_x = nt(v[...], x[...])
+    loads[0].wait()
+    hid = jnp.concatenate([hid_x, nt(v[...], both[n:])], axis=1).astype(BF)
+    loads[1].wait()
+    prod[n:] = (both[n:].astype(F32) * pup[...].astype(F32)).astype(BF)
     half(own_rows(hid.astype(F32), core).astype(BF), prod, 0)
-    for part in loads:
+    for part in later:
         part.wait()
     hgr = nt(u[...], prod[...]).astype(BF)
     half(own_rows(hgr.astype(F32), core).astype(BF), both, width)
@@ -232,24 +237,24 @@
         dense_kernel,
         "dense",
         [((NX, NJ, 2 * width), BF), ((2 * samples, TABLES * EMB), BF)],
+        v_weight,
         cross_input,
         px,
         upstream,
         pup,
-        v_weight,
         u_weight,
         bias,
-        specs=[VMEM] * 4 + [HBM] * 2 + [VMEM],
+        specs=[VMEM, VMEM, HBM, VMEM, HBM, HBM, VMEM],
         out_specs=[HBM] * 2,
         scratch=[pltpu.VMEM((2 * samples, width), BF)] * 2
-        + [pltpu.VMEM((RANK, width), BF)] * 2
+        + [pltpu.VMEM((samples, width), BF), pltpu.VMEM((RANK, width), BF)]
         + [
             pltpu.VMEM((NX, NJ, 2 * width), BF),
             pltpu.VMEM((2 * samples, TABLES * EMB), BF),
             pltpu.SemaphoreType.DMA((4,)),
             pltpu.SemaphoreType.DMA((10,)),
         ],
-        vmem=50 << 20,
+        vmem=45 << 20,
         flops=6 * 256 * 256 * width,
         size=6 << 20,
     )

time: 80.5 us -> 82 us (1.019)
  local copies, waits for them, and re-layouts: 1.54 us -> 3.05 us
  waiting for transfers between devices: 14.5 us -> 13.1 us
  blocking collectives: 24.4 us -> 25.6 us
    unnamed x14 -> x18, local copies, waits for them, and re-layouts: 1.54 us -> 3.05 us
    all_to_all x1, blocking collectives: 24.4 us -> 25.6 us  [on_device(): routed = lax.all_to_all(routed, ('y', 'z'), 0, 0, tiled=True)]
    all_to_all x1, waiting for transfers between devices: 2.48 us -> 1.38 us  [on_device(): ids = lax.all_to_all(ids, ('y', 'z'), 0, 0, tiled=True)]
where the time goes in v10:
time: 82 us; the launch traced here: 81.7 us
  starting transfers between devices  27 us (33%)
  blocking collectives  25.6 us (31%)
  waiting for transfers between devices  13.1 us (16%)
  Pallas kernels  12.1 us (15%)
  local copies, waits for them, and re-layouts  3.05 us (4%)
    all_to_all x1, blocking collectives, on_device(): routed = lax.all_to_all(routed, ('y', 'z'), 0, 0, tiled=True)  25.6 us
    pallas_call x8, Pallas kernels, call(): pl.pallas_call(kernel, out_shape=tuple((jax.ShapeDtypeStruct(shape, dtype...  12.1 us
    ppermute x6, waiting for transfers between devices, shift(): lax.ppermute(chunks[d], axis, [(i, (i + d) % n) for i in range(n)])  11.7 us
    all_to_all x1, starting transfers between devices, on_device(): ids = lax.all_to_all(ids, ('y', 'z'), 0, 0, tiled=True)  11.4 us
    ppermute x6, starting transfers between devices, shift(): lax.ppermute(chunks[d], axis, [(i, (i + d) % n) for i in range(n)])  10.5 us
    all_to_all x1, starting transfers between devices, on_device(): cross = lax.all_to_all(cross, 'x', 0, 0, tiled=True)  4.42 us
    unnamed x18, local copies, waits for them, and re-layouts  3.05 us
  transfers between devices with their start and end apart: 11, of which 5 were waited for; matrix products, arithmetic and copies ran while one was open for 0% of the time, Pallas kernels for 13%

profile of v10, /device:TPU:32, one launch (start us, length us, event | category | flops | bytes accessed | tf_op | source)
XLA Modules:
  0.0 81.7 jit_solution(11189075462309699379)
XLA Ops:
  0.6 0.0 copy-start.1
  0.6 0.0 copy-start.2
  0.7 0.0 copy-start.4
  0.7 0.0 copy-start
  0.7 0.1 collective-permute-start
  0.8 0.5 collective-permute-start.1
  1.3 0.0 copy-start.8
  1.3 1.2 %copy-done.8 = s32[2,4,4096]{2,1,0:T(4,128)S(1)} copy-done((s32[2,4,4096]{2,1,0:T(4,128)S(1)}, s32[2,4,4096]{2,1,0:T(4,128)}, u32[]{:S(2)}) %copy-start.8) | copy-done | bytes 131096
  2.5 0.0 copy-start.3
  2.5 0.6 copy-done.3
  3.1 11.4 %all-to-all-start = ((s16[32,8,128]{2,1,0:T(8,128)(2,1)}), s16[32,8,128]{2,1,0:T(8,128)(2,1)}, u32[]{:S(2)}, u32[]{:S(2)}) async-start(s16[32,8,128]{2,1,0:T(8,128)(2,1)} %copy-done.3), calls=%async_computation | async-start | bytes 131072 | tf_op jit(solution)/shard_map/all_to_all | solution.py:234
  14.6 0.0 collective-permute-done.px
  14.6 0.0 collective-permute-done.1.pup_in
  14.6 0.0 copy-done.1
  14.6 0.0 copy-done.2
  14.6 0.0 copy-done.4
  14.6 0.0 copy-done
  14.6 6.5 %dense.1 = (bf16[4,32,6912]{2,1,0:T(8,128)(2,1)}, bf16[256,3328]{1,0:T(8,128)(2,1)S(1)}) custom-call(bf16[256,3456]{1,0:T(8,128)(2,1)S(1)} %copy-done, bf16[128,3456]{1,0:T(8,128)(2,1)S(1)} %copy-done.1, bf16[128,3456]{1,0:T(8,128)(2,1)} %collective-permute-done.px, bf16[128,3456]{1,0:T(8,128)(2,1)S(1)} %copy-done.2, ...), custom_call_target="tpu_custom_call" | custom-call | flops 1358954496 | bytes 6291456 | tf_op jit(solution)/shard_map/dense/pallas_call | solution.py:35
  21.1 0.0 copy-start.6
  21.1 1.2 %copy-done.6 = bf16[256,3328]{1,0:T(8,128)(2,1)} copy-done((bf16[256,3328]{1,0:T(8,128)(2,1)}, bf16[256,3328]{1,0:T(8,128)(2,1)S(1)}, u32[]{:S(2)}) %copy-start.6) | copy-done | bytes 1703960
  22.3 1.4 %all-to-all-done.ids = s16[32,8,128]{2,1,0:T(8,128)(2,1)} async-done(((s16[32,8,128]{2,1,0:T(8,128)(2,1)}), s16[32,8,128]{2,1,0:T(8,128)(2,1)}, u32[]{:S(2)}, u32[]{:S(2)}) %all-to-all-start) | async-done | bytes 65568 | tf_op jit(solution)/shard_map/all_to_all | solution.py:234
  23.7 0.0 copy-start.5
  23.7 4.4 %all-to-all-start.1 = ((bf16[4,32,6912]{2,1,0:T(8,128)(2,1)}), bf16[4,32,6912]{2,1,0:T(8,128)(2,1)S(1)}, u32[]{:S(2)}, u32[]{:S(2)}) async-start(bf16[4,32,6912]{2,1,0:T(8,128)(2,1)} %get-tuple-element.15), calls=%async_computation.1 | async-start | bytes 3538944 | tf_op jit(solution)/shard_map/all_to_all | solution.py:262
  28.1 0.0 copy-start.7
  28.1 0.0 collective-permute-start.2
  28.1 0.0 copy-done.5
  28.1 1.7 %counts.1.mine = bf16[26,128,128]{2,1,0:T(8,128)(2,1)S(1)} custom-call(s32[26]{0:T(128)S(1)} %copy-done.5, s16[32,8,128]{2,1,0:T(8,128)(2,1)} %all-to-all-done.ids), custom_call_target="tpu_custom_call" | custom-call | flops 1073741824 | bytes 1048576 | tf_op jit(solution)/shard_map/counts/pallas_call | solution.py:35
  29.9 0.0 collective-permute-done.2.pids
  29.9 0.0 copy-done.7
  29.9 1.7 %tables.1 = (f32[26,32,128]{2,1,0:T(8,128)S(1)}, bf16[26,32,128]{2,1,0:T(8,128)(2,1)S(1)}, bf16[26,32,128]{2,1,0:T(8,128)(2,1)S(1)}, bf16[26,32,128]{2,1,0:T(8,128)(2,1)S(1)}) custom-call(s32[26]{0:T(128)S(1)} %copy-done.5, bf16[26,128,128]{2,1,0:T(8,128)(2,1)S(1)} %counts.1.mine, bf16[256,3328]{1,0:T(8,128)(2,1)S(1)} %copy-done.7, ...), custom_call_target="tpu_custom_call" | custom-call | flops 1358954496 | bytes 9437184 | tf_op jit(solution)/shard_map/tables/pallas_call | solution.py:35
  31.6 0.7 collective-permute-start.3
  32.3 2.2 %collective-permute-start.4 = (bf16[26,32,128]{2,1,0:T(8,128)(2,1)S(1)}, bf16[26,32,128]{2,1,0:T(8,128)(2,1)S(1)}, u32[]{:S(2)}, u32[]{:S(2)}) collective-permute-start(bf16[26,32,128]{2,1,0:T(8,128)(2,1)S(1)} %get-tuple-element.20), channel_id=1, source_target_pairs={{0,16},{8,24},{16,0},{24,8},{1,17},{9,25},{17,1},{25,9},{2,18},{10... | collective-permute-start | bytes 638984 | tf_op jit(solution)/shard_map/ppermute | solution.py:222
  34.5 1.4 %collective-permute-start.5 = (bf16[26,32,128]{2,1,0:T(8,128)(2,1)S(1)}, bf16[26,32,128]{2,1,0:T(8,128)(2,1)S(1)}, u32[]{:S(2)}, u32[]{:S(2)}) collective-permute-start(bf16[26,32,128]{2,1,0:T(8,128)(2,1)S(1)} %get-tuple-element.21), channel_id=1, source_target_pairs={{0,24},{8,0},{16,8},{24,16},{1,25},{9,1},{17,9},{25,17},{2,26},{10... | collective-permute-start | bytes 638984 | tf_op jit(solution)/shard_map/ppermute | solution.py:222
  35.9 9.1 %collective-permute-done.3.refs_1_ = bf16[26,32,128]{2,1,0:T(8,128)(2,1)S(1)} collective-permute-done((bf16[26,32,128]{2,1,0:T(8,128)(2,1)S(1)}, bf16[26,32,128]{2,1,0:T(8,128)(2,1)S(1)}, u32[]{:S(2)}, u32[]{:S(2)}) %collective-permute-start.3) | collective-permute-done | bytes 213024 | tf_op jit(solution)/shard_map/ppermute | solution.py:222
  44.9 0.0 collective-permute-done.4.refs_2_
  44.9 0.6 collective-permute-done.5.refs_3_
  45.6 0.1 table_second.1
  45.7 2.1 %collective-permute-start.6 = (bf16[26,8,128]{2,1,0:T(8,128)(2,1)S(1)}, bf16[26,8,128]{2,1,0:T(8,128)(2,1)S(1)}, u32[]{:S(2)}, u32[]{:S(2)}) collective-permute-start(bf16[26,8,128]{2,1,0:T(8,128)(2,1)S(1)} %get-tuple-element.23), channel_id=1, source_target_pairs={{0,64},{64,128},{128,192},{192,0},{1,65},{65,129},{129,193},{193,1... | collective-permute-start | bytes 159752 | tf_op jit(solution)/shard_map/ppermute | solution.py:222
  47.8 2.7 %collective-permute-start.7 = (bf16[26,8,128]{2,1,0:T(8,128)(2,1)S(1)}, bf16[26,8,128]{2,1,0:T(8,128)(2,1)S(1)}, u32[]{:S(2)}, u32[]{:S(2)}) collective-permute-start(bf16[26,8,128]{2,1,0:T(8,128)(2,1)S(1)} %get-tuple-element.24), channel_id=1, source_target_pairs={{0,128},{64,192},{128,0},{192,64},{1,129},{65,193},{129,1},{193,65... | collective-permute-start | bytes 159752 | tf_op jit(solution)/shard_map/ppermute | solution.py:222
  50.4 1.5 %collective-permute-start.8 = (bf16[26,8,128]{2,1,0:T(8,128)(2,1)S(1)}, bf16[26,8,128]{2,1,0:T(8,128)(2,1)S(1)}, u32[]{:S(2)}, u32[]{:S(2)}) collective-permute-start(bf16[26,8,128]{2,1,0:T(8,128)(2,1)S(1)} %get-tuple-element.25), channel_id=1, source_target_pairs={{0,192},{64,0},{128,64},{192,128},{1,193},{65,1},{129,65},{193,129... | collective-permute-start | bytes 159752 | tf_op jit(solution)/shard_map/ppermute | solution.py:222
  51.9 0.0 all-to-all-done.1.came
  51.9 0.6 cross_sum.1.cross
  52.6 0.0 collective-permute-done.6.refs_1_
  52.6 0.8 %collective-permute-done.7.refs_2_ = bf16[26,8,128]{2,1,0:T(8,128)(2,1)S(1)} collective-permute-done((bf16[26,8,128]{2,1,0:T(8,128)(2,1)S(1)}, bf16[26,8,128]{2,1,0:T(8,128)(2,1)S(1)}, u32[]{:S(2)}, u32[]{:S(2)}) %collective-permute-start.7) | collective-permute-done | bytes 53280 | tf_op jit(solution)/shard_map/ppermute | solution.py:222
  53.4 1.2 %collective-permute-done.8.refs_3_ = bf16[26,8,128]{2,1,0:T(8,128)(2,1)S(1)} collective-permute-done((bf16[26,8,128]{2,1,0:T(8,128)(2,1)S(1)}, bf16[26,8,128]{2,1,0:T(8,128)(2,1)S(1)}, u32[]{:S(2)}, u32[]{:S(2)}) %collective-permute-start.8) | collective-permute-done | bytes 53280 | tf_op jit(solution)/shard_map/ppermute | solution.py:222
  54.6 0.8 route.1
  55.4 25.6 %all_to_all.15.came = bf16[32,70,128]{2,1,0:T(8,128)(2,1)S(1)} all-to-all(bf16[32,70,128]{2,1,0:T(8,128)(2,1)S(1)} %route.1), channel_id=1, replica_groups=mesh['x'=4,'c'=2,'y'=4,'z'=8] {'y','z'}, dimensions={0} | all-to-all | bytes 1146880 | tf_op jit(solution)/shard_map/all_to_all | solution.py:322
  80.9 0.7 last.1
  (1 shorter events, 0.0 us)
Async XLA Ops:
  0.6 14.0 %copy-start.1 = (bf16[128,3456]{1,0:T(8,128)(2,1)S(1)}, bf16[128,3456]{1,0:T(8,128)(2,1)}, u32[]{:S(2)}) copy-start(bf16[128,3456]{1,0:T(8,128)(2,1)} %x.1) | copy-start | bytes 2654212
  0.6 14.0 %copy-start.2 = (bf16[128,3456]{1,0:T(8,128)(2,1)S(1)}, bf16[128,3456]{1,0:T(8,128)(2,1)}, u32[]{:S(2)}) copy-start(bf16[128,3456]{1,0:T(8,128)(2,1)} %up.1) | copy-start | bytes 2654212
  0.7 14.0 %copy-start.4 = (f32[3456]{0:T(1024)S(1)}, f32[3456]{0:T(1024)}, u32[]{:S(2)}) copy-start(f32[3456]{0:T(1024)} %bias.1) | copy-start | bytes 41476
  0.7 14.0 %copy-start = (bf16[256,3456]{1,0:T(8,128)(2,1)S(1)}, bf16[256,3456]{1,0:T(8,128)(2,1)}, u32[]{:S(2)}) copy-start(bf16[256,3456]{1,0:T(8,128)(2,1)} %v.1) | copy-start | bytes 5308420
  0.7 13.9 %collective-permute-start = (bf16[128,3456]{1,0:T(8,128)(2,1)}, bf16[128,3456]{1,0:T(8,128)(2,1)}, u32[]{:S(2)}, u32[]{:S(2)}) collective-permute-start(bf16[128,3456]{1,0:T(8,128)(2,1)} %x.1), channel_id=1, source_target_pairs={{0,32},{32,0},{1,33},{33,1},{2,34},{34,2},{3,35},{35,3},{4,36},{36... | collective-permute-start | bytes 2654216 | tf_op jit(solution)/shard_map/ppermute | solution.py:230
  0.8 13.8 %collective-permute-start.1 = (bf16[128,3456]{1,0:T(8,128)(2,1)}, bf16[128,3456]{1,0:T(8,128)(2,1)}, u32[]{:S(2)}, u32[]{:S(2)}) collective-permute-start(bf16[128,3456]{1,0:T(8,128)(2,1)} %up.1), channel_id=1, source_target_pairs={{0,32},{32,0},{1,33},{33,1},{2,34},{34,2},{3,35},{35,3},{4,36},{36... | collective-permute-start | bytes 2654216 | tf_op jit(solution)/shard_map/ppermute | solution.py:231
  1.3 1.2 %copy-start.8 = (s32[2,4,4096]{2,1,0:T(4,128)S(1)}, s32[2,4,4096]{2,1,0:T(4,128)}, u32[]{:S(2)}) copy-start(s32[2,4,4096]{2,1,0:T(4,128)} %ids.3) | copy-start | bytes 393220
  2.5 0.6 copy-start.3
  3.1 20.6 %all-to-all-start = ((s16[32,8,128]{2,1,0:T(8,128)(2,1)}), s16[32,8,128]{2,1,0:T(8,128)(2,1)}, u32[]{:S(2)}, u32[]{:S(2)}) async-start(s16[32,8,128]{2,1,0:T(8,128)(2,1)} %copy-done.3), calls=%async_computation | async-start | bytes 131072 | tf_op jit(solution)/shard_map/all_to_all | solution.py:234
  21.1 1.2 %copy-start.6 = (bf16[256,3328]{1,0:T(8,128)(2,1)}, bf16[256,3328]{1,0:T(8,128)(2,1)S(1)}, u32[]{:S(2)}) copy-start(bf16[256,3328]{1,0:T(8,128)(2,1)S(1)} %get-tuple-element.17.pooled) | copy-start | bytes 5111812
  23.7 4.4 %copy-start.5 = (s32[26]{0:T(128)S(1)}, s32[26]{0:T(128)}, u32[]{:S(2)}) copy-start(s32[26]{0:T(128)} %placement.5) | copy-start | bytes 316
  23.7 28.2 %all-to-all-start.1 = ((bf16[4,32,6912]{2,1,0:T(8,128)(2,1)}), bf16[4,32,6912]{2,1,0:T(8,128)(2,1)S(1)}, u32[]{:S(2)}, u32[]{:S(2)}) async-start(bf16[4,32,6912]{2,1,0:T(8,128)(2,1)} %get-tuple-element.15), calls=%async_computation.1 | async-start | bytes 3538944 | tf_op jit(solution)/shard_map/all_to_all | solution.py:262
  28.1 1.7 %copy-start.7 = (bf16[256,3328]{1,0:T(8,128)(2,1)S(1)}, bf16[256,3328]{1,0:T(8,128)(2,1)}, u32[]{:S(2)}) copy-start(bf16[256,3328]{1,0:T(8,128)(2,1)} %copy-done.6) | copy-start | bytes 5111812
  28.1 1.7 %collective-permute-start.2 = (s16[32,8,128]{2,1,0:T(8,128)(2,1)}, s16[32,8,128]{2,1,0:T(8,128)(2,1)S(1)}, u32[]{:S(2)}, u32[]{:S(2)}) collective-permute-start(s16[32,8,128]{2,1,0:T(8,128)(2,1)} %all-to-all-done.ids), channel_id=1, source_target_pairs={{0,32},{32,0},{1,33},{33,1},{2,34},{34,2},{3,35},{35,3},{4,36},{36... | collective-permute-start | bytes 196616 | tf_op jit(solution)/shard_map/ppermute | solution.py:263
  31.6 13.4 %collective-permute-start.3 = (bf16[26,32,128]{2,1,0:T(8,128)(2,1)S(1)}, bf16[26,32,128]{2,1,0:T(8,128)(2,1)S(1)}, u32[]{:S(2)}, u32[]{:S(2)}) collective-permute-start(bf16[26,32,128]{2,1,0:T(8,128)(2,1)S(1)} %get-tuple-element.19), channel_id=1, source_target_pairs={{0,8},{8,16},{16,24},{24,0},{1,9},{9,17},{17,25},{25,1},{2,10},{10... | collective-permute-start | bytes 638984 | tf_op jit(solution)/shard_map/ppermute | solution.py:222
  32.3 12.7 %collective-permute-start.4 = (bf16[26,32,128]{2,1,0:T(8,128)(2,1)S(1)}, bf16[26,32,128]{2,1,0:T(8,128)(2,1)S(1)}, u32[]{:S(2)}, u32[]{:S(2)}) collective-permute-start(bf16[26,32,128]{2,1,0:T(8,128)(2,1)S(1)} %get-tuple-element.20), channel_id=1, source_target_pairs={{0,16},{8,24},{16,0},{24,8},{1,17},{9,25},{17,1},{25,9},{2,18},{10... | collective-permute-start | bytes 638984 | tf_op jit(solution)/shard_map/ppermute | solution.py:222
  34.5 11.1 %collective-permute-start.5 = (bf16[26,32,128]{2,1,0:T(8,128)(2,1)S(1)}, bf16[26,32,128]{2,1,0:T(8,128)(2,1)S(1)}, u32[]{:S(2)}, u32[]{:S(2)}) collective-permute-start(bf16[26,32,128]{2,1,0:T(8,128)(2,1)S(1)} %get-tuple-element.21), channel_id=1, source_target_pairs={{0,24},{8,0},{16,8},{24,16},{1,25},{9,1},{17,9},{25,17},{2,26},{10... | collective-permute-start | bytes 638984 | tf_op jit(solution)/shard_map/ppermute | solution.py:222
  45.7 6.9 %collective-permute-start.6 = (bf16[26,8,128]{2,1,0:T(8,128)(2,1)S(1)}, bf16[26,8,128]{2,1,0:T(8,128)(2,1)S(1)}, u32[]{:S(2)}, u32[]{:S(2)}) collective-permute-start(bf16[26,8,128]{2,1,0:T(8,128)(2,1)S(1)} %get-tuple-element.23), channel_id=1, source_target_pairs={{0,64},{64,128},{128,192},{192,0},{1,65},{65,129},{129,193},{193,1... | collective-permute-start | bytes 159752 | tf_op jit(solution)/shard_map/ppermute | solution.py:222
  47.8 5.6 %collective-permute-start.7 = (bf16[26,8,128]{2,1,0:T(8,128)(2,1)S(1)}, bf16[26,8,128]{2,1,0:T(8,128)(2,1)S(1)}, u32[]{:S(2)}, u32[]{:S(2)}) collective-permute-start(bf16[26,8,128]{2,1,0:T(8,128)(2,1)S(1)} %get-tuple-element.24), channel_id=1, source_target_pairs={{0,128},{64,192},{128,0},{192,64},{1,129},{65,193},{129,1},{193,65... | collective-permute-start | bytes 159752 | tf_op jit(solution)/shard_map/ppermute | solution.py:222
  50.4 4.1 %collective-permute-start.8 = (bf16[26,8,128]{2,1,0:T(8,128)(2,1)S(1)}, bf16[26,8,128]{2,1,0:T(8,128)(2,1)S(1)}, u32[]{:S(2)}, u32[]{:S(2)}) collective-permute-start(bf16[26,8,128]{2,1,0:T(8,128)(2,1)S(1)} %get-tuple-element.25), channel_id=1, source_target_pairs={{0,192},{64,0},{128,64},{192,128},{1,193},{65,1},{129,65},{193,129... | collective-permute-start | bytes 159752 | tf_op jit(solution)/shard_map/ppermute | solution.py:222

commit v11 on v9

--- a/solution.py
+++ b/solution.py
@@ -133,14 +133,16 @@
     at = lax.broadcasted_iota(I32, (RANK // 2, n), 0)
     row = lax.rem(lax.axis_index("x") + (at // 8) % 4, NX) * 64 + at % 8
     row = row + lax.rem(lax.axis_index("y") + at // 32, NY) * 8 + lax.axis_index("c") * 32
+    row = row.astype(F32).astype(BF)
 
     def count_rows(table, owner, slot):
         eight = state[owner]
-        four = jnp.where(slot == 0, eight[:4], eight[4:])
-        count = jnp.where(four[0:1] == row, 1.0, 0.0)
+        four = jnp.where(slot == 0, eight[:4], eight[4:]).astype(F32).astype(BF)
+        one, none = jnp.ones(row.shape, BF), jnp.zeros(row.shape, BF)
+        count = jnp.where(four[0:1] == row, one, none)
         for k in range(1, 4):
-            count = count + jnp.where(four[k : k + 1] == row, 1.0, 0.0)
-        counts[table] = count.astype(BF)
+            count = count + jnp.where(four[k : k + 1] == row, one, none)
+        counts[table] = count
 
     slots_of(placement, used, count_rows)
 

time: 80.5 us -> 80 us (level)
  no operation moved by 1% of the time
where the time goes in v11:
time: 80 us; the launch traced here: 79.7 us
  starting transfers between devices  26.7 us (33%)
  blocking collectives  24.4 us (30%)
  waiting for transfers between devices  14.5 us (18%)
  Pallas kernels  11.8 us (15%)
  local copies, waits for them, and re-layouts  1.54 us (2%)
  between operations  0.8 us (1%)
    all_to_all x1, blocking collectives, on_device(): routed = lax.all_to_all(routed, ('y', 'z'), 0, 0, tiled=True)  24.4 us
    ppermute x6, waiting for transfers between devices, shift(): lax.ppermute(chunks[d], axis, [(i, (i + d) % n) for i in range(n)])  12 us
    pallas_call x8, Pallas kernels, call(): pl.pallas_call(kernel, out_shape=tuple((jax.ShapeDtypeStruct(shape, dtype...  11.8 us
    all_to_all x1, starting transfers between devices, on_device(): ids = lax.all_to_all(ids, ('y', 'z'), 0, 0, tiled=True)  11.4 us
    ppermute x6, starting transfers between devices, shift(): lax.ppermute(chunks[d], axis, [(i, (i + d) % n) for i in range(n)])  10.2 us
    all_to_all x1, starting transfers between devices, on_device(): cross = lax.all_to_all(cross, 'x', 0, 0, tiled=True)  4.42 us
    all_to_all x1, waiting for transfers between devices, on_device(): ids = lax.all_to_all(ids, ('y', 'z'), 0, 0, tiled=True)  2.48 us
  transfers between devices with their start and end apart: 11, of which 5 were waited for; matrix products, arithmetic and copies ran while one was open for 0% of the time, Pallas kernels for 13%

profile of v11, /device:TPU:32, one launch (start us, length us, event | category | flops | bytes accessed | tf_op | source)
XLA Modules:
  0.0 79.7 jit_solution(11970952497763892132)
XLA Ops:
  0.6 0.0 copy-start
  0.6 0.0 copy-start.1
  0.7 0.0 copy-start.3
  0.7 0.1 collective-permute-start
  0.8 0.5 collective-permute-start.1
  1.3 0.0 copy-start.6
  1.3 0.9 %copy-done.6 = s32[2,4,4096]{2,1,0:T(4,128)S(1)} copy-done((s32[2,4,4096]{2,1,0:T(4,128)S(1)}, s32[2,4,4096]{2,1,0:T(4,128)}, u32[]{:S(2)}) %copy-start.6) | copy-done | bytes 131096
  2.2 0.0 copy-start.2
  2.2 0.6 copy-done.2
  2.8 11.4 %all-to-all-start = ((s16[32,8,128]{2,1,0:T(8,128)(2,1)}), s16[32,8,128]{2,1,0:T(8,128)(2,1)}, u32[]{:S(2)}, u32[]{:S(2)}) async-start(s16[32,8,128]{2,1,0:T(8,128)(2,1)} %copy-done.2), calls=%async_computation | async-start | bytes 131072 | tf_op jit(solution)/shard_map/all_to_all | solution.py:231
  14.2 0.0 collective-permute-done.px
  14.2 0.0 collective-permute-done.1.pup
  14.3 0.0 copy-done
  14.3 0.0 copy-done.1
  14.3 0.0 copy-done.3
  14.3 6.6 %dense.1 = (bf16[4,32,6912]{2,1,0:T(8,128)(2,1)}, bf16[256,3328]{1,0:T(8,128)(2,1)}) custom-call(bf16[128,3456]{1,0:T(8,128)(2,1)S(1)} %copy-done, bf16[128,3456]{1,0:T(8,128)(2,1)S(1)} %collective-permute-done.px, bf16[128,3456]{1,0:T(8,128)(2,1)S(1)} %copy-done.1, bf16[128,3456]{1,0:T(8,128)(2,1)S(1)} %collective-permute-done.1.pup, ...), custom_call_target="tpu_custom_call" | custom-call | flops 1358954496 | bytes 6291456 | tf_op jit(solution)/shard_map/dense/pallas_call | solution.py:35
  20.9 2.5 %all-to-all-done.ids = s16[32,8,128]{2,1,0:T(8,128)(2,1)} async-done(((s16[32,8,128]{2,1,0:T(8,128)(2,1)}), s16[32,8,128]{2,1,0:T(8,128)(2,1)}, u32[]{:S(2)}, u32[]{:S(2)}) %all-to-all-start) | async-done | bytes 65568 | tf_op jit(solution)/shard_map/all_to_all | solution.py:231
  23.4 0.0 copy-start.4
  23.4 4.4 %all-to-all-start.1 = ((bf16[4,32,6912]{2,1,0:T(8,128)(2,1)}), bf16[4,32,6912]{2,1,0:T(8,128)(2,1)S(1)}, u32[]{:S(2)}, u32[]{:S(2)}) async-start(bf16[4,32,6912]{2,1,0:T(8,128)(2,1)} %get-tuple-element.15), calls=%async_computation.1 | async-start | bytes 3538944 | tf_op jit(solution)/shard_map/all_to_all | solution.py:259
  27.8 0.0 copy-start.5
  27.8 0.0 collective-permute-start.2
  27.8 0.0 copy-done.4
  27.8 1.5 %counts.1.mine = bf16[26,128,128]{2,1,0:T(8,128)(2,1)S(1)} custom-call(s32[26]{0:T(128)S(1)} %copy-done.4, s16[32,8,128]{2,1,0:T(8,128)(2,1)} %all-to-all-done.ids), custom_call_target="tpu_custom_call" | custom-call | flops 1073741824 | bytes 1048576 | tf_op jit(solution)/shard_map/counts/pallas_call | solution.py:35
  29.3 0.0 collective-permute-done.2.pids
  29.3 0.0 copy-done.5
  29.3 1.5 %tables.1 = (f32[26,32,128]{2,1,0:T(8,128)S(1)}, bf16[26,32,128]{2,1,0:T(8,128)(2,1)S(1)}, bf16[26,32,128]{2,1,0:T(8,128)(2,1)S(1)}, bf16[26,32,128]{2,1,0:T(8,128)(2,1)S(1)}) custom-call(s32[26]{0:T(128)S(1)} %copy-done.4, bf16[26,128,128]{2,1,0:T(8,128)(2,1)S(1)} %counts.1.mine, bf16[256,3328]{1,0:T(8,128)(2,1)S(1)} %copy-done.5, ...), custom_call_target="tpu_custom_call" | custom-call | flops 1358954496 | bytes 9437184 | tf_op jit(solution)/shard_map/tables/pallas_call | solution.py:35
  30.8 0.7 collective-permute-start.3
  31.5 2.0 %collective-permute-start.4 = (bf16[26,32,128]{2,1,0:T(8,128)(2,1)S(1)}, bf16[26,32,128]{2,1,0:T(8,128)(2,1)S(1)}, u32[]{:S(2)}, u32[]{:S(2)}) collective-permute-start(bf16[26,32,128]{2,1,0:T(8,128)(2,1)S(1)} %get-tuple-element.20), channel_id=1, source_target_pairs={{0,16},{8,24},{16,0},{24,8},{1,17},{9,25},{17,1},{25,9},{2,18},{10... | collective-permute-start | bytes 638984 | tf_op jit(solution)/shard_map/ppermute | solution.py:219
  33.5 1.3 %collective-permute-start.5 = (bf16[26,32,128]{2,1,0:T(8,128)(2,1)S(1)}, bf16[26,32,128]{2,1,0:T(8,128)(2,1)S(1)}, u32[]{:S(2)}, u32[]{:S(2)}) collective-permute-start(bf16[26,32,128]{2,1,0:T(8,128)(2,1)S(1)} %get-tuple-element.21), channel_id=1, source_target_pairs={{0,24},{8,0},{16,8},{24,16},{1,25},{9,1},{17,9},{25,17},{2,26},{10... | collective-permute-start | bytes 638984 | tf_op jit(solution)/shard_map/ppermute | solution.py:219
  34.8 9.4 %collective-permute-done.3.refs_1_ = bf16[26,32,128]{2,1,0:T(8,128)(2,1)S(1)} collective-permute-done((bf16[26,32,128]{2,1,0:T(8,128)(2,1)S(1)}, bf16[26,32,128]{2,1,0:T(8,128)(2,1)S(1)}, u32[]{:S(2)}, u32[]{:S(2)}) %collective-permute-start.3) | collective-permute-done | bytes 213024 | tf_op jit(solution)/shard_map/ppermute | solution.py:219
  44.2 0.0 collective-permute-done.4.refs_2_
  44.2 0.6 collective-permute-done.5.refs_3_
  44.8 0.1 table_second.1
  44.9 2.1 %collective-permute-start.6 = (bf16[26,8,128]{2,1,0:T(8,128)(2,1)S(1)}, bf16[26,8,128]{2,1,0:T(8,128)(2,1)S(1)}, u32[]{:S(2)}, u32[]{:S(2)}) collective-permute-start(bf16[26,8,128]{2,1,0:T(8,128)(2,1)S(1)} %get-tuple-element.23), channel_id=1, source_target_pairs={{0,64},{64,128},{128,192},{192,0},{1,65},{65,129},{129,193},{193,1... | collective-permute-start | bytes 159752 | tf_op jit(solution)/shard_map/ppermute | solution.py:219
  47.0 2.7 %collective-permute-start.7 = (bf16[26,8,128]{2,1,0:T(8,128)(2,1)S(1)}, bf16[26,8,128]{2,1,0:T(8,128)(2,1)S(1)}, u32[]{:S(2)}, u32[]{:S(2)}) collective-permute-start(bf16[26,8,128]{2,1,0:T(8,128)(2,1)S(1)} %get-tuple-element.24), channel_id=1, source_target_pairs={{0,128},{64,192},{128,0},{192,64},{1,129},{65,193},{129,1},{193,65... | collective-permute-start | bytes 159752 | tf_op jit(solution)/shard_map/ppermute | solution.py:219
  49.7 1.5 %collective-permute-start.8 = (bf16[26,8,128]{2,1,0:T(8,128)(2,1)S(1)}, bf16[26,8,128]{2,1,0:T(8,128)(2,1)S(1)}, u32[]{:S(2)}, u32[]{:S(2)}) collective-permute-start(bf16[26,8,128]{2,1,0:T(8,128)(2,1)S(1)} %get-tuple-element.25), channel_id=1, source_target_pairs={{0,192},{64,0},{128,64},{192,128},{1,193},{65,1},{129,65},{193,129... | collective-permute-start | bytes 159752 | tf_op jit(solution)/shard_map/ppermute | solution.py:219
  51.1 0.0 all-to-all-done.1.came
  51.1 0.6 cross_sum.1.cross
  51.8 0.0 collective-permute-done.6.refs_1_
  51.8 0.8 %collective-permute-done.7.refs_2_ = bf16[26,8,128]{2,1,0:T(8,128)(2,1)S(1)} collective-permute-done((bf16[26,8,128]{2,1,0:T(8,128)(2,1)S(1)}, bf16[26,8,128]{2,1,0:T(8,128)(2,1)S(1)}, u32[]{:S(2)}, u32[]{:S(2)}) %collective-permute-start.7) | collective-permute-done | bytes 53280 | tf_op jit(solution)/shard_map/ppermute | solution.py:219
  52.6 1.2 %collective-permute-done.8.refs_3_ = bf16[26,8,128]{2,1,0:T(8,128)(2,1)S(1)} collective-permute-done((bf16[26,8,128]{2,1,0:T(8,128)(2,1)S(1)}, bf16[26,8,128]{2,1,0:T(8,128)(2,1)S(1)}, u32[]{:S(2)}, u32[]{:S(2)}) %collective-permute-start.8) | collective-permute-done | bytes 53280 | tf_op jit(solution)/shard_map/ppermute | solution.py:219
  53.8 0.8 route.1
  54.6 24.4 %all_to_all.15.came = bf16[32,70,128]{2,1,0:T(8,128)(2,1)S(1)} all-to-all(bf16[32,70,128]{2,1,0:T(8,128)(2,1)S(1)} %route.1), channel_id=1, replica_groups=mesh['x'=4,'c'=2,'y'=4,'z'=8] {'y','z'}, dimensions={0} | all-to-all | bytes 1146880 | tf_op jit(solution)/shard_map/all_to_all | solution.py:319
  79.0 0.7 last.1
  (1 shorter events, 0.0 us)
Async XLA Ops:
  0.6 13.6 %copy-start = (bf16[128,3456]{1,0:T(8,128)(2,1)S(1)}, bf16[128,3456]{1,0:T(8,128)(2,1)}, u32[]{:S(2)}) copy-start(bf16[128,3456]{1,0:T(8,128)(2,1)} %x.1) | copy-start | bytes 2654212
  0.6 13.6 %copy-start.1 = (bf16[128,3456]{1,0:T(8,128)(2,1)S(1)}, bf16[128,3456]{1,0:T(8,128)(2,1)}, u32[]{:S(2)}) copy-start(bf16[128,3456]{1,0:T(8,128)(2,1)} %up.1) | copy-start | bytes 2654212
  0.7 13.6 %copy-start.3 = (f32[3456]{0:T(1024)S(1)}, f32[3456]{0:T(1024)}, u32[]{:S(2)}) copy-start(f32[3456]{0:T(1024)} %bias.1) | copy-start | bytes 41476
  0.7 13.6 %collective-permute-start = (bf16[128,3456]{1,0:T(8,128)(2,1)}, bf16[128,3456]{1,0:T(8,128)(2,1)S(1)}, u32[]{:S(2)}, u32[]{:S(2)}) collective-permute-start(bf16[128,3456]{1,0:T(8,128)(2,1)} %x.1), channel_id=1, source_target_pairs={{0,32},{32,0},{1,33},{33,1},{2,34},{34,2},{3,35},{35,3},{4,36},{36... | collective-permute-start | bytes 2654216 | tf_op jit(solution)/shard_map/ppermute | solution.py:227
  0.8 13.5 %collective-permute-start.1 = (bf16[128,3456]{1,0:T(8,128)(2,1)}, bf16[128,3456]{1,0:T(8,128)(2,1)S(1)}, u32[]{:S(2)}, u32[]{:S(2)}) collective-permute-start(bf16[128,3456]{1,0:T(8,128)(2,1)} %up.1), channel_id=1, source_target_pairs={{0,32},{32,0},{1,33},{33,1},{2,34},{34,2},{3,35},{35,3},{4,36},{36... | collective-permute-start | bytes 2654216 | tf_op jit(solution)/shard_map/ppermute | solution.py:228
  1.3 0.9 %copy-start.6 = (s32[2,4,4096]{2,1,0:T(4,128)S(1)}, s32[2,4,4096]{2,1,0:T(4,128)}, u32[]{:S(2)}) copy-start(s32[2,4,4096]{2,1,0:T(4,128)} %ids.3) | copy-start | bytes 393220
  2.2 0.6 copy-start.2
  2.8 20.6 %all-to-all-start = ((s16[32,8,128]{2,1,0:T(8,128)(2,1)}), s16[32,8,128]{2,1,0:T(8,128)(2,1)}, u32[]{:S(2)}, u32[]{:S(2)}) async-start(s16[32,8,128]{2,1,0:T(8,128)(2,1)} %copy-done.2), calls=%async_computation | async-start | bytes 131072 | tf_op jit(solution)/shard_map/all_to_all | solution.py:231
  23.4 4.4 %copy-start.4 = (s32[26]{0:T(128)S(1)}, s32[26]{0:T(128)}, u32[]{:S(2)}) copy-start(s32[26]{0:T(128)} %placement.5) | copy-start | bytes 316
  23.4 27.7 %all-to-all-start.1 = ((bf16[4,32,6912]{2,1,0:T(8,128)(2,1)}), bf16[4,32,6912]{2,1,0:T(8,128)(2,1)S(1)}, u32[]{:S(2)}, u32[]{:S(2)}) async-start(bf16[4,32,6912]{2,1,0:T(8,128)(2,1)} %get-tuple-element.15), calls=%async_computation.1 | async-start | bytes 3538944 | tf_op jit(solution)/shard_map/all_to_all | solution.py:259
  27.8 1.5 %copy-start.5 = (bf16[256,3328]{1,0:T(8,128)(2,1)S(1)}, bf16[256,3328]{1,0:T(8,128)(2,1)}, u32[]{:S(2)}) copy-start(bf16[256,3328]{1,0:T(8,128)(2,1)} %get-tuple-element.17.pooled) | copy-start | bytes 5111812
  27.8 1.5 %collective-permute-start.2 = (s16[32,8,128]{2,1,0:T(8,128)(2,1)}, s16[32,8,128]{2,1,0:T(8,128)(2,1)S(1)}, u32[]{:S(2)}, u32[]{:S(2)}) collective-permute-start(s16[32,8,128]{2,1,0:T(8,128)(2,1)} %all-to-all-done.ids), channel_id=1, source_target_pairs={{0,32},{32,0},{1,33},{33,1},{2,34},{34,2},{3,35},{35,3},{4,36},{36... | collective-permute-start | bytes 196616 | tf_op jit(solution)/shard_map/ppermute | solution.py:260
  30.8 13.4 %collective-permute-start.3 = (bf16[26,32,128]{2,1,0:T(8,128)(2,1)S(1)}, bf16[26,32,128]{2,1,0:T(8,128)(2,1)S(1)}, u32[]{:S(2)}, u32[]{:S(2)}) collective-permute-start(bf16[26,32,128]{2,1,0:T(8,128)(2,1)S(1)} %get-tuple-element.19), channel_id=1, source_target_pairs={{0,8},{8,16},{16,24},{24,0},{1,9},{9,17},{17,25},{25,1},{2,10},{10... | collective-permute-start | bytes 638984 | tf_op jit(solution)/shard_map/ppermute | solution.py:219
  31.5 12.7 %collective-permute-start.4 = (bf16[26,32,128]{2,1,0:T(8,128)(2,1)S(1)}, bf16[26,32,128]{2,1,0:T(8,128)(2,1)S(1)}, u32[]{:S(2)}, u32[]{:S(2)}) collective-permute-start(bf16[26,32,128]{2,1,0:T(8,128)(2,1)S(1)} %get-tuple-element.20), channel_id=1, source_target_pairs={{0,16},{8,24},{16,0},{24,8},{1,17},{9,25},{17,1},{25,9},{2,18},{10... | collective-permute-start | bytes 638984 | tf_op jit(solution)/shard_map/ppermute | solution.py:219
  33.5 11.3 %collective-permute-start.5 = (bf16[26,32,128]{2,1,0:T(8,128)(2,1)S(1)}, bf16[26,32,128]{2,1,0:T(8,128)(2,1)S(1)}, u32[]{:S(2)}, u32[]{:S(2)}) collective-permute-start(bf16[26,32,128]{2,1,0:T(8,128)(2,1)S(1)} %get-tuple-element.21), channel_id=1, source_target_pairs={{0,24},{8,0},{16,8},{24,16},{1,25},{9,1},{17,9},{25,17},{2,26},{10... | collective-permute-start | bytes 638984 | tf_op jit(solution)/shard_map/ppermute | solution.py:219
  44.9 6.9 %collective-permute-start.6 = (bf16[26,8,128]{2,1,0:T(8,128)(2,1)S(1)}, bf16[26,8,128]{2,1,0:T(8,128)(2,1)S(1)}, u32[]{:S(2)}, u32[]{:S(2)}) collective-permute-start(bf16[26,8,128]{2,1,0:T(8,128)(2,1)S(1)} %get-tuple-element.23), channel_id=1, source_target_pairs={{0,64},{64,128},{128,192},{192,0},{1,65},{65,129},{129,193},{193,1... | collective-permute-start | bytes 159752 | tf_op jit(solution)/shard_map/ppermute | solution.py:219
  47.0 5.6 %collective-permute-start.7 = (bf16[26,8,128]{2,1,0:T(8,128)(2,1)S(1)}, bf16[26,8,128]{2,1,0:T(8,128)(2,1)S(1)}, u32[]{:S(2)}, u32[]{:S(2)}) collective-permute-start(bf16[26,8,128]{2,1,0:T(8,128)(2,1)S(1)} %get-tuple-element.24), channel_id=1, source_target_pairs={{0,128},{64,192},{128,0},{192,64},{1,129},{65,193},{129,1},{193,65... | collective-permute-start | bytes 159752 | tf_op jit(solution)/shard_map/ppermute | solution.py:219
  49.7 4.1 %collective-permute-start.8 = (bf16[26,8,128]{2,1,0:T(8,128)(2,1)S(1)}, bf16[26,8,128]{2,1,0:T(8,128)(2,1)S(1)}, u32[]{:S(2)}, u32[]{:S(2)}) collective-permute-start(bf16[26,8,128]{2,1,0:T(8,128)(2,1)S(1)} %get-tuple-element.25), channel_id=1, source_target_pairs={{0,192},{64,0},{128,64},{192,128},{1,193},{65,1},{129,65},{193,129... | collective-permute-start | bytes 159752 | tf_op jit(solution)/shard_map/ppermute | solution.py:219
